TPU v7x, 512 devices: a whole 4x8x8 slice. The times are simulated.
512 devices in a mesh: tile: 128 (over z, y, x_hi), depth: 4 (over x_lo, core).
Axes of the slice: x: 4 (x_hi: 2, x_lo: 2; x = x_hi * 2 + x_lo), y: 8, z: 8, core: 2. Of those that a mesh axis runs over, the one named last changes fastest.
Arguments:
- positions: float32 [3, 262144], P(None, 'tile'), may hold values from -4 to 4
- log_scales: float32 [3, 262144], P(None, 'tile'), may hold values from -2 to 0
- opacity_logits: float32 [1, 262144], P(None, 'tile'), may hold values from -3 to 1.5
- colors: float32 [3, 262144], P(None, 'tile'), may hold values from 0 to 1
- first_moment: float32 [10, 262144], P(None, 'tile'), may hold values from -3 to 3
- second_moment: float32 [10, 262144], P(None, 'tile'), may hold values from 0.01 to 1
- cameras: float32 [4, 2, 4], replicated, may hold values from -6.4 to 6.4
- background: float32 [3], replicated, may hold values from 0 to 1
- target: float32 [512, 3, 1024], P('tile'), may hold values from 0 to 1
- tile_view: int32 [512], P('tile'), may hold values from 0 to 3
- tile_length: int32 [512], P('tile'), may hold values from 128 to 512
- list_owner: int32 [4, 512, 128, 1], P('depth', 'tile'), may hold values from 0 to 127; in each aligned block of 512 rows (0 to 511, 512 to 1023, ..., all dimensions but the last counted through in order) at most 10 rows name the same one
- list_row: int32 [4, 512, 128], P('depth', 'tile'), may hold values from 0 to 2047
Outputs:
- image: float32 [512, 3, 1024], P('tile')
- new_params: float32 [10, 262144], P(None, 'tile')
- new_first: float32 [10, 262144], P(None, 'tile')
- new_second: float32 [10, 262144], P(None, 'tile')
Inputs may be any that keep to these rules, and one draw needn't show every extreme that they name: `list_owner`: within the entries of one device's block (one depth slab of the tiles of one tile index), no owner is named more than 10 times, a bound that some block reaches.
All inputs are finite; a program needn't handle non-finite values.
Results may differ from a plain program's by a relative error of at most 0.00008.
Values sent between devices are 32-bit elements; how exact they have to be, the bound alone decides.
No kernel may reach another device: no remote copies, remote signals or barrier semaphores. Data moves between devices by JAX's collectives and lax.ppermute only.
A program may use at most 64 MiB of HBM per device.

v0:
```python
import math

import jax
import jax.numpy as jnp
from jax import lax
from jax.sharding import Mesh
from jax.sharding import PartitionSpec as P

TILE_SIDE = 32
TILE = ("tile_0", "tile_1", "tile_2")


def sent_together(arrays, axis, dim, along):
    widths = [math.prod(a.shape[along:]) for a in arrays]
    both = jnp.concatenate(
        [a.reshape(*a.shape[:along], w) for a, w in zip(arrays, widths)], axis=along
    )
    whole = lax.all_gather(both, axis, axis=dim, tiled=True)
    pieces = jnp.split(whole, [sum(widths[:k]) for k in range(1, len(widths))], axis=along)
    return tuple(
        (b.reshape(*whole.shape[:along], *a.shape[along:]) for a, b in zip(arrays, pieces))
    )


def cut_along(array, dim, length):
    before, after = (array.shape[:dim], array.shape[dim + 1 :])
    return jnp.moveaxis(array.reshape(*before, length, -1, *after), dim, 0)


def joined_along(pieces, dim):
    shape = list(pieces.shape[1:])
    shape[dim] *= pieces.shape[0]
    return jnp.moveaxis(pieces, 0, dim).reshape(shape)


def exchange_in_order(pieces, axes, order):
    inside = pieces.shape[1:]
    whole = pieces.reshape(*(lax.axis_size(a) for a in axes), *inside)
    for k in order:
        whole = lax.all_to_all(whole, axes[k], k, k, tiled=True)
    return whole.reshape(-1, *inside)


def stepwise_exchange(array, axes, order, split_dim, concat_dim):
    pieces = cut_along(array, split_dim, lax.axis_size(axes))
    return joined_along(exchange_in_order(pieces, axes, order), concat_dim)


def copy_for_each(array, axis):
    length = lax.axis_size(axis)
    return lax.all_to_all(
        jnp.broadcast_to(array[None], (length, *array.shape)), axis, 0, 0, tiled=True
    )


def taken_together(array, axis):
    return copy_for_each(array, axis).sum(axis=0)


def project(params, cams):
    position = params[0:3]
    variance = jnp.exp(2.0 * params[3:6])
    first_row = cams[:, 0, 0:3].T
    second_row = cams[:, 1, 0:3].T
    center_x = jnp.sum(first_row * position, axis=0) + cams[:, 0, 3] + 0.5 * TILE_SIDE
    center_y = jnp.sum(second_row * position, axis=0) + cams[:, 1, 3] + 0.5 * TILE_SIDE
    cov_xx = jnp.sum(first_row * first_row * variance, axis=0) + 0.3
    cov_xy = jnp.sum(first_row * second_row * variance, axis=0)
    cov_yy = jnp.sum(second_row * second_row * variance, axis=0) + 0.3
    determinant = cov_xx * cov_yy - cov_xy * cov_xy
    return jnp.stack(
        [
            center_x,
            center_y,
            cov_yy / determinant,
            -cov_xy / determinant,
            cov_xx / determinant,
            jax.nn.sigmoid(params[6]),
            params[7],
            params[8],
            params[9],
        ]
    )


def coverage(screen, alive, pixels):
    pixel = jnp.arange(pixels, dtype=jnp.int32)
    pixel_x = (pixel % TILE_SIDE).astype(jnp.float32) + 0.5
    pixel_y = (pixel // TILE_SIDE).astype(jnp.float32) + 0.5
    offset_x = pixel_x[:, None] - screen[0][None, :]
    offset_y = pixel_y[:, None] - screen[1][None, :]
    quadric = (
        screen[2][None, :] * offset_x * offset_x
        + 2.0 * screen[3][None, :] * offset_x * offset_y
        + screen[4][None, :] * offset_y * offset_y
    )
    falloff = jnp.exp(-0.5 * quadric)
    alpha = screen[5][None, :] * falloff * alive[None, :]
    return (offset_x, offset_y, falloff, alpha)


def running_sum(values, triangle):
    rows = values.shape[0]
    width = triangle.shape[0]
    blocks = values.reshape(rows, values.shape[1] // width, width)
    inner = jnp.einsum("pbk,kj->pbj", blocks, triangle, precision=lax.Precision.HIGHEST)
    sums = jnp.sum(blocks, axis=2)
    lead = jnp.cumsum(sums, axis=1) - sums
    return (inner + lead[:, :, None]).reshape(rows, values.shape[1])


def adam_update(param, first, second, gradient):
    new_first = 0.9 * first + 0.1 * gradient
    new_second = 0.999 * second + 0.001 * gradient * gradient
    corrected = new_first / (1.0 - 0.9**10) / (jnp.sqrt(new_second / (1.0 - 0.999**10)) + 1e-08)
    return (param - 0.05 * corrected, new_first, new_second)


def body(
    positions,
    log_scales,
    opacity_logits,
    colors,
    first_moment,
    second_moment,
    cameras,
    background,
    target,
    tile_view,
    tile_length,
    list_owner,
    list_row,
):
    tiles_here = target.shape[0]
    pixels = target.shape[2]
    slab = list_row.shape[2]
    owner_count = lax.axis_size(TILE)
    depth_count = lax.axis_size("depth")
    depth_index = lax.axis_index("depth")
    capacity = max(2, 5 * tiles_here * slab // (2 * owner_count))
    highest = lax.Precision.HIGHEST
    params = jnp.concatenate([positions, log_scales, opacity_logits, colors], axis=0)
    owner = list_owner.reshape(-1)
    wanted = list_row.reshape(-1)
    viewed = jnp.repeat(tile_view, slab)
    onehot = (owner[:, None] == jnp.arange(owner_count, dtype=jnp.int32)[None, :]).astype(jnp.int32)
    rank = jnp.sum((jnp.cumsum(onehot, axis=0) - onehot) * onehot, axis=1)
    slot = owner * capacity + rank
    request = (
        jnp.zeros((2, owner_count * capacity), jnp.int32)
        .at[:, slot]
        .set(jnp.stack([wanted, viewed]))
    )
    request = request.reshape(2, owner_count, capacity)
    received = lax.all_to_all(request, TILE, split_axis=1, concat_axis=1, tiled=True)
    rows_in = received[0].reshape(-1)
    views_in = received[1].reshape(-1)
    screen = project(params[:, rows_in], cameras[views_in])
    screen = screen.reshape(9, received.shape[1], received.shape[2])
    fetched = lax.all_to_all(screen, TILE, split_axis=1, concat_axis=1, tiled=True)
    entry = fetched.reshape(9, -1)[:, slot].reshape(9, tiles_here, slab).transpose(1, 0, 2)
    place = depth_index * slab + jnp.arange(slab, dtype=jnp.int32)
    live = (place[None, :] < tile_length[:, None]).astype(jnp.float32)
    order = jnp.arange(slab, dtype=jnp.int32)
    strict = (order[:, None] < order[None, :]).astype(jnp.float32)
    inclusive = (order[:, None] <= order[None, :]).astype(jnp.float32)

    def forward(args):
        screen, alive = args
        offset_x, offset_y, falloff, alpha = coverage(screen, alive, pixels)
        leak = jnp.log1p(-alpha)
        before = running_sum(leak, strict)
        weight = alpha * jnp.exp(before)
        color = jnp.einsum("ck,pk->cp", screen[6:9], weight, precision=highest)
        return (jnp.sum(leak, axis=1), color)

    def backward(args):
        screen, alive, start_log, start_color, whole, miss = args
        offset_x, offset_y, falloff, alpha = coverage(screen, alive, pixels)
        leak = jnp.log1p(-alpha)
        local = running_sum(leak, strict)
        carried = jnp.exp(start_log)[:, None]
        inside = jnp.exp(local)
        trans = carried * inside
        weight = alpha * trans
        local_weight = alpha * inside
        d_alpha = jnp.zeros_like(alpha)
        for channel in range(3):
            shade = screen[6 + channel][None, :]
            upto = running_sum(local_weight * shade, inclusive)
            behind = whole[channel][:, None] - start_color[channel][:, None] - carried * upto
            d_alpha = d_alpha + miss[channel][:, None] * (trans * shade - behind / (1.0 - alpha))
        d_color = jnp.einsum("cp,pk->ck", miss, weight, precision=highest)
        d_quad = d_alpha * (-0.5 * alpha)
        d_opacity = jnp.sum(d_alpha * falloff * alive[None, :], axis=0)
        d_center_x = jnp.sum(
            d_quad * -2.0 * (screen[2][None, :] * offset_x + screen[3][None, :] * offset_y), axis=0
        )
        d_center_y = jnp.sum(
            d_quad * -2.0 * (screen[3][None, :] * offset_x + screen[4][None, :] * offset_y), axis=0
        )
        d_conic_a = jnp.sum(d_quad * offset_x * offset_x, axis=0)
        d_conic_b = jnp.sum(d_quad * 2.0 * offset_x * offset_y, axis=0)
        d_conic_c = jnp.sum(d_quad * offset_y * offset_y, axis=0)
        return jnp.concatenate(
            [
                jnp.stack([d_center_x, d_center_y, d_conic_a, d_conic_b, d_conic_c, d_opacity]),
                d_color,
            ],
            axis=0,
        )

    slab_log, slab_color = lax.map(forward, (entry, live))
    every_log, every_color = sent_together((slab_log[None], slab_color[None]), "depth", 0, 2)
    running = jnp.zeros_like(slab_log)
    before_log = jnp.zeros_like(slab_log)
    before_color = jnp.zeros_like(slab_color)
    total_color = jnp.zeros_like(slab_color)
    for index in range(depth_count):
        earlier = (index < depth_index).astype(jnp.float32)
        weighted = jnp.exp(running)[:, None, :] * every_color[index]
        before_log = before_log + earlier * every_log[index]
        before_color = before_color + earlier * weighted
        total_color = total_color + weighted
        running = running + every_log[index]
    image = total_color + jnp.exp(running)[:, None, :] * background[None, :, None]
    error = image - target
    entry_grad = lax.map(backward, (entry, live, before_log, before_color, image, error))
    flat_grad = entry_grad.transpose(1, 0, 2).reshape(9, -1)
    outgoing = jnp.zeros((9, owner_count * capacity), jnp.float32).at[:, slot].set(flat_grad)
    outgoing = outgoing.reshape(9, owner_count, capacity)
    incoming = stepwise_exchange(outgoing, TILE, (0, 1, 2), 1, 1)
    rows_in = received[0].reshape(-1)
    views_in = received[1].reshape(-1)
    chosen_cams = cameras[views_in]
    unused, pullback = jax.vjp(lambda chosen: project(chosen, chosen_cams), params[:, rows_in])
    (slot_grad,) = pullback(incoming.reshape(9, -1))
    gradient = jnp.zeros_like(params).at[:, rows_in].add(slot_grad)
    gradient = taken_together(gradient, "depth")
    new_params, new_first, new_second = adam_update(params, first_moment, second_moment, gradient)
    return (image, new_params, new_first, new_second)


def solution(mesh):
    torus = Mesh(
        mesh.devices.reshape(8, 8, 2, mesh.shape["depth"]), ("tile_0", "tile_1", "tile_2", "depth")
    )
    placed = (
        P(None, TILE),
        P(None, TILE),
        P(None, TILE),
        P(None, TILE),
        P(None, TILE),
        P(None, TILE),
        P(),
        P(),
        P(TILE, None, None),
        P(TILE),
        P(TILE),
        P("depth", TILE, None, None),
        P("depth", TILE, None),
    )
    return jax.shard_map(
        body,
        mesh=torus,
        in_specs=placed,
        out_specs=(P(TILE, None, None), P(None, TILE), P(None, TILE), P(None, TILE)),
        check_vma=False,
    )
```

profile of v0, /device:TPU:1, one launch (start us, length us, event | category | flops | bytes accessed | tf_op | source)
XLA Modules:
  0.0 244.9 jit_solution(12501443936985024378)
XLA Ops:
  0.7 0.8 copy.226
  2.4 1.9 scatter_custom_fusion
  5.4 21.3 %all-to-all-start = ((s32[2,128,10]{2,0,1:T(2,128)}), s32[2,128,10]{2,0,1:T(2,128)S(1)}, u32[]{:S(2)}, u32[]{:S(2)}) async-start(s32[2,128,10]{2,0,1:T(2,128)} %copy.230), calls=%async_computation | async-start | bytes 262144 | tf_op jit(solution)/shard_map/all_to_all | solution.py:155
  27.3 11.9 %all-to-all-done = s32[2,128,10]{2,0,1:T(2,128)S(1)} async-done(((s32[2,128,10]{2,0,1:T(2,128)}), s32[2,128,10]{2,0,1:T(2,128)S(1)}, u32[]{:S(2)}, u32[]{:S(2)}) %all-to-all-start) | async-done | bytes 10272 | tf_op jit(solution)/shard_map/all_to_all | solution.py:155
  40.0 4.3 %gather_fusion = f32[1280,2,4]{2,1,0:T(2,128)S(1)} fusion(f32[4,2,4]{2,1,0:T(2,128)S(1)} %copy-done, s32[2048]{0:T(1024)S(1)} %get-tuple-element.464), kind=kCustom, calls=%fused_computation | custom fusion | bytes 87040 | tf_op jit(solution)/shard_map/gather | solution.py:158
  44.4 36.3 %slice_reduce_fusion = (f32[1280]{0:T(1024)S(1)}, f32[1280]{0:T(1024)S(1)}) fusion(f32[1280,2,4]{2,1,0:T(2,128)S(1)} %gather_fusion), kind=kLoop, calls=%fused_computation.224 | loop fusion | bytes 20480 | tf_op jit(solution)/shard_map/slice | solution.py:66
  80.7 1.8 fusion.168
  82.4 2.3 gather_fusion.1
  87.7 1.4 copy.235
  89.0 6.2 %all-to-all-start.1 = ((f32[9,128,10]{2,0,1:T(8,128)}), f32[9,128,10]{2,0,1:T(8,128)S(1)}, u32[]{:S(2)}, u32[]{:S(2)}) async-start(f32[9,128,10]{2,0,1:T(8,128)} %copy.235), calls=%async_computation.1 | async-start | bytes 2097152 | tf_op jit(solution)/shard_map/all_to_all | solution.py:160
  95.2 26.4 %all-to-all-done.1 = f32[9,128,10]{2,0,1:T(8,128)S(1)} async-done(((f32[9,128,10]{2,0,1:T(8,128)}), f32[9,128,10]{2,0,1:T(8,128)S(1)}, u32[]{:S(2)}, u32[]{:S(2)}) %all-to-all-start.1) | async-done | bytes 46112 | tf_op jit(solution)/shard_map/all_to_all | solution.py:160
  122.4 1.0 gather_fusion.2
  123.6 11.9 %while.29 = (s32[]{:T(128)}, f32[4,1024]{1,0:T(4,128)S(1)}, f32[4,3,1024]{2,1,0:T(4,128)S(1)}, f32[4,9,128]{2,1,0:T(8,128)S(1)}, f32[4,128]{1,0:T(4,128)S(1)}, /...) while((s32[]{:T(128)}, f32[4,1024]{1,0:T(4,128)S(1)}, ...), condition=%wide.region_12.13_spmd.clone, body=%wide.region_9.12_spmd.clone.sunk | while | flops 213826688 | bytes 1152237 | solution.py:213
  124.9 1.1 fusion.209
  127.9 1.1 fusion.209
  130.9 1.1 fusion.209
  133.8 1.1 fusion.209
  135.6 11.1 %all_gather.3 = f32[4,4,4096]{2,1,0:T(4,128)S(1)} all-gather(f32[1,4,4096]{2,1,0:T(4,128)S(1)} %pad_maximum_fusion.1), channel_id=1, replica_groups=mesh['tile_0'=8,'tile_1'=8,'tile_2'=2,'depth'=4] {'depth'}, dimensions={0}, use_global_device_ids=true | all-gather | bytes 327680 | tf_op jit(solution)/shard_map/all_gather | solution.py:18
  146.8 31.7 %while.30 = (s32[]{:T(128)}, f32[4,9,128]{2,1,0:T(8,128)S(1)}, f32[4,3,1024]{2,0,1:T(4,128)S(1)}, f32[4,1024]{1,0:T(4,128)S(1)}, f32[4,9,128]{2,1,0:T(8,128)S(1)...) while((s32[]{:T(128)}, f32[4,9,128]{2,1,0:T(8,128)S(1)}, ...), condition=%wide.region_24.25_spmd.clone.clone, body=%wide.region_13.24_spmd.clone.clone.sunk | while | flops 838093184 | bytes 7204689 | solution.py:228
  147.9 1.5 multiply_reduce_fusion.8
  150.2 1.3 fusion.225
  151.4 1.3 fusion.224
  152.7 1.3 multiply_multiply_fusion.7
  155.7 1.5 multiply_reduce_fusion.8
  158.0 1.3 fusion.225
  159.3 1.3 fusion.224
  160.6 1.3 multiply_multiply_fusion.7
  163.6 1.5 multiply_reduce_fusion.8
  165.9 1.3 fusion.225
  167.2 1.3 fusion.224
  168.5 1.3 multiply_multiply_fusion.7
  171.5 1.5 multiply_reduce_fusion.8
  173.8 1.3 fusion.225
  175.1 1.3 fusion.224
  176.3 1.3 multiply_multiply_fusion.7
  178.7 1.9 scatter_custom_fusion.1
  181.5 0.9 reshape.1872
  182.4 9.8 %all_to_all.30 = f32[8,1,1440]{2,1,0:T(1,128)S(1)} all-to-all(f32[8,1,1440]{2,1,0:T(1,128)S(1)} %reshape.1872), channel_id=1, replica_groups=mesh['tile_0'=8,'tile_1'=8,'tile_2'=2,'depth'=4] {'tile_0'}, dimensions={0} | all-to-all | bytes 92160 | tf_op jit(solution)/shard_map/all_to_all | solution.py:40
  193.5 0.8 reshape.1873
  194.5 0.9 reshape.1874
  195.4 12.0 %all_to_all.31 = f32[8,1,1440]{2,1,0:T(1,128)S(1)} all-to-all(f32[8,1,1440]{2,1,0:T(1,128)S(1)} %reshape.1874), channel_id=1, replica_groups=mesh['tile_0'=8,'tile_1'=8,'tile_2'=2,'depth'=4] {'tile_1'}, dimensions={0} | all-to-all | bytes 92160 | tf_op jit(solution)/shard_map/all_to_all | solution.py:40
  207.4 0.8 reduce.45
  208.2 0.8 reshape.1875
  209.6 6.7 %all_to_all.32 = f32[2,1,5760]{2,1,0:T(1,128)S(1)} all-to-all(f32[2,1,5760]{2,1,0:T(1,128)S(1)} %reshape.1876), channel_id=1, replica_groups=mesh['tile_0'=8,'tile_1'=8,'tile_2'=2,'depth'=4] {'tile_2'}, dimensions={0} | all-to-all | bytes 92160 | tf_op jit(solution)/shard_map/all_to_all | solution.py:40
  216.4 0.8 reduce.46
  219.9 9.2 %scatter_custom_fusion.2 = f32[10,2048]{0,1:T(8,128)S(1)} fusion(s32[1280]{0:T(1024)S(1)} %fusion.157, f32[1280,10]{1,0:T(8,128)S(1)} %copy.249, f32[]{:T(128)} %constant.217.clone.1), kind=kCustom, calls=%fused_computation.226 | custom fusion | flops 12800 | bytes 81924 | tf_op jit(solution)/shard_map/scatter-add | solution.py:238
  229.6 14.2 %all_to_all.33 = f32[4,10,2048]{2,1,0:T(8,128)S(1)} all-to-all(f32[4,10,2048]{2,1,0:T(8,128)S(1)} %broadcast_in_dim.113), channel_id=1, replica_groups=mesh['tile_0'=8,'tile_1'=8,'tile_2'=2,'depth'=4] {'depth'}, dimensions={0} | all-to-all | bytes 655360 | tf_op jit(solution)/shard_map/all_to_all | solution.py:51
  243.8 0.8 multiply_subtract_fusion
  (237 shorter events, 29.7 us)
Async XLA Ops:
  0.6 39.4 %copy-start = (f32[4,2,4]{2,1,0:T(2,128)S(1)}, f32[4,2,4]{2,1,0:T(2,128)}, u32[]{:S(2)}) copy-start(f32[4,2,4]{2,1,0:T(2,128)} %param.23) | copy-start | bytes 388
  0.6 1.2 copy-start.10
  0.7 1.6 copy-start.11
  0.7 1.5 copy-start.12
  1.8 25.0 %copy-start.3 = (f32[3,2048]{1,0:T(4,128)S(1)}, f32[3,2048]{1,0:T(4,128)}, u32[]{:S(2)}) copy-start(f32[3,2048]{1,0:T(4,128)} %param.20) | copy-start | bytes 73732
  1.8 25.0 %copy-start.4 = (f32[3,2048]{1,0:T(4,128)S(1)}, f32[3,2048]{1,0:T(4,128)}, u32[]{:S(2)}) copy-start(f32[3,2048]{1,0:T(4,128)} %param.18) | copy-start | bytes 73732
  1.9 25.0 %copy-start.5 = (f32[3,2048]{1,0:T(4,128)S(1)}, f32[3,2048]{1,0:T(4,128)}, u32[]{:S(2)}) copy-start(f32[3,2048]{1,0:T(4,128)} %param.17) | copy-start | bytes 73732
  1.9 25.0 %copy-start.9 = (f32[1,2048]{1,0:T(1,128)S(1)}, f32[1,2048]{1,0:T(1,128)}, u32[]{:S(2)}) copy-start(f32[1,2048]{1,0:T(1,128)} %param.19) | copy-start | bytes 24580
  2.1 24.8 %copy-start.13 = (s32[4]{0:T(128)S(1)}, s32[4]{0:T(128)}, u32[]{:S(2)}) copy-start(s32[4]{0:T(128)} %param.27) | copy-start | bytes 52
  5.4 33.8 %all-to-all-start = ((s32[2,128,10]{2,0,1:T(2,128)}), s32[2,128,10]{2,0,1:T(2,128)S(1)}, u32[]{:S(2)}, u32[]{:S(2)}) async-start(s32[2,128,10]{2,0,1:T(2,128)} %copy.230), calls=%async_computation | async-start | bytes 262144 | tf_op jit(solution)/shard_map/all_to_all | solution.py:155
  82.4 2.8 %copy-start.1 = (f32[1280,1,3]{2,1,0:T(1,128)S(1)}, f32[1280,1,3]{2,1,0:T(1,128)}, u32[]{:S(2)}) copy-start(f32[1280,1,3]{2,1,0:T(1,128)} %get-tuple-element.434) | copy-start | bytes 46084
  89.0 32.6 %all-to-all-start.1 = ((f32[9,128,10]{2,0,1:T(8,128)}), f32[9,128,10]{2,0,1:T(8,128)S(1)}, u32[]{:S(2)}, u32[]{:S(2)}) async-start(f32[9,128,10]{2,0,1:T(8,128)} %copy.235), calls=%async_computation.1 | async-start | bytes 2097152 | tf_op jit(solution)/shard_map/all_to_all | solution.py:160
  123.6 23.2 %copy-start.8 = (f32[4,3,1024]{2,0,1:T(4,128)S(1)}, f32[4,3,1024]{2,0,1:T(4,128)}, u32[]{:S(2)}) copy-start(f32[4,3,1024]{2,0,1:T(4,128)} %param.25) | copy-start | bytes 147460
  123.6 23.2 %copy-start.14 = (f32[3]{0:T(128)S(1)}, f32[3]{0:T(128)}, u32[]{:S(2)}) copy-start(f32[3]{0:T(128)} %param.24) | copy-start | bytes 40
  178.5 3.0 %copy-start.2 = (f32[4,3,1024]{2,0,1:T(4,128)}, f32[4,3,1024]{2,0,1:T(4,128)S(1)}, u32[]{:S(2)}) copy-start(f32[4,3,1024]{2,0,1:T(4,128)S(1)} %get-tuple-element.716) | copy-start | bytes 147460
  229.5 14.3 %copy-start.6 = (f32[10,2048]{1,0:T(8,128)S(1)}, f32[10,2048]{1,0:T(8,128)}, u32[]{:S(2)}) copy-start(f32[10,2048]{1,0:T(8,128)} %param.21) | copy-start | bytes 245764
  229.5 14.3 %copy-start.7 = (f32[10,2048]{1,0:T(8,128)S(1)}, f32[10,2048]{1,0:T(8,128)}, u32[]{:S(2)}) copy-start(f32[10,2048]{1,0:T(8,128)} %param.22) | copy-start | bytes 245764
where the time goes:
time: 249 us; the launch traced here: 245 us
  local copies, waits for them, and re-layouts  67.5 us (27%)
  blocking collectives  53.8 us (22%)
  waiting for transfers between devices  38.3 us (15%)
  matrix products  31 us (12%)
  starting transfers between devices  27.5 us (11%)
  other arithmetic  23.8 us (10%)
    slice x1, local copies, waits for them, and re-layouts, project(): cams[:, 1, 3]  36.3 us
    all_to_all x3, blocking collectives, exchange_in_order(): whole = lax.all_to_all(whole, axes[k], k, k, tiled=True)  28.6 us
    all_to_all x1, waiting for transfers between devices, body(): lax.all_to_all(screen, TILE, split_axis=1, concat_axis=1, tiled=True)  26.4 us
    dot_general x20, matrix products, running_sum(): jnp.einsum('pbk,kj->pbj', blocks, triangle, precision=lax.Precision.HIGHEST)  25.9 us
    all_to_all x1, starting transfers between devices, body(): lax.all_to_all(request, TILE, split_axis=1, concat_axis=1, tiled=True)  21.3 us
    all_to_all x1, blocking collectives, copy_for_each(): lax.all_to_all(jnp.broadcast_to(array[None], (length, *array.shape)), axi...  14.2 us
    all_to_all x1, waiting for transfers between devices, body(): lax.all_to_all(request, TILE, split_axis=1, concat_axis=1, tiled=True)  11.9 us
    all_gather x1, blocking collectives, sent_together(): whole = lax.all_gather(both, axis, axis=dim, tiled=True)  11.1 us
  transfers between devices with their start and end apart: 2, of which 2 were waited for; matrix products, arithmetic and copies ran while one was open for 0% of the time, Pallas kernels for 0%

commit v1 on v0

v1 whole, which is shorter than its diff:
```python
import math

import jax
import jax.numpy as jnp
from jax import lax
from jax.experimental import pallas as pl
from jax.experimental.pallas import tpu as pltpu
from jax.sharding import PartitionSpec as P

LANES = 128
TILES = 4
SLAB = 128
DEPTHS = 4
SLOTS = 10
PARAMS = 10
BLOCKS = 16
LOG2E = math.log2(math.e)
VMEM = pl.BlockSpec(memory_space=pltpu.VMEM)
SMEM = pl.BlockSpec(memory_space=pltpu.SMEM)
F32 = jnp.float32
BF16 = jnp.bfloat16
I32 = jnp.int32
NT = (((1,), (1,)), ((), ()))
NN = (((1,), (0,)), ((), ()))


def iota(shape, dim):
    return lax.broadcasted_iota(I32, shape, dim)


def pieces(x):
    high = x.astype(BF16)
    rest = x - high.astype(F32)
    middle = rest.astype(BF16)
    low = (rest - middle.astype(F32)).astype(BF16)
    return high, middle, low


def side_by_side(x):
    return jnp.concatenate(pieces(x), axis=1)


def dot(a, b, dims):
    return lax.dot_general(a, b, dims, preferred_element_type=F32)


def onehot(index, rows):
    return jnp.where(iota((rows, LANES), 0) == index, 1.0, 0.0)


def request_kernel(owner_ref, row_ref, request_ref, rank_ref):
    earlier = jnp.where(iota((SLAB, SLAB), 0) < iota((SLAB, SLAB), 1), 1.0, 0.0).astype(BF16)
    before = jnp.zeros((LANES, 1), F32)
    total = jnp.zeros((LANES, LANES), F32)
    for b in range(TILES):
        named = onehot(owner_ref[b : b + 1, :], LANES)
        named_16 = named.astype(BF16)
        count = dot(named_16, earlier, NN) + before
        before = before + jnp.sum(named, axis=1, keepdims=True)
        rank = jnp.sum(named * count, axis=0, keepdims=True).astype(I32)
        rank_ref[b : b + 1, :] = rank
        row = row_ref[b : b + 1, :]
        here = iota((LANES, SLAB), 0) == rank
        high = jnp.where(here, row >> 4, 0).astype(F32).astype(BF16)
        low = jnp.where(here, row & 15, 0).astype(F32).astype(BF16)
        total = total + 16.0 * dot(named_16, high, NT) + dot(named_16, low, NT)
    request_ref[...] = total.astype(I32)


def reply_kernel(asked_ref, params_ref, reply_ref, columns, held):
    columns[...] = asked_ref[...].T
    table = jnp.concatenate(
        [
            jnp.concatenate(
                [
                    params_ref[:, a * LANES : (a + 1) * LANES],
                    jnp.zeros((16 - PARAMS, LANES), F32),
                ],
                axis=0,
            )
            for a in range(BLOCKS)
        ],
        axis=0,
    )
    table = side_by_side(table)
    for r in range(SLOTS):
        row = columns[r : r + 1, :]
        pick = onehot(row & (LANES - 1), LANES).astype(BF16)
        found = dot(table, jnp.concatenate([pick, pick, pick], axis=0), NN)
        block = row >> 7
        value = jnp.zeros((16, LANES), F32)
        for a in range(BLOCKS):
            value = value + jnp.where(block == a, found[a * 16 : (a + 1) * 16], 0.0)
        held[r * PARAMS : r * PARAMS + 16, :] = value
    held[SLOTS * PARAMS :, :] = jnp.zeros((LANES - SLOTS * PARAMS, LANES), F32)
    reply_ref[...] = held[...].T


def per_tile(values):
    place = iota((TILES, LANES), 0)
    out = jnp.full((TILES, LANES), values[0], F32)
    for b in range(1, TILES):
        out = jnp.where(place == b, values[b], out)
    return out


def camera_rows(view_ref, cams_ref):
    return [
        [per_tile([cams_ref[view_ref[b] * 8 + i * 4 + j] for b in range(TILES)]) for j in range(4)]
        for i in range(2)
    ]


def covariance(scales, jac):
    variance = [jnp.exp(2.0 * s) for s in scales]
    xx = sum(jac[0][j] * jac[0][j] * variance[j] for j in range(3)) + 0.3
    xy = sum(jac[0][j] * jac[1][j] * variance[j] for j in range(3))
    yy = sum(jac[1][j] * jac[1][j] * variance[j] for j in range(3)) + 0.3
    return variance, xx, xy, yy, xx * yy - xy * xy


def forward_kernel(
    fetched_ref,
    owner_ref,
    rank_ref,
    view_ref,
    length_ref,
    cams_ref,
    depth_ref,
    slab_ref,
    alpha_ref,
    weight_ref,
    shade_ref,
    entry_ref,
    found,
    rows,
    spread,
):
    fetched = side_by_side(fetched_ref[...].T)
    for b in range(TILES):
        named = onehot(owner_ref[b : b + 1, :], LANES).astype(BF16)
        found[...] = dot(fetched, jnp.concatenate([named, named, named], axis=0), NN)
        rank = rank_ref[b : b + 1, :]
        value = jnp.zeros((16, LANES), F32)
        for r in range(SLOTS):
            value = value + jnp.where(rank == r, found[r * PARAMS : r * PARAMS + 16, :], 0.0)
        entry_ref[b * 16 : (b + 1) * 16, :] = value
    entry = [entry_ref[pl.ds(p, TILES, stride=16), :] for p in range(PARAMS)]
    jac = camera_rows(view_ref, cams_ref)
    center_x = sum(jac[0][j] * entry[j] for j in range(3)) + jac[0][3] + 16.0
    center_y = sum(jac[1][j] * entry[j] for j in range(3)) + jac[1][3] + 16.0
    _, xx, xy, yy, det = covariance(entry[3:6], jac)
    place = depth_ref[0] * SLAB + iota((TILES, LANES), 1).astype(I32)
    length = per_tile([length_ref[b].astype(F32) for b in range(TILES)])
    live = jnp.where(place.astype(F32) < length, 1.0, 0.0)
    opacity = jax.nn.sigmoid(entry[6]) * live
    factors = [
        center_x,
        center_y,
        (-0.5 * LOG2E) * (yy / det),
        LOG2E * (xy / det),
        (-0.5 * LOG2E) * (xx / det),
        opacity,
        *entry[7:10],
    ]
    for p, factor in enumerate(factors):
        rows[p * TILES : (p + 1) * TILES, :] = factor
    rows[len(factors) * TILES :, :] = jnp.zeros((LANES - len(factors) * TILES, LANES), F32)
    turned = rows[...].T
    for p in range(9):
        for b in range(TILES):
            column = turned[:, p * TILES + b : p * TILES + b + 1]
            wide = jnp.broadcast_to(column, (SLAB, LANES))
            if p < 6:
                spread[p, b * SLAB : (b + 1) * SLAB, :] = wide
            else:
                shade_ref[p - 6, b * SLAB : (b + 1) * SLAB, :] = wide
    lane = iota((8, LANES), 1)
    pixel_x = (lane & 31).astype(F32) + 0.5
    pixel_y = (iota((8, LANES), 0) * 4 + (lane >> 5)).astype(F32) + 0.5

    def step(k, carry):
        out = []
        for b in range(TILES):
            trans, red, green, blue = carry[4 * b : 4 * b + 4]
            at = b * SLAB + k
            get = lambda ref, p: jnp.broadcast_to(ref[p, pl.ds(at, 1), :], (8, LANES))
            ex = pixel_x - get(spread, 0)
            ey = pixel_y - get(spread, 1)
            power = ex * (get(spread, 2) * ex + get(spread, 3) * ey) + get(spread, 4) * ey * ey
            alpha = get(spread, 5) * jnp.exp2(power)
            weight = alpha * trans
            alpha_ref[at] = alpha
            weight_ref[at] = weight
            out += [
                trans - weight,
                red + weight * get(shade_ref, 0),
                green + weight * get(shade_ref, 1),
                blue + weight * get(shade_ref, 2),
            ]
        return tuple(out)

    one, zero = jnp.ones((8, LANES), F32), jnp.zeros((8, LANES), F32)
    out = lax.fori_loop(0, SLAB, step, (one, zero, zero, zero) * TILES, unroll=4)
    for q in range(4 * TILES):
        slab_ref[q * 8 : (q + 1) * 8, :] = out[q]


def backward_kernel(
    slabs_ref,
    alpha_ref,
    weight_ref,
    shade_ref,
    entry_ref,
    owner_ref,
    rank_ref,
    view_ref,
    cams_ref,
    depth_ref,
    back_ref,
    target_ref,
    image_ref,
    outgoing_ref,
    slope,
    moment,
    grads,
    placed,
    picture,
):
    depth = depth_ref[0]
    back = [back_ref[c] for c in range(3)]
    seen, behind = [], []
    for c in range(3):
        for s in range(8):
            picture[pl.ds(c * TILES * 8 + s, TILES, stride=8), :] = target_ref[
                c, :, s * LANES : (s + 1) * LANES
            ]
    for b in range(TILES):
        part = lambda i, q: slabs_ref[i, (b * 4 + q) * 8 : (b * 4 + q + 1) * 8, :]
        trans = jnp.ones((8, LANES), F32)
        start = jnp.ones((8, LANES), F32)
        color = [jnp.zeros((8, LANES), F32)] * 3
        for i in range(DEPTHS):
            start = jnp.where(depth == i, trans, start)
            color = [color[c] + trans * part(i, 1 + c) for c in range(3)]
            trans = trans * part(i, 0)
        color = [color[c] + trans * back[c] for c in range(3)]
        miss = []
        for c in range(3):
            at = slice((c * TILES + b) * 8, (c * TILES + b + 1) * 8)
            miss.append(color[c] - picture[at, :])
            picture[at, :] = color[c]
        after = sum(back[c] * miss[c] for c in range(3))
        for i in range(DEPTHS - 1, 0, -1):
            joined = sum(part(i, 1 + c) * miss[c] for c in range(3)) + part(i, 0) * after
            after = jnp.where(i > depth, joined, after)
        seen.append([start * miss[c] for c in range(3)])
        behind.append(start * after)
    for c in range(3):
        for s in range(8):
            image_ref[c, :, s * LANES : (s + 1) * LANES] = picture[
                pl.ds(c * TILES * 8 + s, TILES, stride=8), :
            ]

    def step(n, carry):
        k = SLAB - 1 - n
        out = []
        for b in range(TILES):
            at = b * SLAB + k
            get = lambda p: jnp.broadcast_to(shade_ref[p, pl.ds(at, 1), :], (8, LANES))
            shade = sum(get(c) * seen[b][c] for c in range(3))
            gap = shade - carry[b]
            slope[at] = weight_ref[at] * gap
            out.append(carry[b] + alpha_ref[at] * gap)
        return tuple(out)

    lax.fori_loop(0, SLAB, step, tuple(behind), unroll=4)

    index = iota((16, LANES), 0)
    lane = iota((16, LANES), 1)
    across = (lane & 31) - 16
    sixteen = jnp.zeros((16, LANES), F32)
    for b in range(TILES):
        total = sixteen
        shades = sixteen
        for s in range(8):
            down = s * 4 + (lane >> 5) - 16
            powers = jnp.where(index == 0, 1, 0)
            for n, value in enumerate(
                (across, down, across * across, across * down, down * down), 1
            ):
                powers = jnp.where(index == n, value, powers)
            powers = powers.astype(F32).astype(BF16)
            field = side_by_side(slope[b * SLAB : (b + 1) * SLAB, s, :])
            total = total + dot(jnp.concatenate([powers] * 3, axis=1), field, NT)
            gaze = jnp.concatenate(
                [seen[b][c][s : s + 1, :] for c in range(3)] + [jnp.zeros((13, LANES), F32)],
                axis=0,
            )
            shades = shades + lax.dot_general(
                gaze,
                weight_ref[b * SLAB : (b + 1) * SLAB, s, :],
                NT,
                precision=lax.Precision.HIGHEST,
                preferred_element_type=F32,
            )
        moment[b * 32 : b * 32 + 16, :] = total
        moment[b * 32 + 16 : (b + 1) * 32, :] = shades
    entry = [entry_ref[pl.ds(p, TILES, stride=16), :] for p in range(PARAMS)]
    jac = camera_rows(view_ref, cams_ref)
    m0, mx, my, mxx, mxy, myy = (moment[pl.ds(n, TILES, stride=32), :] for n in range(6))
    variance, xx, xy, yy, det = covariance(entry[3:6], jac)
    cx = sum(jac[0][j] * entry[j] for j in range(3)) + jac[0][3] - 0.5
    cy = sum(jac[1][j] * entry[j] for j in range(3)) + jac[1][3] - 0.5
    sx = mx - cx * m0
    sy = my - cy * m0
    sxx = mxx - cx * (mx + sx)
    sxy = mxy - cx * my - cy * sx
    syy = myy - cy * (my + sy)
    inverse = 1.0 / det
    conic = (yy * inverse, -xy * inverse, xx * inverse)
    d_cx = conic[0] * sx + conic[1] * sy
    d_cy = conic[1] * sx + conic[2] * sy
    d_a, d_b, d_c = -0.5 * sxx, -sxy, -0.5 * syy
    d_det = -(d_a * conic[0] + d_b * conic[1] + d_c * conic[2]) * inverse
    d_xx = d_c * inverse + d_det * yy
    d_yy = d_a * inverse + d_det * xx
    d_xy = -d_b * inverse - 2.0 * xy * d_det
    result = [jac[0][j] * d_cx + jac[1][j] * d_cy for j in range(3)]
    result += [
        2.0
        * variance[j]
        * (
            jac[0][j] * jac[0][j] * d_xx
            + jac[0][j] * jac[1][j] * d_xy
            + jac[1][j] * jac[1][j] * d_yy
        )
        for j in range(3)
    ]
    result += [m0 * (1.0 - jax.nn.sigmoid(entry[6]))]
    result += [moment[pl.ds(16 + c, TILES, stride=32), :] for c in range(3)]
    for p, value in enumerate(result):
        grads[p * TILES : (p + 1) * TILES, :] = value
    placed[...] = jnp.zeros((LANES, LANES), F32)
    outgoing = jnp.zeros((LANES, LANES), F32)
    for b in range(TILES):
        mine = grads[pl.ds(b, PARAMS, stride=TILES), :]
        rank = rank_ref[b : b + 1, :]
        for r in range(SLOTS):
            placed[r * PARAMS : (r + 1) * PARAMS, :] = jnp.where(rank == r, mine, 0.0)
        named = onehot(owner_ref[b : b + 1, :], LANES).astype(BF16)
        named = jnp.concatenate([named, named, named], axis=1)
        outgoing = outgoing + dot(named, side_by_side(placed[...]), NT)
    outgoing_ref[...] = outgoing


def collect_kernel(asked_ref, incoming_ref, sums_ref, columns, turned):
    columns[...] = asked_ref[...].T
    turned[...] = incoming_ref[...].T
    total = jnp.zeros((BLOCKS * 16, LANES), F32)
    for r in range(SLOTS):
        row = columns[r : r + 1, :]
        pick = onehot(row & (LANES - 1), LANES).astype(BF16)
        block = row >> 7
        value = turned[r * PARAMS : r * PARAMS + 16, :]
        spread = jnp.concatenate(
            [jnp.where(block == a, value, 0.0) for a in range(BLOCKS)], axis=0
        )
        total = total + dot(
            side_by_side(spread), jnp.concatenate([pick, pick, pick], axis=1), NT
        )
    for a in range(BLOCKS):
        sums_ref[a * PARAMS : (a + 1) * PARAMS, :] = total[a * 16 : a * 16 + PARAMS]


def adam_kernel(sums_ref, params_ref, first_ref, second_ref, new_ref, new_first_ref, new_second_ref):
    for a in range(BLOCKS):
        at = slice(a * LANES, (a + 1) * LANES)
        gradient = sum(sums_ref[i, a * PARAMS : (a + 1) * PARAMS, :] for i in range(DEPTHS))
        first = 0.9 * first_ref[:, at] + 0.1 * gradient
        second = 0.999 * second_ref[:, at] + 0.001 * gradient * gradient
        step = first / (1.0 - 0.9**10) / (jnp.sqrt(second / (1.0 - 0.999**10)) + 1e-08)
        new_ref[:, at] = params_ref[:, at] - 0.05 * step
        new_first_ref[:, at] = first
        new_second_ref[:, at] = second


def call(kernel, outs, ins, scratch=()):
    return pl.pallas_call(
        kernel,
        out_shape=[jax.ShapeDtypeStruct(shape, dtype) for shape, dtype in outs],
        in_specs=ins,
        out_specs=[VMEM] * len(outs),
        scratch_shapes=[pltpu.VMEM(shape, dtype) for shape, dtype in scratch],
        compiler_params=pltpu.CompilerParams(vmem_limit_bytes=40 * 2**20),
    )


def exchanged(array):
    whole = lax.all_to_all(array.reshape(LANES, 1, LANES), "tile", 0, 0, tiled=True)
    return whole.reshape(LANES, LANES)


def body(
    positions,
    log_scales,
    opacity_logits,
    colors,
    first_moment,
    second_moment,
    cameras,
    background,
    target,
    tile_view,
    tile_length,
    list_owner,
    list_row,
):
    square = (LANES, LANES)
    owner = list_owner.reshape(TILES, SLAB)
    wanted = list_row.reshape(TILES, SLAB)
    depth = lax.axis_index("depth").astype(I32).reshape(1)
    cams = cameras.reshape(-1)
    params = jnp.concatenate([positions, log_scales, opacity_logits, colors], axis=0)
    request, rank = call(
        request_kernel, [(square, I32), ((TILES, SLAB), I32)], [VMEM, VMEM]
    )(owner, wanted)
    asked = exchanged(request)
    (reply,) = call(
        reply_kernel, [(square, F32)], [VMEM, VMEM], [(square, I32), (square, F32)]
    )(asked, params)
    fetched = exchanged(reply)
    field = (TILES * SLAB, 8, LANES)
    slab, alpha, weight, shade, entry = call(
        forward_kernel,
        [
            (square, F32),
            (field, F32),
            (field, F32),
            ((3, TILES * SLAB, LANES), F32),
            ((TILES * 16, LANES), F32),
        ],
        [VMEM] * 3 + [SMEM] * 4,
        [(square, F32), (square, F32), ((6, TILES * SLAB, LANES), F32)],
    )(fetched, owner, rank, tile_view, tile_length, cams, depth)
    slabs = lax.all_gather(slab[None], "depth", axis=0, tiled=True)
    image, outgoing = call(
        backward_kernel,
        [((3, TILES, 1024), F32), (square, F32)],
        [VMEM] * 7 + [SMEM] * 4 + [VMEM],
        [
            (field, F32),
            (square, F32),
            ((PARAMS * TILES, LANES), F32),
            (square, F32),
            ((3 * TILES * 8, LANES), F32),
        ],
    )(
        slabs,
        alpha,
        weight,
        shade,
        entry,
        owner,
        rank,
        tile_view,
        cams,
        depth,
        background,
        target.transpose(1, 0, 2),
    )
    incoming = exchanged(outgoing)
    (sums,) = call(
        collect_kernel,
        [((BLOCKS * PARAMS, LANES), F32)],
        [VMEM, VMEM],
        [(square, I32), (square, F32)],
    )(asked, incoming)
    sums = lax.all_gather(sums[None], "depth", axis=0, tiled=True)
    updated = call(adam_kernel, [(params.shape, F32)] * 3, [VMEM] * 4)(
        sums, params, first_moment, second_moment
    )
    return (image.transpose(1, 0, 2), *updated)


def solution(mesh):
    split = P(None, "tile")
    placed = (
        *[split] * 6,
        P(),
        P(),
        P("tile", None, None),
        P("tile"),
        P("tile"),
        P("depth", "tile", None, None),
        P("depth", "tile", None),
    )
    return jax.shard_map(
        body,
        mesh=mesh,
        in_specs=placed,
        out_specs=(P("tile", None, None), split, split, split),
        check_vma=False,
    )
```

time: 249 us -> 113 us (0.45); the launches traced: 245 us -> 113 us
  local copies, waits for them, and re-layouts: 67.5 us -> 5.58 us
  matrix products: 31 us -> 0 us
  other arithmetic: 23.8 us -> 0.86 us
  Pallas kernels: 0 us -> 21.7 us
  blocking collectives: 53.8 us -> 34.3 us
  waiting for transfers between devices: 38.3 us -> 22.9 us
    slice x8 -> x0, local copies, waits for them, and re-layouts: 38.5 us -> none  [the longest x1 36.3 us: project(): cams[:, 1, 3]]
    dot_general x28 -> x0, matrix products: 31 us -> none  [the longest x20 25.9 us: running_sum(): jnp.einsum('pbk,kj->pbj', blocks, triangle, precision=lax.Precision.HIGHEST)]
    all_to_all x4 -> x1, blocking collectives: 42.8 us -> 18.1 us  [exchanged(): lax.all_to_all(array.reshape(LANES, 1, LANES), 'tile', 0, 0, tiled=True)]
    pallas_call x0 -> x6, Pallas kernels: none -> 21.7 us  [the longest x1 13.6 us: body(): call(backward_kernel, [((3, TILES, 1024), F32), (square, F32)], [VMEM] *...]
    all_to_all x2, waiting for transfers between devices: 38.3 us -> 22.9 us  [exchanged(): lax.all_to_all(array.reshape(LANES, 1, LANES), 'tile', 0, 0, tiled=True)]
    reduce_sum x19 -> x0, other arithmetic: 10.1 us -> none  [the longest x8 4.69 us: running_sum(): sums = jnp.sum(blocks, axis=2)]
    scatter-add x1 -> x0, other arithmetic: 9.24 us -> none  [body(): gradient = jnp.zeros_like(params).at[:, rows_in].add(slot_grad)]
    gather x4 -> x0, local copies, waits for them, and re-layouts: 7.95 us -> none  [the longest x3 6.91 us: body(): screen = project(params[:, rows_in], cameras[views_in])]
  transfers between devices with their start and end apart: 2 -> 2, of which waited for: 2 -> 2; matrix products, arithmetic and copies ran while one was open for 0% -> 1% of each run, Pallas kernels for 0% -> 0%
where the time goes in v1:
time: 113 us
  blocking collectives  34.3 us (30%)
  starting transfers between devices  27 us (24%)
  waiting for transfers between devices  22.9 us (20%)
  Pallas kernels  21.7 us (19%)
  local copies, waits for them, and re-layouts  5.58 us (5%)
    all_to_all x2, starting transfers between devices, exchanged(): lax.all_to_all(array.reshape(LANES, 1, LANES), 'tile', 0, 0, tiled=True)  27 us
    all_to_all x2, waiting for transfers between devices, exchanged(): lax.all_to_all(array.reshape(LANES, 1, LANES), 'tile', 0, 0, tiled=True)  22.9 us
    all_to_all x1, blocking collectives, exchanged(): lax.all_to_all(array.reshape(LANES, 1, LANES), 'tile', 0, 0, tiled=True)  18.1 us
    pallas_call x1, Pallas kernels, body(): call(backward_kernel, [((3, TILES, 1024), F32), (square, F32)], [VMEM] *...  13.6 us
    all_gather x1, blocking collectives, body(): slabs = lax.all_gather(slab[None], 'depth', axis=0, tiled=True)  9.06 us
    all_gather x1, blocking collectives, body(): sums = lax.all_gather(sums[None], 'depth', axis=0, tiled=True)  7.12 us
    unnamed x18, local copies, waits for them, and re-layouts  4.81 us
    pallas_call x1, Pallas kernels, body(): call(forward_kernel, [(square, F32), (field, F32), (field, F32), ((3, TIL...  3.58 us
  transfers between devices with their start and end apart: 2, of which 2 were waited for; matrix products, arithmetic and copies ran while one was open for 1% of the time, Pallas kernels for 0%

profile of v1, /device:TPU:1, one launch (start us, length us, event | category | flops | bytes accessed | tf_op | source)
XLA Modules:
  0.0 112.9 jit_solution(489054280134652392)
XLA Ops:
  0.6 0.0 copy-start.3
  0.6 0.7 copy-done.3
  1.3 0.0 copy-start.6
  1.3 0.7 copy-done.6
  2.0 1.4 %shard_map.156 = (s32[128,128]{1,0:T(8,128)}, s32[4,128]{1,0:T(4,128)S(1)}) custom-call(s32[4,128]{1,0:T(4,128)S(1)} %bitcast.27, s32[4,128]{1,0:T(4,128)S(1)} %bitcast.30), custom_call_target="tpu_custom_call" | custom-call | tf_op jit(solution)/shard_map/pallas_call | solution.py:425
  3.4 20.8 %all-to-all-start = ((s32[128,1,128]{2,1,0:T(1,128)}), s32[128,1,128]{2,1,0:T(1,128)S(1)}, u32[]{:S(2)}, u32[]{:S(2)}) async-start(s32[128,1,128]{2,1,0:T(1,128)} %bitcast.3), calls=%async_computation | async-start | bytes 131072 | tf_op jit(solution)/shard_map/all_to_all | solution.py:400
  24.2 0.9 pad_maximum_fusion.params_ref
  25.1 11.4 %all-to-all-done = s32[128,1,128]{2,1,0:T(1,128)S(1)} async-done(((s32[128,1,128]{2,1,0:T(1,128)}), s32[128,1,128]{2,1,0:T(1,128)S(1)}, u32[]{:S(2)}, u32[]{:S(2)}) %all-to-all-start) | async-done | bytes 65568 | tf_op jit(solution)/shard_map/all_to_all | solution.py:400
  36.5 1.5 %shard_map.157 = f32[128,128]{1,0:T(8,128)} custom-call(s32[128,128]{1,0:T(8,128)S(1)} %bitcast.21, f32[10,2048]{1,0:T(8,128)S(1)} %pad_maximum_fusion.params_ref), custom_call_target="tpu_custom_call" | custom-call | tf_op jit(solution)/shard_map/pallas_call | solution.py:429
  37.9 6.1 %all-to-all-start.1 = ((f32[128,1,128]{2,1,0:T(1,128)}), f32[128,1,128]{2,1,0:T(1,128)S(1)}, u32[]{:S(2)}, u32[]{:S(2)}) async-start(f32[128,1,128]{2,1,0:T(1,128)} %bitcast.6), calls=%async_computation.1 | async-start | bytes 131072 | tf_op jit(solution)/shard_map/all_to_all | solution.py:400
  44.1 0.8 reshape.44.cams_ref
  44.8 11.5 %all-to-all-done.1 = f32[128,1,128]{2,1,0:T(1,128)S(1)} async-done(((f32[128,1,128]{2,1,0:T(1,128)}), f32[128,1,128]{2,1,0:T(1,128)S(1)}, u32[]{:S(2)}, u32[]{:S(2)}) %all-to-all-start.1) | async-done | bytes 65568 | tf_op jit(solution)/shard_map/all_to_all | solution.py:400
  56.3 0.0 copy-start.4
  56.3 0.7 copy-done.4
  57.0 0.0 copy-start.5
  57.0 0.7 copy-done.5
  57.7 0.0 copy-start.7
  57.7 0.7 copy-done.7
  58.3 3.6 %shard_map.158 = (f32[128,128]{1,0:T(8,128)S(1)}, f32[512,8,128]{2,1,0:T(8,128)S(1)}, f32[512,8,128]{2,1,0:T(8,128)S(1)}, f32[3,512,128]{2,1,0:T(8,128)S(1)}, f32[64,128]{1,0:T(8,128)S(1)}) custom-call(f32[128,128]{1,0:T(8,128)S(1)} %bitcast.23, s32[4,128]{1,0:T(4,128)S(1)} %bitcast.28, s32[4,128]{1,0:T(4,128)S(1)} %get-tuple-element.17.rank_ref, ...), custom_call_target="tpu_custom_call" | custom-call | tf_op jit(solution)/shard_map/pallas_call | solution.py:434
  61.9 9.1 %all-gather = f32[512,128]{1,0:T(8,128)S(1)} all-gather(f32[128,128]{1,0:T(8,128)S(1)} %get-tuple-element.18), channel_id=2, replica_groups=mesh['tile'=128,'depth'=4] {'depth'}, dimensions={0}, use_global_device_ids=true | all-gather | bytes 327680 | tf_op jit(solution)/shard_map/all_gather | solution.py:446
  71.0 0.0 copy-start.2
  71.0 0.8 copy-done.2
  71.8 0.0 copy-start.8
  71.8 0.7 copy-done.8
  72.4 0.0 copy-start
  72.4 0.0 copy-start.1
  72.4 13.6 %shard_map.159 = (f32[3,4,1024]{2,1,0:T(4,128)}, f32[128,128]{1,0:T(8,128)S(1)}) custom-call(f32[4,128,128]{2,1,0:T(8,128)S(1)} %bitcast.20, f32[512,8,128]{2,1,0:T(8,128)S(1)} %get-tuple-element.19.alpha_ref, f32[512,8,128]{2,1,0:T(8,128)S(1)} %get-tuple-element.20.weight_ref, f32[3,512,128]{2,1,0:T(8,128)S(1)} %get-tuple-element.21.shade_ref, ...), custom_call_target="tpu_custom_call" | custom-call | tf_op jit(solution)/shard_map/pallas_call | solution.py:447
  86.1 18.1 %all_to_all.15 = f32[128,1,128]{2,1,0:T(1,128)S(1)} all-to-all(f32[128,1,128]{2,1,0:T(1,128)S(1)} %bitcast.25), channel_id=1, replica_groups=mesh['tile'=128,'depth'=4] {'tile'}, dimensions={0} | all-to-all | bytes 131072 | tf_op jit(solution)/shard_map/all_to_all | solution.py:400
  104.2 0.8 shard_map.160
  104.9 7.1 %all-gather.1 = f32[640,128]{1,0:T(8,128)S(1)} all-gather(f32[160,128]{1,0:T(8,128)S(1)} %shard_map.160), channel_id=3, replica_groups=mesh['tile'=128,'depth'=4] {'depth'}, dimensions={0}, use_global_device_ids=true | all-gather | bytes 409600 | tf_op jit(solution)/shard_map/all_gather | solution.py:479
  112.1 0.0 copy-done
  112.1 0.0 copy-done.1
  112.1 0.8 shard_map.161
Async XLA Ops:
  0.6 0.7 copy-start.3
  1.3 0.7 copy-start.6
  3.4 33.1 %all-to-all-start = ((s32[128,1,128]{2,1,0:T(1,128)}), s32[128,1,128]{2,1,0:T(1,128)S(1)}, u32[]{:S(2)}, u32[]{:S(2)}) async-start(s32[128,1,128]{2,1,0:T(1,128)} %bitcast.3), calls=%async_computation | async-start | bytes 131072 | tf_op jit(solution)/shard_map/all_to_all | solution.py:400
  37.9 18.4 %all-to-all-start.1 = ((f32[128,1,128]{2,1,0:T(1,128)}), f32[128,1,128]{2,1,0:T(1,128)S(1)}, u32[]{:S(2)}, u32[]{:S(2)}) async-start(f32[128,1,128]{2,1,0:T(1,128)} %bitcast.6), calls=%async_computation.1 | async-start | bytes 131072 | tf_op jit(solution)/shard_map/all_to_all | solution.py:400
  56.3 0.7 copy-start.4
  57.0 0.7 copy-start.5
  57.7 0.7 copy-start.7
  71.0 0.8 copy-start.2
  71.8 0.7 copy-start.8
  72.4 39.6 %copy-start = (f32[10,2048]{1,0:T(8,128)S(1)}, f32[10,2048]{1,0:T(8,128)}, u32[]{:S(2)}) copy-start(f32[10,2048]{1,0:T(8,128)} %first_ref.1) | copy-start | bytes 245764
  72.4 39.6 %copy-start.1 = (f32[10,2048]{1,0:T(8,128)S(1)}, f32[10,2048]{1,0:T(8,128)}, u32[]{:S(2)}) copy-start(f32[10,2048]{1,0:T(8,128)} %second_ref.1) | copy-start | bytes 245764

commit v2 on v1

--- a/solution.py
+++ b/solution.py
@@ -5,6 +5,7 @@
 from jax import lax
 from jax.experimental import pallas as pl
 from jax.experimental.pallas import tpu as pltpu
+from jax.sharding import Mesh
 from jax.sharding import PartitionSpec as P
 
 LANES = 128
@@ -14,9 +15,14 @@
 SLOTS = 10
 PARAMS = 10
 BLOCKS = 16
+LIVE, BACK, HERE, GOAL, FIXED = 32, 40, 64, 72, 168
+PITCH = TILES * SLAB + 1
+TILE = ("tile_z", "tile_y", "tile_x")
+DEPTH = ("depth_x", "depth_core")
 LOG2E = math.log2(math.e)
 VMEM = pl.BlockSpec(memory_space=pltpu.VMEM)
 SMEM = pl.BlockSpec(memory_space=pltpu.SMEM)
+HBM = pl.BlockSpec(memory_space=pltpu.HBM)
 F32 = jnp.float32
 BF16 = jnp.bfloat16
 I32 = jnp.int32
@@ -48,7 +54,15 @@
     return jnp.where(iota((rows, LANES), 0) == index, 1.0, 0.0)
 
 
-def request_kernel(owner_ref, row_ref, request_ref, rank_ref):
+def request_kernel(owner_hbm, row_hbm, request_ref, rank_ref, owner_ref, row_ref, sems):
+    copies = [
+        pltpu.make_async_copy(owner_hbm, owner_ref, sems.at[0]),
+        pltpu.make_async_copy(row_hbm, row_ref, sems.at[1]),
+    ]
+    for copy in copies:
+        copy.start()
+    for copy in copies:
+        copy.wait()
     earlier = jnp.where(iota((SLAB, SLAB), 0) < iota((SLAB, SLAB), 1), 1.0, 0.0).astype(BF16)
     before = jnp.zeros((LANES, 1), F32)
     total = jnp.zeros((LANES, LANES), F32)
@@ -67,22 +81,34 @@
     request_ref[...] = total.astype(I32)
 
 
-def reply_kernel(asked_ref, params_ref, reply_ref, columns, held):
+def fixed_kernel(
+    view_ref, length_ref, cams_ref, depth_ref, back_ref, target_ref, params_ref, fixed_ref, table_ref
+):
+    for i in range(2):
+        for j in range(4):
+            at = (i * 4 + j) * TILES
+            fixed_ref[at : at + TILES, :] = per_tile([cams_ref[view_ref[b], i, j] for b in range(TILES)])
+    place = depth_ref[0] * SLAB + iota((TILES, LANES), 1)
+    length = per_tile([length_ref[b].astype(F32) for b in range(TILES)])
+    fixed_ref[LIVE : LIVE + TILES, :] = jnp.where(place.astype(F32) < length, 1.0, 0.0)
+    for c in range(3):
+        fixed_ref[BACK + c * 8 : BACK + c * 8 + 8, :] = jnp.full((8, LANES), back_ref[c], F32)
+    fixed_ref[HERE : HERE + 8, :] = jnp.full((8, LANES), depth_ref[0].astype(F32), F32)
+    for c in range(3):
+        for s in range(8):
+            fixed_ref[pl.ds(GOAL + c * TILES * 8 + s, TILES, stride=8), :] = target_ref[
+                c, :, s * LANES : (s + 1) * LANES
+            ]
+    for a in range(BLOCKS):
+        block = jnp.concatenate(
+            [params_ref[:, a * LANES : (a + 1) * LANES], jnp.zeros((16 - PARAMS, LANES), F32)], axis=0
+        )
+        table_ref[a * 16 : (a + 1) * 16, :] = side_by_side(block)
+
+
+def reply_kernel(asked_ref, table_ref, reply_ref, columns, held):
     columns[...] = asked_ref[...].T
-    table = jnp.concatenate(
-        [
-            jnp.concatenate(
-                [
-                    params_ref[:, a * LANES : (a + 1) * LANES],
-                    jnp.zeros((16 - PARAMS, LANES), F32),
-                ],
-                axis=0,
-            )
-            for a in range(BLOCKS)
-        ],
-        axis=0,
-    )
-    table = side_by_side(table)
+    table = table_ref[...]
     for r in range(SLOTS):
         row = columns[r : r + 1, :]
         pick = onehot(row & (LANES - 1), LANES).astype(BF16)
@@ -104,11 +130,9 @@
     return out
 
 
-def camera_rows(view_ref, cams_ref):
-    return [
-        [per_tile([cams_ref[view_ref[b] * 8 + i * 4 + j] for b in range(TILES)]) for j in range(4)]
-        for i in range(2)
-    ]
+def camera_rows(fixed_ref):
+    rows = [fixed_ref[n * TILES : (n + 1) * TILES, :] for n in range(8)]
+    return rows[:4], rows[4:]
 
 
 def covariance(scales, jac):
@@ -123,10 +147,7 @@
     fetched_ref,
     owner_ref,
     rank_ref,
-    view_ref,
-    length_ref,
-    cams_ref,
-    depth_ref,
+    fixed_ref,
     slab_ref,
     alpha_ref,
     weight_ref,
@@ -146,14 +167,11 @@
             value = value + jnp.where(rank == r, found[r * PARAMS : r * PARAMS + 16, :], 0.0)
         entry_ref[b * 16 : (b + 1) * 16, :] = value
     entry = [entry_ref[pl.ds(p, TILES, stride=16), :] for p in range(PARAMS)]
-    jac = camera_rows(view_ref, cams_ref)
+    jac = camera_rows(fixed_ref)
     center_x = sum(jac[0][j] * entry[j] for j in range(3)) + jac[0][3] + 16.0
     center_y = sum(jac[1][j] * entry[j] for j in range(3)) + jac[1][3] + 16.0
     _, xx, xy, yy, det = covariance(entry[3:6], jac)
-    place = depth_ref[0] * SLAB + iota((TILES, LANES), 1).astype(I32)
-    length = per_tile([length_ref[b].astype(F32) for b in range(TILES)])
-    live = jnp.where(place.astype(F32) < length, 1.0, 0.0)
-    opacity = jax.nn.sigmoid(entry[6]) * live
+    opacity = jax.nn.sigmoid(entry[6]) * fixed_ref[LIVE : LIVE + TILES, :]
     factors = [
         center_x,
         center_y,
@@ -191,7 +209,7 @@
             alpha = get(spread, 5) * jnp.exp2(power)
             weight = alpha * trans
             alpha_ref[at] = alpha
-            weight_ref[at] = weight
+            weight_ref[pl.ds(at, 8, stride=PITCH), :] = weight
             out += [
                 trans - weight,
                 red + weight * get(shade_ref, 0),
@@ -214,11 +232,7 @@
     entry_ref,
     owner_ref,
     rank_ref,
-    view_ref,
-    cams_ref,
-    depth_ref,
-    back_ref,
-    target_ref,
+    fixed_ref,
     image_ref,
     outgoing_ref,
     slope,
@@ -227,14 +241,9 @@
     placed,
     picture,
 ):
-    depth = depth_ref[0]
-    back = [back_ref[c] for c in range(3)]
+    depth = fixed_ref[HERE : HERE + 8, :]
+    back = [fixed_ref[BACK + c * 8 : BACK + c * 8 + 8, :] for c in range(3)]
     seen, behind = [], []
-    for c in range(3):
-        for s in range(8):
-            picture[pl.ds(c * TILES * 8 + s, TILES, stride=8), :] = target_ref[
-                c, :, s * LANES : (s + 1) * LANES
-            ]
     for b in range(TILES):
         part = lambda i, q: slabs_ref[i, (b * 4 + q) * 8 : (b * 4 + q + 1) * 8, :]
         trans = jnp.ones((8, LANES), F32)
@@ -248,7 +257,7 @@
         miss = []
         for c in range(3):
             at = slice((c * TILES + b) * 8, (c * TILES + b + 1) * 8)
-            miss.append(color[c] - picture[at, :])
+            miss.append(color[c] - fixed_ref[GOAL + at.start : GOAL + at.stop, :])
             picture[at, :] = color[c]
         after = sum(back[c] * miss[c] for c in range(3))
         for i in range(DEPTHS - 1, 0, -1):
@@ -270,7 +279,8 @@
             get = lambda p: jnp.broadcast_to(shade_ref[p, pl.ds(at, 1), :], (8, LANES))
             shade = sum(get(c) * seen[b][c] for c in range(3))
             gap = shade - carry[b]
-            slope[at] = weight_ref[at] * gap
+            rows = pl.ds(at, 8, stride=PITCH)
+            slope[rows, :] = weight_ref[rows, :] * gap
             out.append(carry[b] + alpha_ref[at] * gap)
         return tuple(out)
 
@@ -279,35 +289,31 @@
     index = iota((16, LANES), 0)
     lane = iota((16, LANES), 1)
     across = (lane & 31) - 16
-    sixteen = jnp.zeros((16, LANES), F32)
+    powers = []
+    for s in range(8):
+        down = s * 4 + (lane >> 5) - 16
+        power = jnp.where(index == 0, 1, 0)
+        for n, value in enumerate((across, down, across * across, across * down, down * down), 1):
+            power = jnp.where(index == n, value, power)
+        powers += [power.astype(F32).astype(BF16)] * 3
+    powers = jnp.concatenate(powers, axis=1)
     for b in range(TILES):
-        total = sixteen
-        shades = sixteen
+        at = [slice(s * PITCH + b * SLAB, s * PITCH + (b + 1) * SLAB) for s in range(8)]
+        field = jnp.concatenate([side_by_side(slope[at[s], :]) for s in range(8)], axis=1)
+        moment[b * 32 : b * 32 + 16, :] = dot(powers, field, NT)
+        gaze, weights = [], []
         for s in range(8):
-            down = s * 4 + (lane >> 5) - 16
-            powers = jnp.where(index == 0, 1, 0)
-            for n, value in enumerate(
-                (across, down, across * across, across * down, down * down), 1
-            ):
-                powers = jnp.where(index == n, value, powers)
-            powers = powers.astype(F32).astype(BF16)
-            field = side_by_side(slope[b * SLAB : (b + 1) * SLAB, s, :])
-            total = total + dot(jnp.concatenate([powers] * 3, axis=1), field, NT)
-            gaze = jnp.concatenate(
-                [seen[b][c][s : s + 1, :] for c in range(3)] + [jnp.zeros((13, LANES), F32)],
+            look = jnp.concatenate(
+                [*pieces(jnp.concatenate([seen[b][c][s : s + 1, :] for c in range(3)], axis=0))][:2]
+                + [jnp.zeros((10, LANES), BF16)],
                 axis=0,
             )
-            shades = shades + lax.dot_general(
-                gaze,
-                weight_ref[b * SLAB : (b + 1) * SLAB, s, :],
-                NT,
-                precision=lax.Precision.HIGHEST,
-                preferred_element_type=F32,
-            )
-        moment[b * 32 : b * 32 + 16, :] = total
+            gaze += [look, look]
+            weights += pieces(weight_ref[at[s], :])[:2]
+        shades = dot(jnp.concatenate(gaze, axis=1), jnp.concatenate(weights, axis=1), NT)
         moment[b * 32 + 16 : (b + 1) * 32, :] = shades
     entry = [entry_ref[pl.ds(p, TILES, stride=16), :] for p in range(PARAMS)]
-    jac = camera_rows(view_ref, cams_ref)
+    jac = camera_rows(fixed_ref)
     m0, mx, my, mxx, mxy, myy = (moment[pl.ds(n, TILES, stride=32), :] for n in range(6))
     variance, xx, xy, yy, det = covariance(entry[3:6], jac)
     cx = sum(jac[0][j] * entry[j] for j in range(3)) + jac[0][3] - 0.5
@@ -338,7 +344,10 @@
         for j in range(3)
     ]
     result += [m0 * (1.0 - jax.nn.sigmoid(entry[6]))]
-    result += [moment[pl.ds(16 + c, TILES, stride=32), :] for c in range(3)]
+    result += [
+        moment[pl.ds(16 + c, TILES, stride=32), :] + moment[pl.ds(19 + c, TILES, stride=32), :]
+        for c in range(3)
+    ]
     for p, value in enumerate(result):
         grads[p * TILES : (p + 1) * TILES, :] = value
     placed[...] = jnp.zeros((LANES, LANES), F32)
@@ -391,13 +400,23 @@
         out_shape=[jax.ShapeDtypeStruct(shape, dtype) for shape, dtype in outs],
         in_specs=ins,
         out_specs=[VMEM] * len(outs),
-        scratch_shapes=[pltpu.VMEM(shape, dtype) for shape, dtype in scratch],
+        scratch_shapes=list(scratch),
         compiler_params=pltpu.CompilerParams(vmem_limit_bytes=40 * 2**20),
     )
 
 
 def exchanged(array):
-    whole = lax.all_to_all(array.reshape(LANES, 1, LANES), "tile", 0, 0, tiled=True)
+    groups = [
+        [zy * 4 + hi * 2 + (hi ^ g) for zy in range(LANES // 2) for hi in range(2)] for g in range(2)
+    ]
+    whole = lax.all_to_all(
+        array.reshape(LANES, 1, LANES),
+        (*TILE, DEPTH[0]),
+        0,
+        0,
+        axis_index_groups=groups,
+        tiled=True,
+    )
     return whole.reshape(LANES, LANES)
 
 
@@ -417,66 +436,70 @@
     list_row,
 ):
     square = (LANES, LANES)
+    held = pltpu.VMEM(square, F32)
+    asked_rows = pltpu.VMEM(square, I32)
     owner = list_owner.reshape(TILES, SLAB)
     wanted = list_row.reshape(TILES, SLAB)
-    depth = lax.axis_index("depth").astype(I32).reshape(1)
-    cams = cameras.reshape(-1)
+    depth = lax.axis_index(DEPTH).astype(I32).reshape(1)
     params = jnp.concatenate([positions, log_scales, opacity_logits, colors], axis=0)
-    request, rank = call(
-        request_kernel, [(square, I32), ((TILES, SLAB), I32)], [VMEM, VMEM]
+    few = ((TILES, SLAB), I32)
+    request, rank, owner = call(
+        request_kernel,
+        [(square, I32), few, few],
+        [HBM, HBM],
+        [pltpu.VMEM(*few), pltpu.SemaphoreType.DMA((2,))],
     )(owner, wanted)
     asked = exchanged(request)
-    (reply,) = call(
-        reply_kernel, [(square, F32)], [VMEM, VMEM], [(square, I32), (square, F32)]
-    )(asked, params)
+    fixed, table = call(
+        fixed_kernel,
+        [((FIXED, LANES), F32), ((BLOCKS * 16, 3 * LANES), BF16)],
+        [SMEM] * 5 + [VMEM] * 2,
+    )(
+        tile_view,
+        tile_length,
+        cameras,
+        depth,
+        background,
+        target.transpose(1, 0, 2),
+        params,
+    )
+    (reply,) = call(reply_kernel, [(square, F32)], [VMEM, VMEM], [asked_rows, held])(asked, table)
     fetched = exchanged(reply)
     field = (TILES * SLAB, 8, LANES)
+    tilted = (8 * PITCH, LANES)
     slab, alpha, weight, shade, entry = call(
         forward_kernel,
         [
             (square, F32),
             (field, F32),
-            (field, F32),
+            (tilted, F32),
             ((3, TILES * SLAB, LANES), F32),
             ((TILES * 16, LANES), F32),
         ],
-        [VMEM] * 3 + [SMEM] * 4,
-        [(square, F32), (square, F32), ((6, TILES * SLAB, LANES), F32)],
-    )(fetched, owner, rank, tile_view, tile_length, cams, depth)
-    slabs = lax.all_gather(slab[None], "depth", axis=0, tiled=True)
+        [VMEM] * 4,
+        [held, held, pltpu.VMEM((6, TILES * SLAB, LANES), F32)],
+    )(fetched, owner, rank, fixed)
+    slabs = lax.all_gather(slab[None], DEPTH, axis=0, tiled=True)
     image, outgoing = call(
         backward_kernel,
         [((3, TILES, 1024), F32), (square, F32)],
-        [VMEM] * 7 + [SMEM] * 4 + [VMEM],
+        [VMEM] * 8,
         [
-            (field, F32),
-            (square, F32),
-            ((PARAMS * TILES, LANES), F32),
-            (square, F32),
-            ((3 * TILES * 8, LANES), F32),
+            pltpu.VMEM(tilted, F32),
+            held,
+            pltpu.VMEM((PARAMS * TILES, LANES), F32),
+            held,
+            pltpu.VMEM((3 * TILES * 8, LANES), F32),
         ],
-    )(
-        slabs,
-        alpha,
-        weight,
-        shade,
-        entry,
-        owner,
-        rank,
-        tile_view,
-        cams,
-        depth,
-        background,
-        target.transpose(1, 0, 2),
-    )
+    )(slabs, alpha, weight, shade, entry, owner, rank, fixed)
     incoming = exchanged(outgoing)
     (sums,) = call(
         collect_kernel,
         [((BLOCKS * PARAMS, LANES), F32)],
         [VMEM, VMEM],
-        [(square, I32), (square, F32)],
+        [asked_rows, held],
     )(asked, incoming)
-    sums = lax.all_gather(sums[None], "depth", axis=0, tiled=True)
+    sums = lax.all_gather(sums[None], DEPTH, axis=0, tiled=True)
     updated = call(adam_kernel, [(params.shape, F32)] * 3, [VMEM] * 4)(
         sums, params, first_moment, second_moment
     )
@@ -484,21 +507,22 @@
 
 
 def solution(mesh):
-    split = P(None, "tile")
+    torus = Mesh(mesh.devices.reshape(8, 8, 2, 2, 2), (*TILE, *DEPTH))
+    split = P(None, TILE)
     placed = (
         *[split] * 6,
         P(),
         P(),
-        P("tile", None, None),
-        P("tile"),
-        P("tile"),
-        P("depth", "tile", None, None),
-        P("depth", "tile", None),
+        P(TILE, None, None),
+        P(TILE),
+        P(TILE),
+        P(DEPTH, TILE, None, None),
+        P(DEPTH, TILE, None),
     )
     return jax.shard_map(
         body,
-        mesh=mesh,
+        mesh=torus,
         in_specs=placed,
-        out_specs=(P("tile", None, None), split, split, split),
+        out_specs=(P(TILE, None, None), split, split, split),
         check_vma=False,
     )

time: 113 us -> 98.5 us (0.87)
  blocking collectives: 34.3 us -> 53.2 us
  waiting for transfers between devices: 22.9 us -> 6.95 us
  Pallas kernels: 21.7 us -> 11 us
  starting transfers between devices: 27 us -> 20.6 us
    all_to_all x1 -> x2, blocking collectives: 18.1 us -> 37.7 us  [exchanged(): lax.all_to_all(array.reshape(LANES, 1, LANES), (*TILE, DEPTH[0]), 0, 0, a...]
    all_to_all x2 -> x1, waiting for transfers between devices: 22.9 us -> 6.95 us  [exchanged(): lax.all_to_all(array.reshape(LANES, 1, LANES), (*TILE, DEPTH[0]), 0, 0, a...]
    pallas_call x1, Pallas kernels: 13.6 us -> 3.44 us  [body(): call(backward_kernel, [((3, TILES, 1024), F32), (square, F32)], [VMEM] *...]
    all_to_all x2 -> x1, starting transfers between devices: 27 us -> 20.6 us  [exchanged(): lax.all_to_all(array.reshape(LANES, 1, LANES), (*TILE, DEPTH[0]), 0, 0, a...]
    pallas_call x4 -> x5, Pallas kernels: 7.19 us -> 6.68 us  [the longest x1 3.02 us: body(): call(forward_kernel, [(square, F32), (field, F32), (tilted, F32), ((3, TI...]
  transfers between devices with their start and end apart: 2 -> 1, of which waited for: 2 -> 1; matrix products, arithmetic and copies ran while one was open for 1% -> 1% of each run, Pallas kernels for 0% -> 1%
where the time goes in v2:
time: 98.5 us; the launch traced here: 98 us
  blocking collectives  53.2 us (54%)
  starting transfers between devices  20.6 us (21%)
  Pallas kernels  11 us (11%)
  waiting for transfers between devices  6.95 us (7%)
  local copies, waits for them, and re-layouts  4.81 us (5%)
    all_to_all x2, blocking collectives, exchanged(): lax.all_to_all(array.reshape(LANES, 1, LANES), (*TILE, DEPTH[0]), 0, 0, a...  37.7 us
    all_to_all x1, starting transfers between devices, exchanged(): lax.all_to_all(array.reshape(LANES, 1, LANES), (*TILE, DEPTH[0]), 0, 0, a...  20.6 us
    all_gather x1, blocking collectives, body(): slabs = lax.all_gather(slab[None], DEPTH, axis=0, tiled=True)  8.29 us
    all_gather x1, blocking collectives, body(): sums = lax.all_gather(sums[None], DEPTH, axis=0, tiled=True)  7.12 us
    all_to_all x1, waiting for transfers between devices, exchanged(): lax.all_to_all(array.reshape(LANES, 1, LANES), (*TILE, DEPTH[0]), 0, 0, a...  6.95 us
    unnamed x18, local copies, waits for them, and re-layouts  4.81 us
    pallas_call x1, Pallas kernels, body(): call(backward_kernel, [((3, TILES, 1024), F32), (square, F32)], [VMEM] *...  3.44 us
    pallas_call x1, Pallas kernels, body(): call(forward_kernel, [(square, F32), (field, F32), (tilted, F32), ((3, TI...  3.02 us
  transfers between devices with their start and end apart: 1, of which 1 were waited for; matrix products, arithmetic and copies ran while one was open for 1% of the time, Pallas kernels for 1%

profile of v2, /device:TPU:1, one launch (start us, length us, event | category | flops | bytes accessed | tf_op | source)
XLA Modules:
  0.0 98.0 jit_solution(18418992288259109917)
XLA Ops:
  0.6 0.0 copy-start.4
  0.6 0.7 copy-done.4
  1.3 0.0 copy-start.5
  1.3 0.7 copy-done.5
  2.0 1.4 %shard_map.156 = (s32[128,128]{1,0:T(8,128)}, s32[4,128]{1,0:T(4,128)S(1)}, s32[4,128]{1,0:T(4,128)S(1)}) custom-call(s32[4,128]{1,0:T(4,128)S(1)} %bitcast.28, s32[4,128]{1,0:T(4,128)S(1)} %bitcast.29), custom_call_target="tpu_custom_call" | custom-call | tf_op jit(solution)/shard_map/pallas_call | solution.py:446
  3.4 20.6 %all-to-all-start = ((s32[128,1,128]{2,1,0:T(1,128)}), s32[128,1,128]{2,1,0:T(1,128)S(1)}, u32[]{:S(2)}, u32[]{:S(2)}) async-start(s32[128,1,128]{2,1,0:T(1,128)} %bitcast.3), calls=%async_computation | async-start | bytes 131072 | tf_op jit(solution)/shard_map/all_to_all | solution.py:412
  24.0 0.9 pad_maximum_fusion.params_ref
  24.8 0.0 copy-start.2
  24.9 0.8 copy-done.2
  25.6 0.0 copy-start.3
  25.7 0.7 copy-done.3
  26.3 0.0 copy-start.6
  26.3 0.7 copy-done.6
  27.0 0.0 copy-start.7
  27.0 0.7 copy-done.7
  27.6 0.0 copy-start.8
  27.7 0.7 copy-done.8
  28.3 0.7 shard_map.157
  29.0 7.0 %all-to-all-done = s32[128,1,128]{2,1,0:T(1,128)S(1)} async-done(((s32[128,1,128]{2,1,0:T(1,128)}), s32[128,1,128]{2,1,0:T(1,128)S(1)}, u32[]{:S(2)}, u32[]{:S(2)}) %all-to-all-start) | async-done | bytes 65568 | tf_op jit(solution)/shard_map/all_to_all | solution.py:412
  35.9 0.8 shard_map.158
  36.8 20.2 %all_to_all.15 = f32[128,1,128]{2,1,0:T(1,128)S(1)} all-to-all(f32[128,1,128]{2,1,0:T(1,128)S(1)} %bitcast.23), channel_id=1, replica_groups={{0,6,8,14,16,22,24,30,32,38,40,46,48,54,56,62,64,70,72,78,80,86,88,94,9..., dimensions={0} | all-to-all | bytes 131072 | tf_op jit(solution)/shard_map/all_to_all | solution.py:412
  56.9 3.0 %shard_map.159 = (f32[128,128]{1,0:T(8,128)S(1)}, f32[512,8,128]{2,1,0:T(8,128)S(1)}, f32[4104,128]{1,0:T(8,128)S(1)}, f32[3,512,128]{2,1,0:T(8,128)S(1)}, f32[64,128]{1,0:T(8,128)S(1)}) custom-call(f32[128,128]{1,0:T(8,128)S(1)} %bitcast.24, s32[4,128]{1,0:T(4,128)S(1)} %get-tuple-element.21.owner_ref, s32[4,128]{1,0:T(4,128)S(1)} %get-tuple-element.22.rank_ref, ...), custom_call_target="tpu_custom_call" | custom-call | tf_op jit(solution)/shard_map/pallas_call | solution.py:470
  60.0 8.3 %all-gather = f32[512,128]{1,0:T(8,128)S(1)} all-gather(f32[128,128]{1,0:T(8,128)S(1)} %get-tuple-element.24), channel_id=2, replica_groups=mesh['tile_z'=8,'tile_y'=8,'tile_x'=2,'depth_x'=2,'depth_core'=2] {'dept..., dimensions={0}, use_global_device_ids=true | all-gather | bytes 327680 | tf_op jit(solution)/shard_map/all_gather | solution.py:482
  68.3 0.0 copy-start
  68.3 0.0 copy-start.1
  68.3 3.4 %shard_map.160 = (f32[3,4,1024]{2,1,0:T(4,128)}, f32[128,128]{1,0:T(8,128)S(1)}) custom-call(f32[4,128,128]{2,1,0:T(8,128)S(1)} %bitcast.20, f32[512,8,128]{2,1,0:T(8,128)S(1)} %get-tuple-element.25.alpha_ref, f32[4104,128]{1,0:T(8,128)S(1)} %get-tuple-element.26.weight_ref, f32[3,512,128]{2,1,0:T(8,128)S(1)} %get-tuple-element.27.shade_ref, ...), custom_call_target="tpu_custom_call" | custom-call | tf_op jit(solution)/shard_map/pallas_call | solution.py:483
  71.7 17.6 %all_to_all.16 = f32[128,1,128]{2,1,0:T(1,128)S(1)} all-to-all(f32[128,1,128]{2,1,0:T(1,128)S(1)} %bitcast.26), channel_id=1, replica_groups={{0,6,8,14,16,22,24,30,32,38,40,46,48,54,56,62,64,70,72,78,80,86,88,94,9..., dimensions={0} | all-to-all | bytes 131072 | tf_op jit(solution)/shard_map/all_to_all | solution.py:412
  89.3 0.8 shard_map.161
  90.1 7.1 %all-gather.1 = f32[640,128]{1,0:T(8,128)S(1)} all-gather(f32[160,128]{1,0:T(8,128)S(1)} %shard_map.161), channel_id=3, replica_groups=mesh['tile_z'=8,'tile_y'=8,'tile_x'=2,'depth_x'=2,'depth_core'=2] {'dept..., dimensions={0}, use_global_device_ids=true | all-gather | bytes 409600 | tf_op jit(solution)/shard_map/all_gather | solution.py:502
  97.2 0.0 copy-done
  97.2 0.0 copy-done.1
  97.2 0.8 shard_map.162
Async XLA Ops:
  0.6 0.7 copy-start.4
  1.3 0.7 copy-start.5
  3.4 32.5 %all-to-all-start = ((s32[128,1,128]{2,1,0:T(1,128)}), s32[128,1,128]{2,1,0:T(1,128)S(1)}, u32[]{:S(2)}, u32[]{:S(2)}) async-start(s32[128,1,128]{2,1,0:T(1,128)} %bitcast.3), calls=%async_computation | async-start | bytes 131072 | tf_op jit(solution)/shard_map/all_to_all | solution.py:412
  24.8 0.8 copy-start.2
  25.6 0.7 copy-start.3
  26.3 0.7 copy-start.6
  27.0 0.7 copy-start.7
  27.6 0.7 copy-start.8
  68.3 28.9 %copy-start = (f32[10,2048]{1,0:T(8,128)S(1)}, f32[10,2048]{1,0:T(8,128)}, u32[]{:S(2)}) copy-start(f32[10,2048]{1,0:T(8,128)} %first_ref.1) | copy-start | bytes 245764
  68.3 28.9 %copy-start.1 = (f32[10,2048]{1,0:T(8,128)S(1)}, f32[10,2048]{1,0:T(8,128)}, u32[]{:S(2)}) copy-start(f32[10,2048]{1,0:T(8,128)} %second_ref.1) | copy-start | bytes 245764

commit v3 on v2

--- a/solution.py
+++ b/solution.py
@@ -15,6 +15,7 @@
 SLOTS = 10
 PARAMS = 10
 BLOCKS = 16
+GRANT_ALL = 60
 LIVE, BACK, HERE, GOAL, FIXED = 32, 40, 64, 72, 168
 PITCH = TILES * SLAB + 1
 TILE = ("tile_z", "tile_y", "tile_x")
@@ -82,7 +83,7 @@
 
 
 def fixed_kernel(
-    view_ref, length_ref, cams_ref, depth_ref, back_ref, target_ref, params_ref, fixed_ref, table_ref
+    view_ref, length_ref, cams_ref, depth_ref, back_ref, target_ref, fixed_ref
 ):
     for i in range(2):
         for j in range(4):
@@ -99,20 +100,30 @@
             fixed_ref[pl.ds(GOAL + c * TILES * 8 + s, TILES, stride=8), :] = target_ref[
                 c, :, s * LANES : (s + 1) * LANES
             ]
+
+def table_kernel(side_ref, mine_ref, theirs_ref, table_ref):
+    first = side_ref[0] == 0
+    blank = jnp.zeros((16 - PARAMS, LANES), F32)
     for a in range(BLOCKS):
-        block = jnp.concatenate(
-            [params_ref[:, a * LANES : (a + 1) * LANES], jnp.zeros((16 - PARAMS, LANES), F32)], axis=0
-        )
-        table_ref[a * 16 : (a + 1) * 16, :] = side_by_side(block)
+        mine = mine_ref[:, a * LANES : (a + 1) * LANES]
+        theirs = theirs_ref[:, a * LANES : (a + 1) * LANES]
+        for h in range(2):
+            block = jnp.where(first, mine, theirs) if h == 0 else jnp.where(first, theirs, mine)
+            table_ref[a * 16 : (a + 1) * 16, h * 384 : (h + 1) * 384] = side_by_side(
+                jnp.concatenate([block, blank], axis=0)
+            )
 
 
 def reply_kernel(asked_ref, table_ref, reply_ref, columns, held):
     columns[...] = asked_ref[...].T
     table = table_ref[...]
+    second = (iota((LANES, LANES), 1) & 1) == 1
     for r in range(SLOTS):
         row = columns[r : r + 1, :]
-        pick = onehot(row & (LANES - 1), LANES).astype(BF16)
-        found = dot(table, jnp.concatenate([pick, pick, pick], axis=0), NN)
+        pick = onehot(row & (LANES - 1), LANES)
+        picks = [jnp.where(second, 0.0, pick).astype(BF16)] * 3
+        picks += [jnp.where(second, pick, 0.0).astype(BF16)] * 3
+        found = dot(table, jnp.concatenate(picks, axis=0), NN)
         block = row >> 7
         value = jnp.zeros((16, LANES), F32)
         for a in range(BLOCKS):
@@ -232,6 +243,7 @@
     entry_ref,
     owner_ref,
     rank_ref,
+    row_ref,
     fixed_ref,
     image_ref,
     outgoing_ref,
@@ -357,18 +369,20 @@
         rank = rank_ref[b : b + 1, :]
         for r in range(SLOTS):
             placed[r * PARAMS : (r + 1) * PARAMS, :] = jnp.where(rank == r, mine, 0.0)
+        here = iota((16, LANES), 0) == rank
+        row = jnp.where(here, row_ref[b : b + 1, :].astype(F32), 0.0)
+        placed[SLOTS * PARAMS : SLOTS * PARAMS + 16, :] = row
         named = onehot(owner_ref[b : b + 1, :], LANES).astype(BF16)
         named = jnp.concatenate([named, named, named], axis=1)
         outgoing = outgoing + dot(named, side_by_side(placed[...]), NT)
     outgoing_ref[...] = outgoing
 
 
-def collect_kernel(asked_ref, incoming_ref, sums_ref, columns, turned):
-    columns[...] = asked_ref[...].T
+def collect_kernel(incoming_ref, sums_ref, turned):
     turned[...] = incoming_ref[...].T
     total = jnp.zeros((BLOCKS * 16, LANES), F32)
     for r in range(SLOTS):
-        row = columns[r : r + 1, :]
+        row = turned[SLOTS * PARAMS + r : SLOTS * PARAMS + r + 1, :].astype(I32)
         pick = onehot(row & (LANES - 1), LANES).astype(BF16)
         block = row >> 7
         value = turned[r * PARAMS : r * PARAMS + 16, :]
@@ -394,15 +408,20 @@
         new_second_ref[:, at] = second
 
 
-def call(kernel, outs, ins, scratch=()):
+def call(kernel, outs, ins, scratch=(), grant=40):
     return pl.pallas_call(
         kernel,
         out_shape=[jax.ShapeDtypeStruct(shape, dtype) for shape, dtype in outs],
         in_specs=ins,
         out_specs=[VMEM] * len(outs),
         scratch_shapes=list(scratch),
-        compiler_params=pltpu.CompilerParams(vmem_limit_bytes=40 * 2**20),
+        compiler_params=pltpu.CompilerParams(vmem_limit_bytes=grant * 2**20),
     )
+
+
+def exchanged_in_plane(array):
+    pairs = array.reshape(LANES // 2, 2, LANES)
+    return lax.all_to_all(pairs, TILE[:2], 0, 0, tiled=True).reshape(LANES, LANES)
 
 
 def exchanged(array):
@@ -443,28 +462,24 @@
     depth = lax.axis_index(DEPTH).astype(I32).reshape(1)
     params = jnp.concatenate([positions, log_scales, opacity_logits, colors], axis=0)
     few = ((TILES, SLAB), I32)
-    request, rank, owner = call(
+    request, rank, owner, wanted = call(
         request_kernel,
-        [(square, I32), few, few],
+        [(square, I32), few, few, few],
         [HBM, HBM],
-        [pltpu.VMEM(*few), pltpu.SemaphoreType.DMA((2,))],
+        [pltpu.SemaphoreType.DMA((2,))],
+        GRANT_ALL,
     )(owner, wanted)
-    asked = exchanged(request)
-    fixed, table = call(
-        fixed_kernel,
-        [((FIXED, LANES), F32), ((BLOCKS * 16, 3 * LANES), BF16)],
-        [SMEM] * 5 + [VMEM] * 2,
-    )(
-        tile_view,
-        tile_length,
-        cameras,
-        depth,
-        background,
-        target.transpose(1, 0, 2),
-        params,
+    asked = exchanged_in_plane(request)
+    theirs = lax.ppermute(params, (TILE[2], DEPTH[0]), [(0, 3), (3, 0), (1, 2), (2, 1)])
+    (fixed,) = call(fixed_kernel, [((FIXED, LANES), F32)], [SMEM] * 5 + [VMEM])(
+        tile_view, tile_length, cameras, depth, background, target.transpose(1, 0, 2)
     )
+    side = lax.axis_index(TILE[2]).astype(I32).reshape(1)
+    (table,) = call(
+        table_kernel, [((BLOCKS * 16, 6 * LANES), BF16)], [SMEM, VMEM, VMEM]
+    )(side, params, theirs)
     (reply,) = call(reply_kernel, [(square, F32)], [VMEM, VMEM], [asked_rows, held])(asked, table)
-    fetched = exchanged(reply)
+    fetched = exchanged_in_plane(reply)
     field = (TILES * SLAB, 8, LANES)
     tilted = (8 * PITCH, LANES)
     slab, alpha, weight, shade, entry = call(
@@ -483,7 +498,7 @@
     image, outgoing = call(
         backward_kernel,
         [((3, TILES, 1024), F32), (square, F32)],
-        [VMEM] * 8,
+        [VMEM] * 9,
         [
             pltpu.VMEM(tilted, F32),
             held,
@@ -491,14 +506,14 @@
             held,
             pltpu.VMEM((3 * TILES * 8, LANES), F32),
         ],
-    )(slabs, alpha, weight, shade, entry, owner, rank, fixed)
+    )(slabs, alpha, weight, shade, entry, owner, rank, wanted, fixed)
     incoming = exchanged(outgoing)
     (sums,) = call(
         collect_kernel,
         [((BLOCKS * PARAMS, LANES), F32)],
-        [VMEM, VMEM],
-        [asked_rows, held],
-    )(asked, incoming)
+        [VMEM],
+        [held],
+    )(incoming)
     sums = lax.all_gather(sums[None], DEPTH, axis=0, tiled=True)
     updated = call(adam_kernel, [(params.shape, F32)] * 3, [VMEM] * 4)(
         sums, params, first_moment, second_moment

time: 98.5 us -> 99.6 us (1.011)
  blocking collectives: 53.2 us -> 36.4 us
  starting transfers between devices: 20.6 us -> 30.5 us
  waiting for transfers between devices: 6.95 us -> 12.7 us
  Pallas kernels: 11 us -> 13.1 us
    all_to_all x2 -> x1, blocking collectives: 37.7 us -> 19.5 us  [exchanged(): lax.all_to_all(array.reshape(LANES, 1, LANES), (*TILE, DEPTH[0]), 0, 0, a...]
    all_to_all x1 -> x2, starting transfers between devices: 20.6 us -> 26.1 us  [exchanged_in_plane(): lax.all_to_all(pairs, TILE[:2], 0, 0, tiled=True).reshape(LANES, LANES)]
    ppermute x0 -> x1, starting transfers between devices: none -> 4.39 us  [body(): lax.ppermute(params, (TILE[2], DEPTH[0]), [(0, 3), (3, 0), (1, 2), (2, 1)])]
    all_to_all x1 -> x2, waiting for transfers between devices: 6.95 us -> 9.86 us  [exchanged_in_plane(): lax.all_to_all(pairs, TILE[:2], 0, 0, tiled=True).reshape(LANES, LANES)]
    ppermute x0 -> x1, waiting for transfers between devices: none -> 2.82 us  [body(): lax.ppermute(params, (TILE[2], DEPTH[0]), [(0, 3), (3, 0), (1, 2), (2, 1)])]
    all_gather x1, blocking collectives: 8.29 us -> 9.47 us  [body(): slabs = lax.all_gather(slab[None], DEPTH, axis=0, tiled=True)]
    pallas_call x1, Pallas kernels: 0.81 us -> 1.98 us  [body(): call(reply_kernel, [(square, F32)], [VMEM, VMEM], [asked_rows, held])]
    pallas_call x3 -> x4, Pallas kernels: 2.85 us -> 3.63 us  [the longest x1 2.1 us: body(): call(request_kernel, [(square, I32), few, few, few], [HBM, HBM], [pltpu.S...]
  transfers between devices with their start and end apart: 1 -> 3, of which waited for: 1 -> 3; matrix products, arithmetic and copies ran while one was open for 1% -> 1% of each run, Pallas kernels for 1% -> 1%
where the time goes in v3:
time: 99.6 us; the launch traced here: 99 us
  blocking collectives  36.4 us (37%)
  starting transfers between devices  30.5 us (31%)
  Pallas kernels  13.1 us (13%)
  waiting for transfers between devices  12.7 us (13%)
  local copies, waits for them, and re-layouts  4.82 us (5%)
    all_to_all x2, starting transfers between devices, exchanged_in_plane(): lax.all_to_all(pairs, TILE[:2], 0, 0, tiled=True).reshape(LANES, LANES)  26.1 us
    all_to_all x1, blocking collectives, exchanged(): lax.all_to_all(array.reshape(LANES, 1, LANES), (*TILE, DEPTH[0]), 0, 0, a...  19.5 us
    all_to_all x2, waiting for transfers between devices, exchanged_in_plane(): lax.all_to_all(pairs, TILE[:2], 0, 0, tiled=True).reshape(LANES, LANES)  9.86 us
    all_gather x1, blocking collectives, body(): slabs = lax.all_gather(slab[None], DEPTH, axis=0, tiled=True)  9.47 us
    all_gather x1, blocking collectives, body(): sums = lax.all_gather(sums[None], DEPTH, axis=0, tiled=True)  7.39 us
    unnamed x20, local copies, waits for them, and re-layouts  4.82 us
    ppermute x1, starting transfers between devices, body(): lax.ppermute(params, (TILE[2], DEPTH[0]), [(0, 3), (3, 0), (1, 2), (2, 1)])  4.39 us
    pallas_call x1, Pallas kernels, body(): call(backward_kernel, [((3, TILES, 1024), F32), (square, F32)], [VMEM] *...  3.6 us
  transfers between devices with their start and end apart: 3, of which 3 were waited for; matrix products, arithmetic and copies ran while one was open for 1% of the time, Pallas kernels for 1%

profile of v3, /device:TPU:1, one launch (start us, length us, event | category | flops | bytes accessed | tf_op | source)
XLA Modules:
  0.0 99.0 jit_solution(16030236034958754549)
XLA Ops:
  0.6 2.1 %shard_map.156 = (s32[128,128]{1,0:T(8,128)}, s32[4,128]{1,0:T(4,128)}, s32[4,128]{1,0:T(4,128)}, s32[4,128]{1,0:T(4,128)}) custom-call(s32[4,128]{1,0:T(4,128)} %bitcast.24, s32[4,128]{1,0:T(4,128)} %bitcast.25), custom_call_target="tpu_custom_call" | custom-call | tf_op jit(solution)/shard_map/pallas_call | solution.py:465
  2.7 0.0 copy-start.6
  2.8 17.1 %all-to-all-start = ((s32[64,2,128]{2,1,0:T(2,128)}), s32[64,2,128]{2,1,0:T(2,128)S(1)}, u32[]{:S(2)}, u32[]{:S(2)}) async-start(s32[64,2,128]{2,1,0:T(2,128)} %bitcast.23), calls=%async_computation | async-start | bytes 131072 | tf_op jit(solution)/shard_map/all_to_all | solution.py:424
  19.9 0.9 pad_maximum_fusion.mine_ref.params_ref
  20.8 4.4 %collective-permute-start = (f32[10,2048]{1,0:T(8,128)S(1)}, f32[10,2048]{1,0:T(8,128)S(1)}, u32[]{:S(2)}, u32[]{:S(2)}) collective-permute-start(f32[10,2048]{1,0:T(8,128)S(1)} %pad_maximum_fusion.mine_ref.params_ref), channel_id=1, source_target_pairs={{0,6},{6,0},{2,4},{4,2},{1,7},{7,1},{3,5},{5,3},{8,14},{14,8},{10,... | collective-permute-start | bytes 245768 | tf_op jit(solution)/shard_map/ppermute | solution.py:473
  25.2 2.8 %collective-permute-done.theirs_ref = f32[10,2048]{1,0:T(8,128)S(1)} collective-permute-done((f32[10,2048]{1,0:T(8,128)S(1)}, f32[10,2048]{1,0:T(8,128)S(1)}, u32[]{:S(2)}, u32[]{:S(2)}) %collective-permute-start) | collective-permute-done | bytes 81952 | tf_op jit(solution)/shard_map/ppermute | solution.py:473
  28.0 0.1 shard_map.157.table_ref
  28.1 2.9 %all-to-all-done = s32[64,2,128]{2,1,0:T(2,128)S(1)} async-done(((s32[64,2,128]{2,1,0:T(2,128)}), s32[64,2,128]{2,1,0:T(2,128)S(1)}, u32[]{:S(2)}, u32[]{:S(2)}) %all-to-all-start) | async-done | bytes 65568 | tf_op jit(solution)/shard_map/all_to_all | solution.py:424
  31.0 2.0 %shard_map.158 = f32[128,128]{1,0:T(8,128)} custom-call(s32[128,128]{1,0:T(8,128)S(1)} %bitcast.20, bf16[256,768]{1,0:T(8,128)(2,1)S(1)} %shard_map.157.table_ref), custom_call_target="tpu_custom_call" | custom-call | tf_op jit(solution)/shard_map/pallas_call | solution.py:481
  33.0 8.9 %all-to-all-start.1 = ((f32[64,2,128]{2,1,0:T(2,128)}), f32[64,2,128]{2,1,0:T(2,128)S(1)}, u32[]{:S(2)}, u32[]{:S(2)}) async-start(f32[64,2,128]{2,1,0:T(2,128)} %bitcast.5), calls=%async_computation.1 | async-start | bytes 131072 | tf_op jit(solution)/shard_map/all_to_all | solution.py:424
  41.9 0.0 copy-start.2
  41.9 0.8 copy-done.2
  42.7 0.0 copy-start.5
  42.7 0.7 copy-done.5
  43.4 0.0 copy-start.7
  43.4 0.7 copy-done.7
  44.1 0.0 copy-start.8
  44.1 0.7 copy-done.8
  44.7 0.0 copy-start.9
  44.7 0.7 copy-done.9
  45.4 0.6 shard_map.159.fixed_ref
  46.0 7.0 %all-to-all-done.1 = f32[64,2,128]{2,1,0:T(2,128)S(1)} async-done(((f32[64,2,128]{2,1,0:T(2,128)}), f32[64,2,128]{2,1,0:T(2,128)S(1)}, u32[]{:S(2)}, u32[]{:S(2)}) %all-to-all-start.1) | async-done | bytes 65568 | tf_op jit(solution)/shard_map/all_to_all | solution.py:424
  53.0 0.0 copy-start.3
  53.0 0.7 copy-done.3
  53.7 0.0 copy-start.4
  53.7 0.7 copy-done.4
  54.3 3.0 %shard_map.160 = (f32[128,128]{1,0:T(8,128)S(1)}, f32[512,8,128]{2,1,0:T(8,128)S(1)}, f32[4104,128]{1,0:T(8,128)S(1)}, f32[3,512,128]{2,1,0:T(8,128)S(1)}, f32[64,128]{1,0:T(8,128)S(1)}) custom-call(f32[128,128]{1,0:T(8,128)S(1)} %bitcast.18, s32[4,128]{1,0:T(4,128)S(1)} %copy-done.4, s32[4,128]{1,0:T(4,128)S(1)} %copy-done.3, ...), custom_call_target="tpu_custom_call" | custom-call | tf_op jit(solution)/shard_map/pallas_call | solution.py:485
  57.4 9.5 %all-gather = f32[512,128]{1,0:T(8,128)S(1)} all-gather(f32[128,128]{1,0:T(8,128)S(1)} %get-tuple-element.21), channel_id=2, replica_groups=mesh['tile_z'=8,'tile_y'=8,'tile_x'=2,'depth_x'=2,'depth_core'=2] {'dept..., dimensions={0}, use_global_device_ids=true | all-gather | bytes 327680 | tf_op jit(solution)/shard_map/all_gather | solution.py:497
  66.9 0.0 copy-done.6
  66.9 0.0 copy-start
  66.9 0.0 copy-start.1
  66.9 3.6 %shard_map.161 = (f32[3,4,1024]{2,1,0:T(4,128)}, f32[128,128]{1,0:T(8,128)S(1)}) custom-call(f32[4,128,128]{2,1,0:T(8,128)S(1)} %bitcast.17, f32[512,8,128]{2,1,0:T(8,128)S(1)} %get-tuple-element.22.alpha_ref, f32[4104,128]{1,0:T(8,128)S(1)} %get-tuple-element.23.weight_ref, f32[3,512,128]{2,1,0:T(8,128)S(1)} %get-tuple-element.24.shade_ref, ...), custom_call_target="tpu_custom_call" | custom-call | tf_op jit(solution)/shard_map/pallas_call | solution.py:498
  70.5 19.5 %all_to_all.15 = f32[128,1,128]{2,1,0:T(1,128)S(1)} all-to-all(f32[128,1,128]{2,1,0:T(1,128)S(1)} %bitcast.21), channel_id=1, replica_groups={{0,6,8,14,16,22,24,30,32,38,40,46,48,54,56,62,64,70,72,78,80,86,88,94,9..., dimensions={0} | all-to-all | bytes 131072 | tf_op jit(solution)/shard_map/all_to_all | solution.py:431
  90.0 0.8 shard_map.162
  90.8 7.4 %all-gather.1 = f32[640,128]{1,0:T(8,128)S(1)} all-gather(f32[160,128]{1,0:T(8,128)S(1)} %shard_map.162), channel_id=3, replica_groups=mesh['tile_z'=8,'tile_y'=8,'tile_x'=2,'depth_x'=2,'depth_core'=2] {'dept..., dimensions={0}, use_global_device_ids=true | all-gather | bytes 409600 | tf_op jit(solution)/shard_map/all_gather | solution.py:517
  98.2 0.0 copy-done
  98.2 0.0 copy-done.1
  98.2 0.8 shard_map.163
Async XLA Ops:
  2.7 64.1 %copy-start.6 = (s32[4,128]{1,0:T(4,128)S(1)}, s32[4,128]{1,0:T(4,128)}, u32[]{:S(2)}) copy-start(s32[4,128]{1,0:T(4,128)} %get-tuple-element.26.row_ref) | copy-start | bytes 6148
  2.8 28.2 %all-to-all-start = ((s32[64,2,128]{2,1,0:T(2,128)}), s32[64,2,128]{2,1,0:T(2,128)S(1)}, u32[]{:S(2)}, u32[]{:S(2)}) async-start(s32[64,2,128]{2,1,0:T(2,128)} %bitcast.23), calls=%async_computation | async-start | bytes 131072 | tf_op jit(solution)/shard_map/all_to_all | solution.py:424
  20.8 7.2 %collective-permute-start = (f32[10,2048]{1,0:T(8,128)S(1)}, f32[10,2048]{1,0:T(8,128)S(1)}, u32[]{:S(2)}, u32[]{:S(2)}) collective-permute-start(f32[10,2048]{1,0:T(8,128)S(1)} %pad_maximum_fusion.mine_ref.params_ref), channel_id=1, source_target_pairs={{0,6},{6,0},{2,4},{4,2},{1,7},{7,1},{3,5},{5,3},{8,14},{14,8},{10,... | collective-permute-start | bytes 245768 | tf_op jit(solution)/shard_map/ppermute | solution.py:473
  33.0 20.0 %all-to-all-start.1 = ((f32[64,2,128]{2,1,0:T(2,128)}), f32[64,2,128]{2,1,0:T(2,128)S(1)}, u32[]{:S(2)}, u32[]{:S(2)}) async-start(f32[64,2,128]{2,1,0:T(2,128)} %bitcast.5), calls=%async_computation.1 | async-start | bytes 131072 | tf_op jit(solution)/shard_map/all_to_all | solution.py:424
  41.9 0.8 copy-start.2
  42.7 0.7 copy-start.5
  43.4 0.7 copy-start.7
  44.1 0.7 copy-start.8
  44.7 0.7 copy-start.9
  53.0 0.7 copy-start.3
  53.7 0.7 copy-start.4
  66.9 31.3 %copy-start = (f32[10,2048]{1,0:T(8,128)S(1)}, f32[10,2048]{1,0:T(8,128)}, u32[]{:S(2)}) copy-start(f32[10,2048]{1,0:T(8,128)} %first_ref.1) | copy-start | bytes 245764
  66.9 31.3 %copy-start.1 = (f32[10,2048]{1,0:T(8,128)S(1)}, f32[10,2048]{1,0:T(8,128)}, u32[]{:S(2)}) copy-start(f32[10,2048]{1,0:T(8,128)} %second_ref.1) | copy-start | bytes 245764

commit v4 on v3

--- a/solution.py
+++ b/solution.py
@@ -16,7 +16,8 @@
 PARAMS = 10
 BLOCKS = 16
 GRANT_ALL = 60
-LIVE, BACK, HERE, GOAL, FIXED = 32, 40, 64, 72, 168
+LIVE, BACK, HERE, GOAL, OWNER, FIXED = 32, 40, 64, 72, 168, 184
+RANK, ROW = OWNER + TILES, OWNER + 2 * TILES
 PITCH = TILES * SLAB + 1
 TILE = ("tile_z", "tile_y", "tile_x")
 DEPTH = ("depth_x", "depth_core")
@@ -55,82 +56,117 @@
     return jnp.where(iota((rows, LANES), 0) == index, 1.0, 0.0)
 
 
-def request_kernel(owner_hbm, row_hbm, request_ref, rank_ref, owner_ref, row_ref, sems):
+def request_kernel(
+    owner_hbm,
+    row_hbm,
+    position_hbm,
+    scale_hbm,
+    opacity_hbm,
+    color_hbm,
+    request_ref,
+    list_ref,
+    params_ref,
+    owner_ref,
+    row_ref,
+    position,
+    scale,
+    opacity,
+    color,
+    sems,
+):
+    sources = (owner_hbm, row_hbm, position_hbm, scale_hbm, opacity_hbm, color_hbm)
+    held = (owner_ref, row_ref, position, scale, opacity, color)
     copies = [
-        pltpu.make_async_copy(owner_hbm, owner_ref, sems.at[0]),
-        pltpu.make_async_copy(row_hbm, row_ref, sems.at[1]),
+        pltpu.make_async_copy(source, there, sems.at[n])
+        for n, (source, there) in enumerate(zip(sources, held))
     ]
     for copy in copies:
         copy.start()
-    for copy in copies:
+    for copy in copies[:2]:
         copy.wait()
     earlier = jnp.where(iota((SLAB, SLAB), 0) < iota((SLAB, SLAB), 1), 1.0, 0.0).astype(BF16)
     before = jnp.zeros((LANES, 1), F32)
-    total = jnp.zeros((LANES, LANES), F32)
+    total = jnp.zeros((LANES // 2, LANES), F32)
     for b in range(TILES):
-        named = onehot(owner_ref[b : b + 1, :], LANES)
-        named_16 = named.astype(BF16)
-        count = dot(named_16, earlier, NN) + before
+        owner = owner_ref[b : b + 1, :]
+        row = row_ref[b : b + 1, :]
+        named = onehot(owner, LANES)
+        count = dot(named.astype(BF16), earlier, NN) + before
         before = before + jnp.sum(named, axis=1, keepdims=True)
         rank = jnp.sum(named * count, axis=0, keepdims=True).astype(I32)
-        rank_ref[b : b + 1, :] = rank
-        row = row_ref[b : b + 1, :]
-        here = iota((LANES, SLAB), 0) == rank
+        here = iota((LANES, SLAB), 0) == (owner & 1) * 16 + rank
         high = jnp.where(here, row >> 4, 0).astype(F32).astype(BF16)
         low = jnp.where(here, row & 15, 0).astype(F32).astype(BF16)
-        total = total + 16.0 * dot(named_16, high, NT) + dot(named_16, low, NT)
+        place = onehot(owner >> 1, LANES // 2).astype(BF16)
+        total = total + 16.0 * dot(place, high, NT) + dot(place, low, NT)
+        list_ref[b : b + 1, :] = owner
+        list_ref[TILES + b : TILES + b + 1, :] = rank
+        list_ref[2 * TILES + b : 2 * TILES + b + 1, :] = row
+    list_ref[3 * TILES :, :] = jnp.zeros((TILES, LANES), I32)
     request_ref[...] = total.astype(I32)
-
-
-def fixed_kernel(
-    view_ref, length_ref, cams_ref, depth_ref, back_ref, target_ref, fixed_ref
-):
+    for copy in copies[2:]:
+        copy.wait()
+    for a in range(BLOCKS):
+        at = slice(a * LANES, (a + 1) * LANES)
+        params_ref[a * PARAMS : a * PARAMS + 3, :] = position[:, at]
+        params_ref[a * PARAMS + 3 : a * PARAMS + 6, :] = scale[:, at]
+        params_ref[a * PARAMS + 6 : a * PARAMS + 7, :] = opacity[:, at]
+        params_ref[a * PARAMS + 7 : a * PARAMS + 10, :] = color[:, at]
+
+
+def fixed_kernel(scalar_ref, target_ref, list_ref, fixed_ref):
     for i in range(2):
         for j in range(4):
             at = (i * 4 + j) * TILES
-            fixed_ref[at : at + TILES, :] = per_tile([cams_ref[view_ref[b], i, j] for b in range(TILES)])
-    place = depth_ref[0] * SLAB + iota((TILES, LANES), 1)
-    length = per_tile([length_ref[b].astype(F32) for b in range(TILES)])
-    fixed_ref[LIVE : LIVE + TILES, :] = jnp.where(place.astype(F32) < length, 1.0, 0.0)
+            fixed_ref[at : at + TILES, :] = per_tile(
+                [scalar_ref[scalar_ref[b].astype(I32) * 8 + i * 4 + j + 12] for b in range(TILES)]
+            )
+    depth = scalar_ref[11]
+    place = depth * SLAB + iota((TILES, LANES), 1).astype(F32)
+    length = per_tile([scalar_ref[4 + b] for b in range(TILES)])
+    fixed_ref[LIVE : LIVE + TILES, :] = jnp.where(place < length, 1.0, 0.0)
     for c in range(3):
-        fixed_ref[BACK + c * 8 : BACK + c * 8 + 8, :] = jnp.full((8, LANES), back_ref[c], F32)
-    fixed_ref[HERE : HERE + 8, :] = jnp.full((8, LANES), depth_ref[0].astype(F32), F32)
+        fixed_ref[BACK + c * 8 : BACK + c * 8 + 8, :] = jnp.full((8, LANES), scalar_ref[8 + c], F32)
+    fixed_ref[HERE : HERE + 8, :] = jnp.full((8, LANES), depth, F32)
     for c in range(3):
         for s in range(8):
             fixed_ref[pl.ds(GOAL + c * TILES * 8 + s, TILES, stride=8), :] = target_ref[
                 c, :, s * LANES : (s + 1) * LANES
             ]
+    fixed_ref[OWNER : OWNER + 16, :] = list_ref[...].astype(F32)
+
 
 def table_kernel(side_ref, mine_ref, theirs_ref, table_ref):
     first = side_ref[0] == 0
     blank = jnp.zeros((16 - PARAMS, LANES), F32)
     for a in range(BLOCKS):
-        mine = mine_ref[:, a * LANES : (a + 1) * LANES]
-        theirs = theirs_ref[:, a * LANES : (a + 1) * LANES]
+        mine = mine_ref[a * PARAMS : (a + 1) * PARAMS, :]
+        theirs = theirs_ref[a * PARAMS : (a + 1) * PARAMS, :]
         for h in range(2):
             block = jnp.where(first, mine, theirs) if h == 0 else jnp.where(first, theirs, mine)
-            table_ref[a * 16 : (a + 1) * 16, h * 384 : (h + 1) * 384] = side_by_side(
-                jnp.concatenate([block, blank], axis=0)
-            )
+            at = h * BLOCKS * 16 + a * 16
+            table_ref[at : at + 16, :] = side_by_side(jnp.concatenate([block, blank], axis=0))
 
 
 def reply_kernel(asked_ref, table_ref, reply_ref, columns, held):
+    half = LANES // 2
     columns[...] = asked_ref[...].T
-    table = table_ref[...]
-    second = (iota((LANES, LANES), 1) & 1) == 1
-    for r in range(SLOTS):
-        row = columns[r : r + 1, :]
-        pick = onehot(row & (LANES - 1), LANES)
-        picks = [jnp.where(second, 0.0, pick).astype(BF16)] * 3
-        picks += [jnp.where(second, pick, 0.0).astype(BF16)] * 3
-        found = dot(table, jnp.concatenate(picks, axis=0), NN)
-        block = row >> 7
-        value = jnp.zeros((16, LANES), F32)
-        for a in range(BLOCKS):
-            value = value + jnp.where(block == a, found[a * 16 : (a + 1) * 16], 0.0)
-        held[r * PARAMS : r * PARAMS + 16, :] = value
-    held[SLOTS * PARAMS :, :] = jnp.zeros((LANES - SLOTS * PARAMS, LANES), F32)
-    reply_ref[...] = held[...].T
+    for h in range(2):
+        slots = columns[h * 16 : h * 16 + 16, :]
+        rows = jnp.concatenate([slots[:5], slots[5:10]], axis=1)
+        table = table_ref[h * BLOCKS * 16 : (h + 1) * BLOCKS * 16, :]
+        for q in range(5):
+            row = rows[q : q + 1, :]
+            pick = onehot(row & (LANES - 1), LANES).astype(BF16)
+            found = dot(table, jnp.concatenate([pick, pick, pick], axis=0), NN)
+            block = row >> 7
+            value = jnp.zeros((16, LANES), F32)
+            for a in range(BLOCKS):
+                value = value + jnp.where(block == a, found[a * 16 : (a + 1) * 16], 0.0)
+            held[q * PARAMS : q * PARAMS + 16, :] = value
+        held[5 * PARAMS :, :] = jnp.zeros((LANES - 5 * PARAMS, LANES), F32)
+        turned = held[...].T
+        reply_ref[:, h, :] = turned[:half] + pltpu.roll(turned[half:], 5 * PARAMS, 1)
 
 
 def per_tile(values):
@@ -146,6 +182,10 @@
     return rows[:4], rows[4:]
 
 
+def listed(fixed_ref, at, b):
+    return fixed_ref[at + b : at + b + 1, :].astype(I32)
+
+
 def covariance(scales, jac):
     variance = [jnp.exp(2.0 * s) for s in scales]
     xx = sum(jac[0][j] * jac[0][j] * variance[j] for j in range(3)) + 0.3
@@ -156,8 +196,6 @@
 
 def forward_kernel(
     fetched_ref,
-    owner_ref,
-    rank_ref,
     fixed_ref,
     slab_ref,
     alpha_ref,
@@ -170,9 +208,9 @@
 ):
     fetched = side_by_side(fetched_ref[...].T)
     for b in range(TILES):
-        named = onehot(owner_ref[b : b + 1, :], LANES).astype(BF16)
+        named = onehot(listed(fixed_ref, OWNER, b), LANES).astype(BF16)
         found[...] = dot(fetched, jnp.concatenate([named, named, named], axis=0), NN)
-        rank = rank_ref[b : b + 1, :]
+        rank = listed(fixed_ref, RANK, b)
         value = jnp.zeros((16, LANES), F32)
         for r in range(SLOTS):
             value = value + jnp.where(rank == r, found[r * PARAMS : r * PARAMS + 16, :], 0.0)
@@ -241,9 +279,6 @@
     weight_ref,
     shade_ref,
     entry_ref,
-    owner_ref,
-    rank_ref,
-    row_ref,
     fixed_ref,
     image_ref,
     outgoing_ref,
@@ -366,13 +401,13 @@
     outgoing = jnp.zeros((LANES, LANES), F32)
     for b in range(TILES):
         mine = grads[pl.ds(b, PARAMS, stride=TILES), :]
-        rank = rank_ref[b : b + 1, :]
+        rank = listed(fixed_ref, RANK, b)
         for r in range(SLOTS):
             placed[r * PARAMS : (r + 1) * PARAMS, :] = jnp.where(rank == r, mine, 0.0)
         here = iota((16, LANES), 0) == rank
-        row = jnp.where(here, row_ref[b : b + 1, :].astype(F32), 0.0)
+        row = jnp.where(here, fixed_ref[ROW + b : ROW + b + 1, :], 0.0)
         placed[SLOTS * PARAMS : SLOTS * PARAMS + 16, :] = row
-        named = onehot(owner_ref[b : b + 1, :], LANES).astype(BF16)
+        named = onehot(listed(fixed_ref, OWNER, b), LANES).astype(BF16)
         named = jnp.concatenate([named, named, named], axis=1)
         outgoing = outgoing + dot(named, side_by_side(placed[...]), NT)
     outgoing_ref[...] = outgoing
@@ -403,7 +438,7 @@
         first = 0.9 * first_ref[:, at] + 0.1 * gradient
         second = 0.999 * second_ref[:, at] + 0.001 * gradient * gradient
         step = first / (1.0 - 0.9**10) / (jnp.sqrt(second / (1.0 - 0.999**10)) + 1e-08)
-        new_ref[:, at] = params_ref[:, at] - 0.05 * step
+        new_ref[:, at] = params_ref[a * PARAMS : (a + 1) * PARAMS, :] - 0.05 * step
         new_first_ref[:, at] = first
         new_second_ref[:, at] = second
 
@@ -420,8 +455,7 @@
 
 
 def exchanged_in_plane(array):
-    pairs = array.reshape(LANES // 2, 2, LANES)
-    return lax.all_to_all(pairs, TILE[:2], 0, 0, tiled=True).reshape(LANES, LANES)
+    return lax.all_to_all(array, TILE[:2], 0, 0, tiled=True)
 
 
 def exchanged(array):
@@ -456,30 +490,44 @@
 ):
     square = (LANES, LANES)
     held = pltpu.VMEM(square, F32)
-    asked_rows = pltpu.VMEM(square, I32)
-    owner = list_owner.reshape(TILES, SLAB)
-    wanted = list_row.reshape(TILES, SLAB)
-    depth = lax.axis_index(DEPTH).astype(I32).reshape(1)
-    params = jnp.concatenate([positions, log_scales, opacity_logits, colors], axis=0)
-    few = ((TILES, SLAB), I32)
-    request, rank, owner, wanted = call(
+    plane = LANES // 2
+    flat = (BLOCKS * PARAMS, LANES)
+    lists = (TILES, SLAB)
+    sources = (
+        list_owner.reshape(lists),
+        list_row.reshape(lists),
+        positions,
+        log_scales,
+        opacity_logits,
+        colors,
+    )
+    request, listing, params = call(
         request_kernel,
-        [(square, I32), few, few, few],
-        [HBM, HBM],
-        [pltpu.SemaphoreType.DMA((2,))],
+        [((plane, LANES), I32), ((16, LANES), I32), (flat, F32)],
+        [HBM] * 6,
+        [pltpu.VMEM(a.shape, a.dtype) for a in sources] + [pltpu.SemaphoreType.DMA((6,))],
         GRANT_ALL,
-    )(owner, wanted)
-    asked = exchanged_in_plane(request)
+    )(*sources)
+    asked = exchanged_in_plane(request.reshape(plane, 1, LANES)).reshape(plane, LANES)
     theirs = lax.ppermute(params, (TILE[2], DEPTH[0]), [(0, 3), (3, 0), (1, 2), (2, 1)])
-    (fixed,) = call(fixed_kernel, [((FIXED, LANES), F32)], [SMEM] * 5 + [VMEM])(
-        tile_view, tile_length, cameras, depth, background, target.transpose(1, 0, 2)
-    )
     side = lax.axis_index(TILE[2]).astype(I32).reshape(1)
     (table,) = call(
-        table_kernel, [((BLOCKS * 16, 6 * LANES), BF16)], [SMEM, VMEM, VMEM]
+        table_kernel, [((2 * BLOCKS * 16, 3 * LANES), BF16)], [SMEM, VMEM, VMEM]
     )(side, params, theirs)
-    (reply,) = call(reply_kernel, [(square, F32)], [VMEM, VMEM], [asked_rows, held])(asked, table)
-    fetched = exchanged_in_plane(reply)
+    (reply,) = call(
+        reply_kernel,
+        [((plane, 2, LANES), F32)],
+        [VMEM, VMEM],
+        [pltpu.VMEM((LANES, plane), I32), held],
+    )(asked, table)
+    fetched = exchanged_in_plane(reply).reshape(square)
+    depth = lax.axis_index(DEPTH).astype(F32).reshape(1)
+    scalars = jnp.concatenate(
+        [tile_view.astype(F32), tile_length.astype(F32), background, depth, cameras.reshape(-1)]
+    )
+    (fixed,) = call(fixed_kernel, [((FIXED, LANES), F32)], [SMEM, VMEM, VMEM])(
+        scalars, target.transpose(1, 0, 2), listing
+    )
     field = (TILES * SLAB, 8, LANES)
     tilted = (8 * PITCH, LANES)
     slab, alpha, weight, shade, entry = call(
@@ -491,14 +539,14 @@
             ((3, TILES * SLAB, LANES), F32),
             ((TILES * 16, LANES), F32),
         ],
-        [VMEM] * 4,
+        [VMEM] * 2,
         [held, held, pltpu.VMEM((6, TILES * SLAB, LANES), F32)],
-    )(fetched, owner, rank, fixed)
+    )(fetched, fixed)
     slabs = lax.all_gather(slab[None], DEPTH, axis=0, tiled=True)
     image, outgoing = call(
         backward_kernel,
         [((3, TILES, 1024), F32), (square, F32)],
-        [VMEM] * 9,
+        [VMEM] * 6,
         [
             pltpu.VMEM(tilted, F32),
             held,
@@ -506,7 +554,7 @@
             held,
             pltpu.VMEM((3 * TILES * 8, LANES), F32),
         ],
-    )(slabs, alpha, weight, shade, entry, owner, rank, wanted, fixed)
+    )(slabs, alpha, weight, shade, entry, fixed)
     incoming = exchanged(outgoing)
     (sums,) = call(
         collect_kernel,
@@ -515,7 +563,7 @@
         [held],
     )(incoming)
     sums = lax.all_gather(sums[None], DEPTH, axis=0, tiled=True)
-    updated = call(adam_kernel, [(params.shape, F32)] * 3, [VMEM] * 4)(
+    updated = call(adam_kernel, [(first_moment.shape, F32)] * 3, [VMEM] * 4)(
         sums, params, first_moment, second_moment
     )
     return (image.transpose(1, 0, 2), *updated)

time: 99.6 us -> 96.3 us (0.967)
  starting transfers between devices: 30.5 us -> 26.2 us
  waiting for transfers between devices: 12.7 us -> 15.9 us
  blocking collectives: 36.4 us -> 34.7 us
    all_to_all x2, waiting for transfers between devices: 9.86 us -> 15.9 us  [exchanged_in_plane(): return lax.all_to_all(array, TILE[:2], 0, 0, tiled=True)]
    all_to_all x2, starting transfers between devices: 26.1 us -> 20.9 us  [exchanged_in_plane(): return lax.all_to_all(array, TILE[:2], 0, 0, tiled=True)]
    ppermute x1, waiting for transfers between devices: 2.82 us -> 0.01 us  [body(): lax.ppermute(params, (TILE[2], DEPTH[0]), [(0, 3), (3, 0), (1, 2), (2, 1)])]
    unnamed x20 -> x12, local copies, waits for them, and re-layouts: 4.82 us -> 2.39 us
    all_to_all x1, blocking collectives: 19.5 us -> 18.2 us  [exchanged(): lax.all_to_all(array.reshape(LANES, 1, LANES), (*TILE, DEPTH[0]), 0, 0, a...]
    convert_element_type x0 -> x2, other arithmetic: none -> 1.32 us  [the longest x1 0.66 us: body(): tile_view.astype(F32)]
  transfers between devices with their start and end apart: 3 -> 3, of which waited for: 3 -> 2; matrix products, arithmetic and copies ran while one was open for 1% -> 3% of each run, Pallas kernels for 1% -> 1%
where the time goes in v4:
time: 96.3 us; the launch traced here: 95.7 us
  blocking collectives  34.7 us (36%)
  starting transfers between devices  26.2 us (27%)
  waiting for transfers between devices  15.9 us (17%)
  Pallas kernels  13 us (13%)
  local copies, waits for them, and re-layouts  3.89 us (4%)
  other arithmetic  1.32 us (1%)
    all_to_all x2, starting transfers between devices, exchanged_in_plane(): return lax.all_to_all(array, TILE[:2], 0, 0, tiled=True)  20.9 us
    all_to_all x1, blocking collectives, exchanged(): lax.all_to_all(array.reshape(LANES, 1, LANES), (*TILE, DEPTH[0]), 0, 0, a...  18.2 us
    all_to_all x2, waiting for transfers between devices, exchanged_in_plane(): return lax.all_to_all(array, TILE[:2], 0, 0, tiled=True)  15.9 us
    all_gather x1, blocking collectives, body(): slabs = lax.all_gather(slab[None], DEPTH, axis=0, tiled=True)  9.18 us
    all_gather x1, blocking collectives, body(): sums = lax.all_gather(sums[None], DEPTH, axis=0, tiled=True)  7.4 us
    ppermute x1, starting transfers between devices, body(): lax.ppermute(params, (TILE[2], DEPTH[0]), [(0, 3), (3, 0), (1, 2), (2, 1)])  5.22 us
    pallas_call x1, Pallas kernels, body(): call(backward_kernel, [((3, TILES, 1024), F32), (square, F32)], [VMEM] *...  3.87 us
    pallas_call x1, Pallas kernels, body(): call(forward_kernel, [(square, F32), (field, F32), (tilted, F32), ((3, TI...  3.02 us
  transfers between devices with their start and end apart: 3, of which 2 were waited for; matrix products, arithmetic and copies ran while one was open for 3% of the time, Pallas kernels for 1%

profile of v4, /device:TPU:1, one launch (start us, length us, event | category | flops | bytes accessed | tf_op | source)
XLA Modules:
  0.0 95.7 jit_solution(17520436460991299161)
XLA Ops:
  0.6 2.2 %shard_map.156 = (s32[64,128]{1,0:T(8,128)}, s32[16,128]{1,0:T(8,128)}, f32[160,128]{1,0:T(8,128)}) custom-call(s32[4,128]{1,0:T(4,128)} %bitcast.25, s32[4,128]{1,0:T(4,128)} %bitcast.26, f32[3,2048]{1,0:T(4,128)} %position_hbm.1, f32[3,2048]{1,0:T(4,128)} %scale_hbm.1, f32[1,2048]{1,0:T(1,128)} %opacity_hbm.1, f32[3,2048]{1,0:T(4,128)} %color_hbm.1), custom_call_target="tpu_custom_call" | custom-call | tf_op jit(solution)/shard_map/pallas_call | solution.py:504
  2.8 5.2 %collective-permute-start = (f32[160,128]{1,0:T(8,128)}, f32[160,128]{1,0:T(8,128)S(1)}, u32[]{:S(2)}, u32[]{:S(2)}) collective-permute-start(f32[160,128]{1,0:T(8,128)} %get-tuple-element.18.mine_ref.params_ref), channel_id=1, source_target_pairs={{0,6},{6,0},{2,4},{4,2},{1,7},{7,1},{3,5},{5,3},{8,14},{14,8},{10,... | collective-permute-start | bytes 245768 | tf_op jit(solution)/shard_map/ppermute | solution.py:512
  8.0 16.3 %all-to-all-start = ((s32[64,1,128]{2,1,0:T(1,128)}), s32[64,1,128]{2,1,0:T(1,128)S(1)}, u32[]{:S(2)}, u32[]{:S(2)}) async-start(s32[64,1,128]{2,1,0:T(1,128)} %bitcast.24), calls=%async_computation | async-start | bytes 65536 | tf_op jit(solution)/shard_map/all_to_all | solution.py:458
  24.4 0.0 collective-permute-done.theirs_ref
  24.4 0.0 copy-start
  24.4 0.9 copy-done
  25.3 0.1 shard_map.157.table_ref
  25.3 9.8 %all-to-all-done = s32[64,1,128]{2,1,0:T(1,128)S(1)} async-done(((s32[64,1,128]{2,1,0:T(1,128)}), s32[64,1,128]{2,1,0:T(1,128)S(1)}, u32[]{:S(2)}, u32[]{:S(2)}) %all-to-all-start) | async-done | bytes 32800 | tf_op jit(solution)/shard_map/all_to_all | solution.py:458
  35.1 1.6 %shard_map.158 = f32[64,2,128]{2,1,0:T(2,128)} custom-call(s32[64,128]{1,0:T(8,128)S(1)} %bitcast.21, bf16[512,384]{1,0:T(8,128)(2,1)S(1)} %shard_map.157.table_ref), custom_call_target="tpu_custom_call" | custom-call | tf_op jit(solution)/shard_map/pallas_call | solution.py:517
  36.7 4.6 %all-to-all-start.1 = ((f32[64,2,128]{2,1,0:T(2,128)}), f32[64,2,128]{2,1,0:T(2,128)S(1)}, u32[]{:S(2)}, u32[]{:S(2)}) async-start(f32[64,2,128]{2,1,0:T(2,128)} %shard_map.158), calls=%async_computation.1 | async-start | bytes 131072 | tf_op jit(solution)/shard_map/all_to_all | solution.py:458
  41.4 0.8 reshape.45
  42.1 0.7 convert_element_type.9
  42.8 0.7 convert_element_type.10
  43.5 0.7 concatenate.3.scalar_ref
  44.2 0.0 copy-start.4
  44.2 0.8 copy-done.4
  45.0 0.0 copy-start.5
  45.0 0.7 copy-done.5
  45.7 0.6 shard_map.159.fixed_ref
  46.3 6.2 %all-to-all-done.1 = f32[64,2,128]{2,1,0:T(2,128)S(1)} async-done(((f32[64,2,128]{2,1,0:T(2,128)}), f32[64,2,128]{2,1,0:T(2,128)S(1)}, u32[]{:S(2)}, u32[]{:S(2)}) %all-to-all-start.1) | async-done | bytes 65568 | tf_op jit(solution)/shard_map/all_to_all | solution.py:458
  52.4 3.0 %shard_map.160 = (f32[128,128]{1,0:T(8,128)S(1)}, f32[512,8,128]{2,1,0:T(8,128)S(1)}, f32[4104,128]{1,0:T(8,128)S(1)}, f32[3,512,128]{2,1,0:T(8,128)S(1)}, f32[64,128]{1,0:T(8,128)S(1)}) custom-call(f32[128,128]{1,0:T(8,128)S(1)} %bitcast.19, f32[184,128]{1,0:T(8,128)S(1)} %shard_map.159.fixed_ref), custom_call_target="tpu_custom_call" | custom-call | tf_op jit(solution)/shard_map/pallas_call | solution.py:533
  55.5 9.2 %all-gather = f32[512,128]{1,0:T(8,128)S(1)} all-gather(f32[128,128]{1,0:T(8,128)S(1)} %get-tuple-element.20), channel_id=2, replica_groups=mesh['tile_z'=8,'tile_y'=8,'tile_x'=2,'depth_x'=2,'depth_core'=2] {'dept..., dimensions={0}, use_global_device_ids=true | all-gather | bytes 327680 | tf_op jit(solution)/shard_map/all_gather | solution.py:545
  64.6 0.0 copy-start.1
  64.6 0.0 copy-start.2
  64.7 0.0 copy-start.3
  64.7 3.9 %shard_map.161 = (f32[3,4,1024]{2,1,0:T(4,128)}, f32[128,128]{1,0:T(8,128)S(1)}) custom-call(f32[4,128,128]{2,1,0:T(8,128)S(1)} %bitcast.18, f32[512,8,128]{2,1,0:T(8,128)S(1)} %get-tuple-element.21.alpha_ref, f32[4104,128]{1,0:T(8,128)S(1)} %get-tuple-element.22.weight_ref, f32[3,512,128]{2,1,0:T(8,128)S(1)} %get-tuple-element.23.shade_ref, ...), custom_call_target="tpu_custom_call" | custom-call | tf_op jit(solution)/shard_map/pallas_call | solution.py:546
  68.5 18.2 %all_to_all.15 = f32[128,1,128]{2,1,0:T(1,128)S(1)} all-to-all(f32[128,1,128]{2,1,0:T(1,128)S(1)} %bitcast.22), channel_id=1, replica_groups={{0,6,8,14,16,22,24,30,32,38,40,46,48,54,56,62,64,70,72,78,80,86,88,94,9..., dimensions={0} | all-to-all | bytes 131072 | tf_op jit(solution)/shard_map/all_to_all | solution.py:465
  86.7 0.8 shard_map.162
  87.5 7.4 %all-gather.1 = f32[640,128]{1,0:T(8,128)S(1)} all-gather(f32[160,128]{1,0:T(8,128)S(1)} %shard_map.162), channel_id=3, replica_groups=mesh['tile_z'=8,'tile_y'=8,'tile_x'=2,'depth_x'=2,'depth_core'=2] {'dept..., dimensions={0}, use_global_device_ids=true | all-gather | bytes 409600 | tf_op jit(solution)/shard_map/all_gather | solution.py:565
  94.9 0.0 copy-done.1
  94.9 0.0 copy-done.2
  94.9 0.0 copy-done.3
  94.9 0.8 shard_map.163
Async XLA Ops:
  2.8 21.6 %collective-permute-start = (f32[160,128]{1,0:T(8,128)}, f32[160,128]{1,0:T(8,128)S(1)}, u32[]{:S(2)}, u32[]{:S(2)}) collective-permute-start(f32[160,128]{1,0:T(8,128)} %get-tuple-element.18.mine_ref.params_ref), channel_id=1, source_target_pairs={{0,6},{6,0},{2,4},{4,2},{1,7},{7,1},{3,5},{5,3},{8,14},{14,8},{10,... | collective-permute-start | bytes 245768 | tf_op jit(solution)/shard_map/ppermute | solution.py:512
  8.0 27.1 %all-to-all-start = ((s32[64,1,128]{2,1,0:T(1,128)}), s32[64,1,128]{2,1,0:T(1,128)S(1)}, u32[]{:S(2)}, u32[]{:S(2)}) async-start(s32[64,1,128]{2,1,0:T(1,128)} %bitcast.24), calls=%async_computation | async-start | bytes 65536 | tf_op jit(solution)/shard_map/all_to_all | solution.py:458
  24.4 0.9 copy-start
  36.7 15.7 %all-to-all-start.1 = ((f32[64,2,128]{2,1,0:T(2,128)}), f32[64,2,128]{2,1,0:T(2,128)S(1)}, u32[]{:S(2)}, u32[]{:S(2)}) async-start(f32[64,2,128]{2,1,0:T(2,128)} %shard_map.158), calls=%async_computation.1 | async-start | bytes 131072 | tf_op jit(solution)/shard_map/all_to_all | solution.py:458
  44.2 0.8 copy-start.4
  45.0 0.7 copy-start.5
  64.6 30.2 %copy-start.1 = (f32[160,128]{1,0:T(8,128)S(1)}, f32[160,128]{1,0:T(8,128)}, u32[]{:S(2)}) copy-start(f32[160,128]{1,0:T(8,128)} %get-tuple-element.18.mine_ref.params_ref) | copy-start | bytes 245764
  64.6 30.2 %copy-start.2 = (f32[10,2048]{1,0:T(8,128)S(1)}, f32[10,2048]{1,0:T(8,128)}, u32[]{:S(2)}) copy-start(f32[10,2048]{1,0:T(8,128)} %first_ref.1) | copy-start | bytes 245764
  64.7 30.2 %copy-start.3 = (f32[10,2048]{1,0:T(8,128)S(1)}, f32[10,2048]{1,0:T(8,128)}, u32[]{:S(2)}) copy-start(f32[10,2048]{1,0:T(8,128)} %second_ref.1) | copy-start | bytes 245764

commit v5 on v4

--- a/solution.py
+++ b/solution.py
@@ -56,34 +56,19 @@
     return jnp.where(iota((rows, LANES), 0) == index, 1.0, 0.0)
 
 
-def request_kernel(
-    owner_hbm,
-    row_hbm,
-    position_hbm,
-    scale_hbm,
-    opacity_hbm,
-    color_hbm,
-    request_ref,
-    list_ref,
-    params_ref,
-    owner_ref,
-    row_ref,
-    position,
-    scale,
-    opacity,
-    color,
-    sems,
-):
-    sources = (owner_hbm, row_hbm, position_hbm, scale_hbm, opacity_hbm, color_hbm)
-    held = (owner_ref, row_ref, position, scale, opacity, color)
+def fetch(sources, held, sems):
     copies = [
         pltpu.make_async_copy(source, there, sems.at[n])
         for n, (source, there) in enumerate(zip(sources, held))
     ]
     for copy in copies:
         copy.start()
-    for copy in copies[:2]:
+    for copy in copies:
         copy.wait()
+
+
+def request_kernel(owner_hbm, row_hbm, request_ref, list_ref, owner_ref, row_ref, sems):
+    fetch((owner_hbm, row_hbm), (owner_ref, row_ref), sems)
     earlier = jnp.where(iota((SLAB, SLAB), 0) < iota((SLAB, SLAB), 1), 1.0, 0.0).astype(BF16)
     before = jnp.zeros((LANES, 1), F32)
     total = jnp.zeros((LANES // 2, LANES), F32)
@@ -103,9 +88,26 @@
         list_ref[TILES + b : TILES + b + 1, :] = rank
         list_ref[2 * TILES + b : 2 * TILES + b + 1, :] = row
     list_ref[3 * TILES :, :] = jnp.zeros((TILES, LANES), I32)
-    request_ref[...] = total.astype(I32)
-    for copy in copies[2:]:
-        copy.wait()
+    request_ref[:, 0, :] = total.astype(I32)
+    request_ref[:, 1, :] = jnp.zeros((LANES // 2, LANES), I32)
+
+
+def layout_kernel(
+    list_hbm,
+    position_hbm,
+    scale_hbm,
+    opacity_hbm,
+    color_hbm,
+    params_ref,
+    position,
+    scale,
+    opacity,
+    color,
+    sems,
+):
+    fetch(
+        (position_hbm, scale_hbm, opacity_hbm, color_hbm), (position, scale, opacity, color), sems
+    )
     for a in range(BLOCKS):
         at = slice(a * LANES, (a + 1) * LANES)
         params_ref[a * PARAMS : a * PARAMS + 3, :] = position[:, at]
@@ -150,7 +152,7 @@
 
 def reply_kernel(asked_ref, table_ref, reply_ref, columns, held):
     half = LANES // 2
-    columns[...] = asked_ref[...].T
+    columns[...] = asked_ref[:, 0, :].T
     for h in range(2):
         slots = columns[h * 16 : h * 16 + 16, :]
         rows = jnp.concatenate([slots[:5], slots[5:10]], axis=1)
@@ -493,22 +495,23 @@
     plane = LANES // 2
     flat = (BLOCKS * PARAMS, LANES)
     lists = (TILES, SLAB)
-    sources = (
-        list_owner.reshape(lists),
-        list_row.reshape(lists),
-        positions,
-        log_scales,
-        opacity_logits,
-        colors,
-    )
-    request, listing, params = call(
+    named = (list_owner.reshape(lists), list_row.reshape(lists))
+    request, listing = call(
         request_kernel,
-        [((plane, LANES), I32), ((16, LANES), I32), (flat, F32)],
-        [HBM] * 6,
-        [pltpu.VMEM(a.shape, a.dtype) for a in sources] + [pltpu.SemaphoreType.DMA((6,))],
+        [((plane, 2, LANES), I32), ((16, LANES), I32)],
+        [HBM] * 2,
+        [pltpu.VMEM(lists, I32)] * 2 + [pltpu.SemaphoreType.DMA((2,))],
         GRANT_ALL,
-    )(*sources)
-    asked = exchanged_in_plane(request.reshape(plane, 1, LANES)).reshape(plane, LANES)
+    )(*named)
+    asked = exchanged_in_plane(request)
+    groups = (positions, log_scales, opacity_logits, colors)
+    (params,) = call(
+        layout_kernel,
+        [(flat, F32)],
+        [HBM] * 5,
+        [pltpu.VMEM(a.shape, F32) for a in groups] + [pltpu.SemaphoreType.DMA((4,))],
+        GRANT_ALL,
+    )(listing, *groups)
     theirs = lax.ppermute(params, (TILE[2], DEPTH[0]), [(0, 3), (3, 0), (1, 2), (2, 1)])
     side = lax.axis_index(TILE[2]).astype(I32).reshape(1)
     (table,) = call(

time: 96.3 us -> 100 us (1.038)
  starting transfers between devices: 26.2 us -> 31.7 us
  waiting for transfers between devices: 15.9 us -> 10.4 us
  blocking collectives: 34.7 us -> 37.2 us
  Pallas kernels: 13 us -> 14.4 us
    all_to_all x2, waiting for transfers between devices: 15.9 us -> 7.86 us  [exchanged_in_plane(): return lax.all_to_all(array, TILE[:2], 0, 0, tiled=True)]
    all_to_all x2, starting transfers between devices: 20.9 us -> 27.3 us  [exchanged_in_plane(): return lax.all_to_all(array, TILE[:2], 0, 0, tiled=True)]
    ppermute x1, waiting for transfers between devices: 0.01 us -> 2.5 us  [body(): lax.ppermute(params, (TILE[2], DEPTH[0]), [(0, 3), (3, 0), (1, 2), (2, 1)])]
    all_to_all x1, blocking collectives: 18.2 us -> 20.3 us  [exchanged(): lax.all_to_all(array.reshape(LANES, 1, LANES), (*TILE, DEPTH[0]), 0, 0, a...]
    pallas_call x1 -> x2, Pallas kernels: 2.16 us -> 3.6 us  [the longest x1 2.1 us: body(): call(request_kernel, [((plane, 2, LANES), I32), ((16, LANES), I32)], [HBM...]
  transfers between devices with their start and end apart: 3 -> 3, of which waited for: 2 -> 3; matrix products, arithmetic and copies ran while one was open for 3% -> 3% of each run, Pallas kernels for 1% -> 2%
where the time goes in v5:
time: 100 us; the launch traced here: 99.6 us
  blocking collectives  37.2 us (37%)
  starting transfers between devices  31.7 us (32%)
  Pallas kernels  14.4 us (14%)
  waiting for transfers between devices  10.4 us (10%)
  local copies, waits for them, and re-layouts  3.9 us (4%)
  other arithmetic  1.32 us (1%)
    all_to_all x2, starting transfers between devices, exchanged_in_plane(): return lax.all_to_all(array, TILE[:2], 0, 0, tiled=True)  27.3 us
    all_to_all x1, blocking collectives, exchanged(): lax.all_to_all(array.reshape(LANES, 1, LANES), (*TILE, DEPTH[0]), 0, 0, a...  20.3 us
    all_gather x1, blocking collectives, body(): slabs = lax.all_gather(slab[None], DEPTH, axis=0, tiled=True)  9.47 us
    all_to_all x2, waiting for transfers between devices, exchanged_in_plane(): return lax.all_to_all(array, TILE[:2], 0, 0, tiled=True)  7.86 us
    all_gather x1, blocking collectives, body(): sums = lax.all_gather(sums[None], DEPTH, axis=0, tiled=True)  7.4 us
    ppermute x1, starting transfers between devices, body(): lax.ppermute(params, (TILE[2], DEPTH[0]), [(0, 3), (3, 0), (1, 2), (2, 1)])  4.38 us
    pallas_call x1, Pallas kernels, body(): call(backward_kernel, [((3, TILES, 1024), F32), (square, F32)], [VMEM] *...  3.87 us
    pallas_call x1, Pallas kernels, body(): call(forward_kernel, [(square, F32), (field, F32), (tilted, F32), ((3, TI...  3.02 us
  transfers between devices with their start and end apart: 3, of which 3 were waited for; matrix products, arithmetic and copies ran while one was open for 3% of the time, Pallas kernels for 2%

profile of v5, /device:TPU:1, one launch (start us, length us, event | category | flops | bytes accessed | tf_op | source)
XLA Modules:
  0.0 99.6 jit_solution(4146131919077133552)
XLA Ops:
  0.6 2.1 %shard_map.156 = (s32[64,2,128]{2,1,0:T(2,128)}, s32[16,128]{1,0:T(8,128)}) custom-call(s32[4,128]{1,0:T(4,128)} %bitcast.19, s32[4,128]{1,0:T(4,128)} %bitcast.20), custom_call_target="tpu_custom_call" | custom-call | tf_op jit(solution)/shard_map/pallas_call | solution.py:499
  2.7 17.2 %all-to-all-start = ((s32[64,2,128]{2,1,0:T(2,128)}), s32[64,2,128]{2,1,0:T(2,128)S(1)}, u32[]{:S(2)}, u32[]{:S(2)}) async-start(s32[64,2,128]{2,1,0:T(2,128)} %get-tuple-element.16), calls=%async_computation | async-start | bytes 131072 | tf_op jit(solution)/shard_map/all_to_all | solution.py:460
  19.9 1.5 %shard_map.157.mine_ref.params_ref = f32[160,128]{1,0:T(8,128)} custom-call(s32[16,128]{1,0:T(8,128)} %get-tuple-element.17.list_hbm.list_ref, f32[3,2048]{1,0:T(4,128)} %position_hbm.1, f32[3,2048]{1,0:T(4,128)} %scale_hbm.1, f32[1,2048]{1,0:T(1,128)} %opacity_hbm.1, f32[3,2048]{1,0:T(4,128)} %color_hbm.1), custom_call_target="tpu_custom_call" | custom-call | tf_op jit(solution)/shard_map/pallas_call | solution.py:508
  21.4 4.4 %collective-permute-start = (f32[160,128]{1,0:T(8,128)}, f32[160,128]{1,0:T(8,128)S(1)}, u32[]{:S(2)}, u32[]{:S(2)}) collective-permute-start(f32[160,128]{1,0:T(8,128)} %shard_map.157.mine_ref.params_ref), channel_id=1, source_target_pairs={{0,6},{6,0},{2,4},{4,2},{1,7},{7,1},{3,5},{5,3},{8,14},{14,8},{10,... | collective-permute-start | bytes 245768 | tf_op jit(solution)/shard_map/ppermute | solution.py:515
  25.8 2.5 %collective-permute-done.theirs_ref = f32[160,128]{1,0:T(8,128)S(1)} collective-permute-done((f32[160,128]{1,0:T(8,128)}, f32[160,128]{1,0:T(8,128)S(1)}, u32[]{:S(2)}, u32[]{:S(2)}) %collective-permute-start) | collective-permute-done | bytes 81952 | tf_op jit(solution)/shard_map/ppermute | solution.py:515
  28.3 0.0 copy-start
  28.3 0.9 copy-done
  29.2 0.1 shard_map.158.table_ref
  29.3 1.7 %all-to-all-done.asked_ref = s32[64,2,128]{2,1,0:T(2,128)S(1)} async-done(((s32[64,2,128]{2,1,0:T(2,128)}), s32[64,2,128]{2,1,0:T(2,128)S(1)}, u32[]{:S(2)}, u32[]{:S(2)}) %all-to-all-start) | async-done | bytes 65568 | tf_op jit(solution)/shard_map/all_to_all | solution.py:460
  31.0 1.6 %shard_map.159 = f32[64,2,128]{2,1,0:T(2,128)} custom-call(s32[64,2,128]{2,1,0:T(2,128)S(1)} %all-to-all-done.asked_ref, bf16[512,384]{1,0:T(8,128)(2,1)S(1)} %shard_map.158.table_ref), custom_call_target="tpu_custom_call" | custom-call | tf_op jit(solution)/shard_map/pallas_call | solution.py:520
  32.6 10.2 %all-to-all-start.1 = ((f32[64,2,128]{2,1,0:T(2,128)}), f32[64,2,128]{2,1,0:T(2,128)S(1)}, u32[]{:S(2)}, u32[]{:S(2)}) async-start(f32[64,2,128]{2,1,0:T(2,128)} %shard_map.159), calls=%async_computation.1 | async-start | bytes 131072 | tf_op jit(solution)/shard_map/all_to_all | solution.py:460
  42.8 0.8 reshape.37
  43.5 0.7 convert_element_type.9
  44.2 0.7 convert_element_type.10
  44.9 0.7 concatenate.3.scalar_ref
  45.6 0.0 copy-start.4
  45.6 0.8 copy-done.4
  46.4 0.0 copy-start.5
  46.4 0.7 copy-done.5
  47.1 0.6 shard_map.160.fixed_ref
  47.7 6.2 %all-to-all-done.1 = f32[64,2,128]{2,1,0:T(2,128)S(1)} async-done(((f32[64,2,128]{2,1,0:T(2,128)}), f32[64,2,128]{2,1,0:T(2,128)S(1)}, u32[]{:S(2)}, u32[]{:S(2)}) %all-to-all-start.1) | async-done | bytes 65568 | tf_op jit(solution)/shard_map/all_to_all | solution.py:460
  53.8 3.0 %shard_map.161 = (f32[128,128]{1,0:T(8,128)S(1)}, f32[512,8,128]{2,1,0:T(8,128)S(1)}, f32[4104,128]{1,0:T(8,128)S(1)}, f32[3,512,128]{2,1,0:T(8,128)S(1)}, f32[64,128]{1,0:T(8,128)S(1)}) custom-call(f32[128,128]{1,0:T(8,128)S(1)} %bitcast.15, f32[184,128]{1,0:T(8,128)S(1)} %shard_map.160.fixed_ref), custom_call_target="tpu_custom_call" | custom-call | tf_op jit(solution)/shard_map/pallas_call | solution.py:536
  56.9 9.5 %all-gather = f32[512,128]{1,0:T(8,128)S(1)} all-gather(f32[128,128]{1,0:T(8,128)S(1)} %get-tuple-element.18), channel_id=2, replica_groups=mesh['tile_z'=8,'tile_y'=8,'tile_x'=2,'depth_x'=2,'depth_core'=2] {'dept..., dimensions={0}, use_global_device_ids=true | all-gather | bytes 327680 | tf_op jit(solution)/shard_map/all_gather | solution.py:548
  66.3 0.0 copy-start.1
  66.3 0.0 copy-start.2
  66.3 0.0 copy-start.3
  66.3 3.9 %shard_map.162 = (f32[3,4,1024]{2,1,0:T(4,128)}, f32[128,128]{1,0:T(8,128)S(1)}) custom-call(f32[4,128,128]{2,1,0:T(8,128)S(1)} %bitcast.14, f32[512,8,128]{2,1,0:T(8,128)S(1)} %get-tuple-element.19.alpha_ref, f32[4104,128]{1,0:T(8,128)S(1)} %get-tuple-element.20.weight_ref, f32[3,512,128]{2,1,0:T(8,128)S(1)} %get-tuple-element.21.shade_ref, ...), custom_call_target="tpu_custom_call" | custom-call | tf_op jit(solution)/shard_map/pallas_call | solution.py:549
  70.2 20.3 %all_to_all.15 = f32[128,1,128]{2,1,0:T(1,128)S(1)} all-to-all(f32[128,1,128]{2,1,0:T(1,128)S(1)} %bitcast.17), channel_id=1, replica_groups={{0,6,8,14,16,22,24,30,32,38,40,46,48,54,56,62,64,70,72,78,80,86,88,94,9..., dimensions={0} | all-to-all | bytes 131072 | tf_op jit(solution)/shard_map/all_to_all | solution.py:467
  90.5 0.8 shard_map.163
  91.3 7.4 %all-gather.1 = f32[640,128]{1,0:T(8,128)S(1)} all-gather(f32[160,128]{1,0:T(8,128)S(1)} %shard_map.163), channel_id=3, replica_groups=mesh['tile_z'=8,'tile_y'=8,'tile_x'=2,'depth_x'=2,'depth_core'=2] {'dept..., dimensions={0}, use_global_device_ids=true | all-gather | bytes 409600 | tf_op jit(solution)/shard_map/all_gather | solution.py:568
  98.7 0.0 copy-done.1
  98.7 0.0 copy-done.2
  98.8 0.0 copy-done.3
  98.8 0.8 shard_map.164
Async XLA Ops:
  2.7 28.2 %all-to-all-start = ((s32[64,2,128]{2,1,0:T(2,128)}), s32[64,2,128]{2,1,0:T(2,128)S(1)}, u32[]{:S(2)}, u32[]{:S(2)}) async-start(s32[64,2,128]{2,1,0:T(2,128)} %get-tuple-element.16), calls=%async_computation | async-start | bytes 131072 | tf_op jit(solution)/shard_map/all_to_all | solution.py:460
  21.4 6.9 %collective-permute-start = (f32[160,128]{1,0:T(8,128)}, f32[160,128]{1,0:T(8,128)S(1)}, u32[]{:S(2)}, u32[]{:S(2)}) collective-permute-start(f32[160,128]{1,0:T(8,128)} %shard_map.157.mine_ref.params_ref), channel_id=1, source_target_pairs={{0,6},{6,0},{2,4},{4,2},{1,7},{7,1},{3,5},{5,3},{8,14},{14,8},{10,... | collective-permute-start | bytes 245768 | tf_op jit(solution)/shard_map/ppermute | solution.py:515
  28.3 0.9 copy-start
  32.6 21.2 %all-to-all-start.1 = ((f32[64,2,128]{2,1,0:T(2,128)}), f32[64,2,128]{2,1,0:T(2,128)S(1)}, u32[]{:S(2)}, u32[]{:S(2)}) async-start(f32[64,2,128]{2,1,0:T(2,128)} %shard_map.159), calls=%async_computation.1 | async-start | bytes 131072 | tf_op jit(solution)/shard_map/all_to_all | solution.py:460
  45.6 0.8 copy-start.4
  46.4 0.7 copy-start.5
  66.3 32.4 %copy-start.1 = (f32[160,128]{1,0:T(8,128)S(1)}, f32[160,128]{1,0:T(8,128)}, u32[]{:S(2)}) copy-start(f32[160,128]{1,0:T(8,128)} %shard_map.157.mine_ref.params_ref) | copy-start | bytes 245764
  66.3 32.4 %copy-start.2 = (f32[10,2048]{1,0:T(8,128)S(1)}, f32[10,2048]{1,0:T(8,128)}, u32[]{:S(2)}) copy-start(f32[10,2048]{1,0:T(8,128)} %first_ref.1) | copy-start | bytes 245764
  66.3 32.4 %copy-start.3 = (f32[10,2048]{1,0:T(8,128)S(1)}, f32[10,2048]{1,0:T(8,128)}, u32[]{:S(2)}) copy-start(f32[10,2048]{1,0:T(8,128)} %second_ref.1) | copy-start | bytes 245764

commit v6 on v4

--- a/solution.py
+++ b/solution.py
@@ -63,15 +63,18 @@
     scale_hbm,
     opacity_hbm,
     color_hbm,
-    request_ref,
-    list_ref,
-    params_ref,
+    request_hbm,
+    list_hbm,
+    params_hbm,
     owner_ref,
     row_ref,
     position,
     scale,
     opacity,
     color,
+    request_ref,
+    list_ref,
+    params_ref,
     sems,
 ):
     sources = (owner_hbm, row_hbm, position_hbm, scale_hbm, opacity_hbm, color_hbm)
@@ -82,6 +85,20 @@
     ]
     for copy in copies:
         copy.start()
+    for copy in copies[2:]:
+        copy.wait()
+    for a in range(BLOCKS):
+        at = slice(a * LANES, (a + 1) * LANES)
+        params_ref[a * PARAMS : a * PARAMS + 3, :] = position[:, at]
+        params_ref[a * PARAMS + 3 : a * PARAMS + 6, :] = scale[:, at]
+        params_ref[a * PARAMS + 6 : a * PARAMS + 7, :] = opacity[:, at]
+        params_ref[a * PARAMS + 7 : a * PARAMS + 10, :] = color[:, at]
+    results = [
+        pltpu.make_async_copy(params_ref, params_hbm, sems.at[6]),
+        pltpu.make_async_copy(request_ref, request_hbm, sems.at[7]),
+        pltpu.make_async_copy(list_ref, list_hbm, sems.at[8]),
+    ]
+    results[0].start()
     for copy in copies[:2]:
         copy.wait()
     earlier = jnp.where(iota((SLAB, SLAB), 0) < iota((SLAB, SLAB), 1), 1.0, 0.0).astype(BF16)
@@ -104,14 +121,10 @@
         list_ref[2 * TILES + b : 2 * TILES + b + 1, :] = row
     list_ref[3 * TILES :, :] = jnp.zeros((TILES, LANES), I32)
     request_ref[...] = total.astype(I32)
-    for copy in copies[2:]:
-        copy.wait()
-    for a in range(BLOCKS):
-        at = slice(a * LANES, (a + 1) * LANES)
-        params_ref[a * PARAMS : a * PARAMS + 3, :] = position[:, at]
-        params_ref[a * PARAMS + 3 : a * PARAMS + 6, :] = scale[:, at]
-        params_ref[a * PARAMS + 6 : a * PARAMS + 7, :] = opacity[:, at]
-        params_ref[a * PARAMS + 7 : a * PARAMS + 10, :] = color[:, at]
+    for result in results[1:]:
+        result.start()
+    for result in results:
+        result.wait()
 
 
 def fixed_kernel(scalar_ref, target_ref, list_ref, fixed_ref):
@@ -251,7 +264,7 @@
         for b in range(TILES):
             trans, red, green, blue = carry[4 * b : 4 * b + 4]
             at = b * SLAB + k
-            get = lambda ref, p: jnp.broadcast_to(ref[p, pl.ds(at, 1), :], (8, LANES))
+            get = lambda ref, p: ref[p, pl.ds(at, 8, stride=0), :]
             ex = pixel_x - get(spread, 0)
             ey = pixel_y - get(spread, 1)
             power = ex * (get(spread, 2) * ex + get(spread, 3) * ey) + get(spread, 4) * ey * ey
@@ -268,9 +281,20 @@
         return tuple(out)
 
     one, zero = jnp.ones((8, LANES), F32), jnp.zeros((8, LANES), F32)
-    out = lax.fori_loop(0, SLAB, step, (one, zero, zero, zero) * TILES, unroll=4)
+    out = lax.fori_loop(0, SLAB, step, (one, zero, zero, zero) * TILES, unroll=32)
     for q in range(4 * TILES):
         slab_ref[q * 8 : (q + 1) * 8, :] = out[q]
+
+
+def row_sums(rows):
+    a = rows[0]
+    b = a + rows[1]
+    c = b + rows[2]
+    d = c + rows[3]
+    e = rows[7]
+    f = e + rows[6]
+    g = f + rows[5]
+    return d + g + rows[4], e + f + g - (a + b + c + d), 7.0 * a + 5.0 * (b + e) + 3.0 * (c + f) + (d + g)
 
 
 def backward_kernel(
@@ -280,13 +304,15 @@
     shade_ref,
     entry_ref,
     fixed_ref,
-    image_ref,
+    image_hbm,
     outgoing_ref,
     slope,
     moment,
     grads,
     placed,
     picture,
+    image_ref,
+    sem,
 ):
     depth = fixed_ref[HERE : HERE + 8, :]
     back = [fixed_ref[BACK + c * 8 : BACK + c * 8 + 8, :] for c in range(3)]
@@ -317,13 +343,15 @@
             image_ref[c, :, s * LANES : (s + 1) * LANES] = picture[
                 pl.ds(c * TILES * 8 + s, TILES, stride=8), :
             ]
+    shown = pltpu.make_async_copy(image_ref, image_hbm, sem)
+    shown.start()
 
     def step(n, carry):
         k = SLAB - 1 - n
         out = []
         for b in range(TILES):
             at = b * SLAB + k
-            get = lambda p: jnp.broadcast_to(shade_ref[p, pl.ds(at, 1), :], (8, LANES))
+            get = lambda p: shade_ref[p, pl.ds(at, 8, stride=0), :]
             shade = sum(get(c) * seen[b][c] for c in range(3))
             gap = shade - carry[b]
             rows = pl.ds(at, 8, stride=PITCH)
@@ -331,22 +359,27 @@
             out.append(carry[b] + alpha_ref[at] * gap)
         return tuple(out)
 
-    lax.fori_loop(0, SLAB, step, tuple(behind), unroll=4)
+    lax.fori_loop(0, SLAB, step, tuple(behind), unroll=8)
 
     index = iota((16, LANES), 0)
     lane = iota((16, LANES), 1)
-    across = (lane & 31) - 16
+    across, down = (lane & 31) - 16, lane >> 5
     powers = []
-    for s in range(8):
-        down = s * 4 + (lane >> 5) - 16
-        power = jnp.where(index == 0, 1, 0)
-        for n, value in enumerate((across, down, across * across, across * down, down * down), 1):
+    for rows in (
+        (1, across, down, across * across, across * down, down * down),
+        (0, 0, 4, 0, 4 * across, 8 * down),
+        (0, 0, 0, 0, 0, 16),
+    ):
+        power = jnp.zeros((16, LANES), I32)
+        for n, value in enumerate(rows):
             power = jnp.where(index == n, value, power)
         powers += [power.astype(F32).astype(BF16)] * 3
     powers = jnp.concatenate(powers, axis=1)
     for b in range(TILES):
         at = [slice(s * PITCH + b * SLAB, s * PITCH + (b + 1) * SLAB) for s in range(8)]
-        field = jnp.concatenate([side_by_side(slope[at[s], :]) for s in range(8)], axis=1)
+        field = jnp.concatenate(
+            [side_by_side(part) for part in row_sums([slope[at[s], :] for s in range(8)])], axis=1
+        )
         moment[b * 32 : b * 32 + 16, :] = dot(powers, field, NT)
         gaze, weights = [], []
         for s in range(8):
@@ -411,6 +444,7 @@
         named = jnp.concatenate([named, named, named], axis=1)
         outgoing = outgoing + dot(named, side_by_side(placed[...]), NT)
     outgoing_ref[...] = outgoing
+    shown.wait()
 
 
 def collect_kernel(incoming_ref, sums_ref, turned):
@@ -443,12 +477,12 @@
         new_second_ref[:, at] = second
 
 
-def call(kernel, outs, ins, scratch=(), grant=40):
+def call(kernel, outs, ins, scratch=(), grant=40, to=None):
     return pl.pallas_call(
         kernel,
         out_shape=[jax.ShapeDtypeStruct(shape, dtype) for shape, dtype in outs],
         in_specs=ins,
-        out_specs=[VMEM] * len(outs),
+        out_specs=to or [VMEM] * len(outs),
         scratch_shapes=list(scratch),
         compiler_params=pltpu.CompilerParams(vmem_limit_bytes=grant * 2**20),
     )
@@ -501,12 +535,16 @@
         opacity_logits,
         colors,
     )
+    results = [((plane, LANES), I32), ((16, LANES), I32), (flat, F32)]
     request, listing, params = call(
         request_kernel,
-        [((plane, LANES), I32), ((16, LANES), I32), (flat, F32)],
+        results,
         [HBM] * 6,
-        [pltpu.VMEM(a.shape, a.dtype) for a in sources] + [pltpu.SemaphoreType.DMA((6,))],
+        [pltpu.VMEM(a.shape, a.dtype) for a in sources]
+        + [pltpu.VMEM(*result) for result in results]
+        + [pltpu.SemaphoreType.DMA((9,))],
         GRANT_ALL,
+        [HBM] * 3,
     )(*sources)
     asked = exchanged_in_plane(request.reshape(plane, 1, LANES)).reshape(plane, LANES)
     theirs = lax.ppermute(params, (TILE[2], DEPTH[0]), [(0, 3), (3, 0), (1, 2), (2, 1)])
@@ -536,11 +574,11 @@
             (square, F32),
             (field, F32),
             (tilted, F32),
-            ((3, TILES * SLAB, LANES), F32),
+            ((3, TILES * SLAB + 8, LANES), F32),
             ((TILES * 16, LANES), F32),
         ],
         [VMEM] * 2,
-        [held, held, pltpu.VMEM((6, TILES * SLAB, LANES), F32)],
+        [held, held, pltpu.VMEM((6, TILES * SLAB + 8, LANES), F32)],
     )(fetched, fixed)
     slabs = lax.all_gather(slab[None], DEPTH, axis=0, tiled=True)
     image, outgoing = call(
@@ -553,7 +591,10 @@
             pltpu.VMEM((PARAMS * TILES, LANES), F32),
             held,
             pltpu.VMEM((3 * TILES * 8, LANES), F32),
+            pltpu.VMEM((3, TILES, 1024), F32),
+            pltpu.SemaphoreType.DMA(()),
         ],
+        to=[HBM, VMEM],
     )(slabs, alpha, weight, shade, entry, fixed)
     incoming = exchanged(outgoing)
     (sums,) = call(

time: 96.3 us -> 95 us (0.987)
  Pallas kernels: 13 us -> 11.7 us
    pallas_call x1, Pallas kernels: 3.87 us -> 2.87 us  [body(): call(backward_kernel, [((3, TILES, 1024), F32), (square, F32)], [VMEM] *...]
where the time goes in v6:
time: 95 us; the launch traced here: 94.5 us
  blocking collectives  34.7 us (37%)
  starting transfers between devices  26.2 us (28%)
  waiting for transfers between devices  16 us (17%)
  Pallas kernels  11.7 us (12%)
  local copies, waits for them, and re-layouts  3.89 us (4%)
  other arithmetic  1.32 us (1%)
    all_to_all x2, starting transfers between devices, exchanged_in_plane(): return lax.all_to_all(array, TILE[:2], 0, 0, tiled=True)  20.9 us
    all_to_all x1, blocking collectives, exchanged(): lax.all_to_all(array.reshape(LANES, 1, LANES), (*TILE, DEPTH[0]), 0, 0, a...  18.1 us
    all_to_all x2, waiting for transfers between devices, exchanged_in_plane(): return lax.all_to_all(array, TILE[:2], 0, 0, tiled=True)  16 us
    all_gather x1, blocking collectives, body(): slabs = lax.all_gather(slab[None], DEPTH, axis=0, tiled=True)  9.18 us
    all_gather x1, blocking collectives, body(): sums = lax.all_gather(sums[None], DEPTH, axis=0, tiled=True)  7.39 us
    ppermute x1, starting transfers between devices, body(): lax.ppermute(params, (TILE[2], DEPTH[0]), [(0, 3), (3, 0), (1, 2), (2, 1)])  5.22 us
    pallas_call x1, Pallas kernels, body(): call(backward_kernel, [((3, TILES, 1024), F32), (square, F32)], [VMEM] *...  2.87 us
    pallas_call x1, Pallas kernels, body(): call(forward_kernel, [(square, F32), (field, F32), (tilted, F32), ((3, TI...  2.62 us
  transfers between devices with their start and end apart: 3, of which 2 were waited for; matrix products, arithmetic and copies ran while one was open for 3% of the time, Pallas kernels for 1%

profile of v6, /device:TPU:1, one launch (start us, length us, event | category | flops | bytes accessed | tf_op | source)
XLA Modules:
  0.0 94.5 jit_solution(14663451709047992490)
XLA Ops:
  0.6 2.3 %shard_map.156 = (s32[64,128]{1,0:T(8,128)}, s32[16,128]{1,0:T(8,128)}, f32[160,128]{1,0:T(8,128)}) custom-call(s32[4,128]{1,0:T(4,128)} %bitcast.25, s32[4,128]{1,0:T(4,128)} %bitcast.26, f32[3,2048]{1,0:T(4,128)} %position_hbm.1, f32[3,2048]{1,0:T(4,128)} %scale_hbm.1, f32[1,2048]{1,0:T(1,128)} %opacity_hbm.1, f32[3,2048]{1,0:T(4,128)} %color_hbm.1), custom_call_target="tpu_custom_call" | custom-call | tf_op jit(solution)/shard_map/pallas_call | solution.py:539
  2.9 5.2 %collective-permute-start = (f32[160,128]{1,0:T(8,128)}, f32[160,128]{1,0:T(8,128)S(1)}, u32[]{:S(2)}, u32[]{:S(2)}) collective-permute-start(f32[160,128]{1,0:T(8,128)} %get-tuple-element.18.mine_ref.params_ref), channel_id=1, source_target_pairs={{0,6},{6,0},{2,4},{4,2},{1,7},{7,1},{3,5},{5,3},{8,14},{14,8},{10,... | collective-permute-start | bytes 245768 | tf_op jit(solution)/shard_map/ppermute | solution.py:550
  8.2 16.3 %all-to-all-start = ((s32[64,1,128]{2,1,0:T(1,128)}), s32[64,1,128]{2,1,0:T(1,128)S(1)}, u32[]{:S(2)}, u32[]{:S(2)}) async-start(s32[64,1,128]{2,1,0:T(1,128)} %bitcast.24), calls=%async_computation | async-start | bytes 65536 | tf_op jit(solution)/shard_map/all_to_all | solution.py:492
  24.5 0.0 collective-permute-done.theirs_ref
  24.5 0.0 copy-start
  24.5 0.9 copy-done
  25.4 0.1 shard_map.157.table_ref
  25.5 9.8 %all-to-all-done = s32[64,1,128]{2,1,0:T(1,128)S(1)} async-done(((s32[64,1,128]{2,1,0:T(1,128)}), s32[64,1,128]{2,1,0:T(1,128)S(1)}, u32[]{:S(2)}, u32[]{:S(2)}) %all-to-all-start) | async-done | bytes 32800 | tf_op jit(solution)/shard_map/all_to_all | solution.py:492
  35.3 1.6 %shard_map.158 = f32[64,2,128]{2,1,0:T(2,128)} custom-call(s32[64,128]{1,0:T(8,128)S(1)} %bitcast.21, bf16[512,384]{1,0:T(8,128)(2,1)S(1)} %shard_map.157.table_ref), custom_call_target="tpu_custom_call" | custom-call | tf_op jit(solution)/shard_map/pallas_call | solution.py:555
  36.9 4.6 %all-to-all-start.1 = ((f32[64,2,128]{2,1,0:T(2,128)}), f32[64,2,128]{2,1,0:T(2,128)S(1)}, u32[]{:S(2)}, u32[]{:S(2)}) async-start(f32[64,2,128]{2,1,0:T(2,128)} %shard_map.158), calls=%async_computation.1 | async-start | bytes 131072 | tf_op jit(solution)/shard_map/all_to_all | solution.py:492
  41.5 0.8 reshape.45
  42.3 0.7 convert_element_type.9
  42.9 0.7 convert_element_type.10
  43.6 0.7 concatenate.3.scalar_ref
  44.3 0.0 copy-start.4
  44.3 0.8 copy-done.4
  45.1 0.0 copy-start.5
  45.1 0.7 copy-done.5
  45.8 0.6 shard_map.159.fixed_ref
  46.4 6.2 %all-to-all-done.1 = f32[64,2,128]{2,1,0:T(2,128)S(1)} async-done(((f32[64,2,128]{2,1,0:T(2,128)}), f32[64,2,128]{2,1,0:T(2,128)S(1)}, u32[]{:S(2)}, u32[]{:S(2)}) %all-to-all-start.1) | async-done | bytes 65568 | tf_op jit(solution)/shard_map/all_to_all | solution.py:492
  52.6 2.6 %shard_map.160 = (f32[128,128]{1,0:T(8,128)S(1)}, f32[512,8,128]{2,1,0:T(8,128)S(1)}, f32[4104,128]{1,0:T(8,128)S(1)}, f32[3,520,128]{2,1,0:T(8,128)S(1)}, f32[64,128]{1,0:T(8,128)S(1)}) custom-call(f32[128,128]{1,0:T(8,128)S(1)} %bitcast.19, f32[184,128]{1,0:T(8,128)S(1)} %shard_map.159.fixed_ref), custom_call_target="tpu_custom_call" | custom-call | tf_op jit(solution)/shard_map/pallas_call | solution.py:571
  55.2 9.2 %all-gather = f32[512,128]{1,0:T(8,128)S(1)} all-gather(f32[128,128]{1,0:T(8,128)S(1)} %get-tuple-element.20), channel_id=2, replica_groups=mesh['tile_z'=8,'tile_y'=8,'tile_x'=2,'depth_x'=2,'depth_core'=2] {'dept..., dimensions={0}, use_global_device_ids=true | all-gather | bytes 327680 | tf_op jit(solution)/shard_map/all_gather | solution.py:583
  64.4 0.0 copy-start.1
  64.4 0.0 copy-start.2
  64.4 0.0 copy-start.3
  64.4 2.9 %shard_map.161 = (f32[3,4,1024]{2,1,0:T(4,128)}, f32[128,128]{1,0:T(8,128)S(1)}) custom-call(f32[4,128,128]{2,1,0:T(8,128)S(1)} %bitcast.18, f32[512,8,128]{2,1,0:T(8,128)S(1)} %get-tuple-element.21.alpha_ref, f32[4104,128]{1,0:T(8,128)S(1)} %get-tuple-element.22.weight_ref, f32[3,520,128]{2,1,0:T(8,128)S(1)} %get-tuple-element.23.shade_ref, ...), custom_call_target="tpu_custom_call" | custom-call | tf_op jit(solution)/shard_map/pallas_call | solution.py:584
  67.3 18.1 %all_to_all.15 = f32[128,1,128]{2,1,0:T(1,128)S(1)} all-to-all(f32[128,1,128]{2,1,0:T(1,128)S(1)} %bitcast.22), channel_id=1, replica_groups={{0,6,8,14,16,22,24,30,32,38,40,46,48,54,56,62,64,70,72,78,80,86,88,94,9..., dimensions={0} | all-to-all | bytes 131072 | tf_op jit(solution)/shard_map/all_to_all | solution.py:499
  85.4 0.8 shard_map.162
  86.2 7.4 %all-gather.1 = f32[640,128]{1,0:T(8,128)S(1)} all-gather(f32[160,128]{1,0:T(8,128)S(1)} %shard_map.162), channel_id=3, replica_groups=mesh['tile_z'=8,'tile_y'=8,'tile_x'=2,'depth_x'=2,'depth_core'=2] {'dept..., dimensions={0}, use_global_device_ids=true | all-gather | bytes 409600 | tf_op jit(solution)/shard_map/all_gather | solution.py:606
  93.6 0.0 copy-done.1
  93.6 0.0 copy-done.2
  93.6 0.0 copy-done.3
  93.6 0.8 shard_map.163
Async XLA Ops:
  2.9 21.6 %collective-permute-start = (f32[160,128]{1,0:T(8,128)}, f32[160,128]{1,0:T(8,128)S(1)}, u32[]{:S(2)}, u32[]{:S(2)}) collective-permute-start(f32[160,128]{1,0:T(8,128)} %get-tuple-element.18.mine_ref.params_ref), channel_id=1, source_target_pairs={{0,6},{6,0},{2,4},{4,2},{1,7},{7,1},{3,5},{5,3},{8,14},{14,8},{10,... | collective-permute-start | bytes 245768 | tf_op jit(solution)/shard_map/ppermute | solution.py:550
  8.2 27.1 %all-to-all-start = ((s32[64,1,128]{2,1,0:T(1,128)}), s32[64,1,128]{2,1,0:T(1,128)S(1)}, u32[]{:S(2)}, u32[]{:S(2)}) async-start(s32[64,1,128]{2,1,0:T(1,128)} %bitcast.24), calls=%async_computation | async-start | bytes 65536 | tf_op jit(solution)/shard_map/all_to_all | solution.py:492
  24.5 0.9 copy-start
  36.9 15.7 %all-to-all-start.1 = ((f32[64,2,128]{2,1,0:T(2,128)}), f32[64,2,128]{2,1,0:T(2,128)S(1)}, u32[]{:S(2)}, u32[]{:S(2)}) async-start(f32[64,2,128]{2,1,0:T(2,128)} %shard_map.158), calls=%async_computation.1 | async-start | bytes 131072 | tf_op jit(solution)/shard_map/all_to_all | solution.py:492
  44.3 0.8 copy-start.4
  45.1 0.7 copy-start.5
  64.4 29.2 %copy-start.1 = (f32[160,128]{1,0:T(8,128)S(1)}, f32[160,128]{1,0:T(8,128)}, u32[]{:S(2)}) copy-start(f32[160,128]{1,0:T(8,128)} %get-tuple-element.18.mine_ref.params_ref) | copy-start | bytes 245764
  64.4 29.2 %copy-start.2 = (f32[10,2048]{1,0:T(8,128)S(1)}, f32[10,2048]{1,0:T(8,128)}, u32[]{:S(2)}) copy-start(f32[10,2048]{1,0:T(8,128)} %first_ref.1) | copy-start | bytes 245764
  64.4 29.2 %copy-start.3 = (f32[10,2048]{1,0:T(8,128)S(1)}, f32[10,2048]{1,0:T(8,128)}, u32[]{:S(2)}) copy-start(f32[10,2048]{1,0:T(8,128)} %second_ref.1) | copy-start | bytes 245764

commit v7 on v6

--- a/solution.py
+++ b/solution.py
@@ -63,18 +63,15 @@
     scale_hbm,
     opacity_hbm,
     color_hbm,
-    request_hbm,
-    list_hbm,
-    params_hbm,
+    request_ref,
+    list_ref,
+    params_ref,
     owner_ref,
     row_ref,
     position,
     scale,
     opacity,
     color,
-    request_ref,
-    list_ref,
-    params_ref,
     sems,
 ):
     sources = (owner_hbm, row_hbm, position_hbm, scale_hbm, opacity_hbm, color_hbm)
@@ -85,20 +82,6 @@
     ]
     for copy in copies:
         copy.start()
-    for copy in copies[2:]:
-        copy.wait()
-    for a in range(BLOCKS):
-        at = slice(a * LANES, (a + 1) * LANES)
-        params_ref[a * PARAMS : a * PARAMS + 3, :] = position[:, at]
-        params_ref[a * PARAMS + 3 : a * PARAMS + 6, :] = scale[:, at]
-        params_ref[a * PARAMS + 6 : a * PARAMS + 7, :] = opacity[:, at]
-        params_ref[a * PARAMS + 7 : a * PARAMS + 10, :] = color[:, at]
-    results = [
-        pltpu.make_async_copy(params_ref, params_hbm, sems.at[6]),
-        pltpu.make_async_copy(request_ref, request_hbm, sems.at[7]),
-        pltpu.make_async_copy(list_ref, list_hbm, sems.at[8]),
-    ]
-    results[0].start()
     for copy in copies[:2]:
         copy.wait()
     earlier = jnp.where(iota((SLAB, SLAB), 0) < iota((SLAB, SLAB), 1), 1.0, 0.0).astype(BF16)
@@ -121,26 +104,53 @@
         list_ref[2 * TILES + b : 2 * TILES + b + 1, :] = row
     list_ref[3 * TILES :, :] = jnp.zeros((TILES, LANES), I32)
     request_ref[...] = total.astype(I32)
-    for result in results[1:]:
-        result.start()
-    for result in results:
-        result.wait()
-
-
-def fixed_kernel(scalar_ref, target_ref, list_ref, fixed_ref):
+    for copy in copies[2:]:
+        copy.wait()
+    for a in range(BLOCKS):
+        at = slice(a * LANES, (a + 1) * LANES)
+        params_ref[a * PARAMS : a * PARAMS + 3, :] = position[:, at]
+        params_ref[a * PARAMS + 3 : a * PARAMS + 6, :] = scale[:, at]
+        params_ref[a * PARAMS + 6 : a * PARAMS + 7, :] = opacity[:, at]
+        params_ref[a * PARAMS + 7 : a * PARAMS + 10, :] = color[:, at]
+
+
+def fixed_kernel(
+    depth_ref,
+    view_hbm,
+    length_hbm,
+    cams_hbm,
+    back_hbm,
+    target_hbm,
+    list_hbm,
+    fixed_ref,
+    view_ref,
+    length_ref,
+    cams_ref,
+    back_ref,
+    target_ref,
+    list_ref,
+    sems,
+):
+    sources = (view_hbm, length_hbm, cams_hbm, back_hbm, target_hbm, list_hbm)
+    held = (view_ref, length_ref, cams_ref, back_ref, target_ref, list_ref)
+    copies = [
+        pltpu.make_async_copy(source, there, sems.at[n])
+        for n, (source, there) in enumerate(zip(sources, held))
+    ]
+    for copy in copies:
+        copy.start()
+    for copy in copies:
+        copy.wait()
     for i in range(2):
         for j in range(4):
             at = (i * 4 + j) * TILES
-            fixed_ref[at : at + TILES, :] = per_tile(
-                [scalar_ref[scalar_ref[b].astype(I32) * 8 + i * 4 + j + 12] for b in range(TILES)]
-            )
-    depth = scalar_ref[11]
-    place = depth * SLAB + iota((TILES, LANES), 1).astype(F32)
-    length = per_tile([scalar_ref[4 + b] for b in range(TILES)])
-    fixed_ref[LIVE : LIVE + TILES, :] = jnp.where(place < length, 1.0, 0.0)
+            fixed_ref[at : at + TILES, :] = per_tile([cams_ref[view_ref[b], i, j] for b in range(TILES)])
+    place = depth_ref[0] * SLAB + iota((TILES, LANES), 1)
+    length = per_tile([length_ref[b].astype(F32) for b in range(TILES)])
+    fixed_ref[LIVE : LIVE + TILES, :] = jnp.where(place.astype(F32) < length, 1.0, 0.0)
     for c in range(3):
-        fixed_ref[BACK + c * 8 : BACK + c * 8 + 8, :] = jnp.full((8, LANES), scalar_ref[8 + c], F32)
-    fixed_ref[HERE : HERE + 8, :] = jnp.full((8, LANES), depth, F32)
+        fixed_ref[BACK + c * 8 : BACK + c * 8 + 8, :] = jnp.full((8, LANES), back_ref[c], F32)
+    fixed_ref[HERE : HERE + 8, :] = jnp.full((8, LANES), depth_ref[0].astype(F32), F32)
     for c in range(3):
         for s in range(8):
             fixed_ref[pl.ds(GOAL + c * TILES * 8 + s, TILES, stride=8), :] = target_ref[
@@ -149,7 +159,8 @@
     fixed_ref[OWNER : OWNER + 16, :] = list_ref[...].astype(F32)
 
 
-def table_kernel(side_ref, mine_ref, theirs_ref, table_ref):
+def table_kernel(side_ref, mine_ref, theirs_ref, loose_ref, table_ref, fixed_ref):
+    fixed_ref[...] = loose_ref[...]
     first = side_ref[0] == 0
     blank = jnp.zeros((16 - PARAMS, LANES), F32)
     for a in range(BLOCKS):
@@ -540,18 +551,35 @@
         request_kernel,
         results,
         [HBM] * 6,
-        [pltpu.VMEM(a.shape, a.dtype) for a in sources]
-        + [pltpu.VMEM(*result) for result in results]
-        + [pltpu.SemaphoreType.DMA((9,))],
+        [pltpu.VMEM(a.shape, a.dtype) for a in sources] + [pltpu.SemaphoreType.DMA((6,))],
         GRANT_ALL,
-        [HBM] * 3,
     )(*sources)
     asked = exchanged_in_plane(request.reshape(plane, 1, LANES)).reshape(plane, LANES)
     theirs = lax.ppermute(params, (TILE[2], DEPTH[0]), [(0, 3), (3, 0), (1, 2), (2, 1)])
+    depth = lax.axis_index(DEPTH).astype(I32).reshape(1)
+    loose = (
+        tile_view,
+        tile_length,
+        cameras,
+        background,
+        target.transpose(1, 0, 2),
+        listing,
+    )
+    (fixed,) = call(
+        fixed_kernel,
+        [((FIXED, LANES), F32)],
+        [SMEM] + [HBM] * 6,
+        [pltpu.SMEM(a.shape, a.dtype) for a in loose[:4]]
+        + [pltpu.VMEM(a.shape, a.dtype) for a in loose[4:]]
+        + [pltpu.SemaphoreType.DMA((6,))],
+        GRANT_ALL,
+    )(depth, *loose)
     side = lax.axis_index(TILE[2]).astype(I32).reshape(1)
-    (table,) = call(
-        table_kernel, [((2 * BLOCKS * 16, 3 * LANES), BF16)], [SMEM, VMEM, VMEM]
-    )(side, params, theirs)
+    table, fixed = call(
+        table_kernel,
+        [((2 * BLOCKS * 16, 3 * LANES), BF16), ((FIXED, LANES), F32)],
+        [SMEM, VMEM, VMEM, VMEM],
+    )(side, params, theirs, fixed)
     (reply,) = call(
         reply_kernel,
         [((plane, 2, LANES), F32)],
@@ -559,13 +587,6 @@
         [pltpu.VMEM((LANES, plane), I32), held],
     )(asked, table)
     fetched = exchanged_in_plane(reply).reshape(square)
-    depth = lax.axis_index(DEPTH).astype(F32).reshape(1)
-    scalars = jnp.concatenate(
-        [tile_view.astype(F32), tile_length.astype(F32), background, depth, cameras.reshape(-1)]
-    )
-    (fixed,) = call(fixed_kernel, [((FIXED, LANES), F32)], [SMEM, VMEM, VMEM])(
-        scalars, target.transpose(1, 0, 2), listing
-    )
     field = (TILES * SLAB, 8, LANES)
     tilted = (8 * PITCH, LANES)
     slab, alpha, weight, shade, entry = call(

time: 95 us -> 92.7 us (0.976)
  blocking collectives: 34.7 us -> 48.9 us
  waiting for transfers between devices: 16 us -> 7.35 us
  starting transfers between devices: 26.2 us -> 21.5 us
  local copies, waits for them, and re-layouts: 3.89 us -> 1.78 us
  other arithmetic: 1.32 us -> 0 us
    all_to_all x0 -> x1, blocking collectives: none -> 15.7 us  [exchanged_in_plane(): return lax.all_to_all(array, TILE[:2], 0, 0, tiled=True)]
    all_to_all x2 -> x1, waiting for transfers between devices: 16 us -> 7.34 us  [exchanged_in_plane(): return lax.all_to_all(array, TILE[:2], 0, 0, tiled=True)]
    all_to_all x2 -> x1, starting transfers between devices: 20.9 us -> 16.3 us  [exchanged_in_plane(): return lax.all_to_all(array, TILE[:2], 0, 0, tiled=True)]
    convert_element_type x2 -> x0, other arithmetic: 1.32 us -> none  [the longest x1 0.66 us: body(): tile_view.astype(F32)]
    pallas_call x2, Pallas kernels: 0.65 us -> 1.62 us  [the longest x1 1.53 us: body(): call(fixed_kernel, [((FIXED, LANES), F32)], [SMEM] + [HBM] * 6, [pltpu.SM...]
    unnamed x12 -> x10, local copies, waits for them, and re-layouts: 2.39 us -> 1.78 us
  transfers between devices with their start and end apart: 3 -> 2, of which waited for: 2 -> 1; matrix products, arithmetic and copies ran while one was open for 3% -> 0% of each run, Pallas kernels for 1% -> 2%
where the time goes in v7:
time: 92.7 us; the launch traced here: 92.2 us
  blocking collectives  48.9 us (53%)
  starting transfers between devices  21.5 us (23%)
  Pallas kernels  11.9 us (13%)
  waiting for transfers between devices  7.35 us (8%)
  local copies, waits for them, and re-layouts  1.78 us (2%)
    all_to_all x1, blocking collectives, exchanged(): lax.all_to_all(array.reshape(LANES, 1, LANES), (*TILE, DEPTH[0]), 0, 0, a...  17.6 us
    all_to_all x1, starting transfers between devices, exchanged_in_plane(): return lax.all_to_all(array, TILE[:2], 0, 0, tiled=True)  16.3 us
    all_to_all x1, blocking collectives, exchanged_in_plane(): return lax.all_to_all(array, TILE[:2], 0, 0, tiled=True)  15.7 us
    all_gather x1, blocking collectives, body(): slabs = lax.all_gather(slab[None], DEPTH, axis=0, tiled=True)  8.58 us
    all_to_all x1, waiting for transfers between devices, exchanged_in_plane(): return lax.all_to_all(array, TILE[:2], 0, 0, tiled=True)  7.34 us
    all_gather x1, blocking collectives, body(): sums = lax.all_gather(sums[None], DEPTH, axis=0, tiled=True)  7.12 us
    ppermute x1, starting transfers between devices, body(): lax.ppermute(params, (TILE[2], DEPTH[0]), [(0, 3), (3, 0), (1, 2), (2, 1)])  5.22 us
    pallas_call x1, Pallas kernels, body(): call(backward_kernel, [((3, TILES, 1024), F32), (square, F32)], [VMEM] *...  2.87 us
  transfers between devices with their start and end apart: 2, of which 1 were waited for; matrix products, arithmetic and copies ran while one was open for 0% of the time, Pallas kernels for 2%

profile of v7, /device:TPU:1, one launch (start us, length us, event | category | flops | bytes accessed | tf_op | source)
XLA Modules:
  0.0 92.2 jit_solution(1361934964088334750)
XLA Ops:
  0.6 2.2 %shard_map.156 = (s32[64,128]{1,0:T(8,128)}, s32[16,128]{1,0:T(8,128)}, f32[160,128]{1,0:T(8,128)}) custom-call(s32[4,128]{1,0:T(4,128)} %bitcast.25, s32[4,128]{1,0:T(4,128)} %bitcast.26, f32[3,2048]{1,0:T(4,128)} %position_hbm.1, f32[3,2048]{1,0:T(4,128)} %scale_hbm.1, f32[1,2048]{1,0:T(1,128)} %opacity_hbm.1, f32[3,2048]{1,0:T(4,128)} %color_hbm.1), custom_call_target="tpu_custom_call" | custom-call | tf_op jit(solution)/shard_map/pallas_call | solution.py:550
  2.8 5.2 %collective-permute-start = (f32[160,128]{1,0:T(8,128)}, f32[160,128]{1,0:T(8,128)S(1)}, u32[]{:S(2)}, u32[]{:S(2)}) collective-permute-start(f32[160,128]{1,0:T(8,128)} %get-tuple-element.20.mine_ref.params_ref), channel_id=1, source_target_pairs={{0,6},{6,0},{2,4},{4,2},{1,7},{7,1},{3,5},{5,3},{8,14},{14,8},{10,... | collective-permute-start | bytes 245768 | tf_op jit(solution)/shard_map/ppermute | solution.py:558
  8.0 16.3 %all-to-all-start = ((s32[64,1,128]{2,1,0:T(1,128)}), s32[64,1,128]{2,1,0:T(1,128)S(1)}, u32[]{:S(2)}, u32[]{:S(2)}) async-start(s32[64,1,128]{2,1,0:T(1,128)} %bitcast.24), calls=%async_computation | async-start | bytes 65536 | tf_op jit(solution)/shard_map/all_to_all | solution.py:503
  24.4 1.5 %shard_map.157.loose_ref = f32[184,128]{1,0:T(8,128)} custom-call(s32[1]{0:T(128)} %bitcast.6.depth_ref, s32[4]{0:T(128)} %view_hbm.1, s32[4]{0:T(128)} %length_hbm.1, f32[4,2,4]{2,1,0:T(2,128)} %cams_hbm.1, f32[3]{0:T(128)} %back_hbm.1, f32[3,4,1024]{2,1,0:T(4,128)} %bitcast.23, s32[16,128]{1,0:T(8,128)} %get-tuple-element.21.list_hbm), custom_call_target="tpu_custom_call" | custom-call | tf_op jit(solution)/shard_map/pallas_call | solution.py:568
  25.9 0.0 collective-permute-done.theirs_ref
  25.9 0.0 copy-start
  25.9 0.9 copy-done
  26.8 0.0 copy-start.1
  26.8 0.9 copy-done.1
  27.7 0.1 shard_map.158
  27.8 7.3 %all-to-all-done = s32[64,1,128]{2,1,0:T(1,128)S(1)} async-done(((s32[64,1,128]{2,1,0:T(1,128)}), s32[64,1,128]{2,1,0:T(1,128)S(1)}, u32[]{:S(2)}, u32[]{:S(2)}) %all-to-all-start) | async-done | bytes 32800 | tf_op jit(solution)/shard_map/all_to_all | solution.py:503
  35.1 1.0 %shard_map.159 = f32[64,2,128]{2,1,0:T(2,128)S(1)} custom-call(s32[64,128]{1,0:T(8,128)S(1)} %bitcast.21, bf16[512,384]{1,0:T(8,128)(2,1)S(1)} %get-tuple-element.22.table_ref), custom_call_target="tpu_custom_call" | custom-call | tf_op jit(solution)/shard_map/pallas_call | solution.py:583
  36.1 15.7 %all_to_all.15 = f32[64,2,128]{2,1,0:T(2,128)S(1)} all-to-all(f32[64,2,128]{2,1,0:T(2,128)S(1)} %shard_map.159), channel_id=1, replica_groups=mesh['tile_z'=8,'tile_y'=8,'tile_x'=2,'depth_x'=2,'depth_core'=2] {'tile..., dimensions={0} | all-to-all | bytes 131072 | tf_op jit(solution)/shard_map/all_to_all | solution.py:503
  51.8 2.6 %shard_map.160 = (f32[128,128]{1,0:T(8,128)S(1)}, f32[512,8,128]{2,1,0:T(8,128)S(1)}, f32[4104,128]{1,0:T(8,128)S(1)}, f32[3,520,128]{2,1,0:T(8,128)S(1)}, f32[64,128]{1,0:T(8,128)S(1)}) custom-call(f32[128,128]{1,0:T(8,128)S(1)} %bitcast.19, f32[184,128]{1,0:T(8,128)S(1)} %get-tuple-element.23.fixed_ref), custom_call_target="tpu_custom_call" | custom-call | tf_op jit(solution)/shard_map/pallas_call | solution.py:592
  54.4 8.6 %all-gather = f32[512,128]{1,0:T(8,128)S(1)} all-gather(f32[128,128]{1,0:T(8,128)S(1)} %get-tuple-element.24), channel_id=2, replica_groups=mesh['tile_z'=8,'tile_y'=8,'tile_x'=2,'depth_x'=2,'depth_core'=2] {'dept..., dimensions={0}, use_global_device_ids=true | all-gather | bytes 327680 | tf_op jit(solution)/shard_map/all_gather | solution.py:604
  63.0 0.0 copy-start.2
  63.0 0.0 copy-start.3
  63.0 0.0 copy-start.4
  63.0 2.9 %shard_map.161 = (f32[3,4,1024]{2,1,0:T(4,128)}, f32[128,128]{1,0:T(8,128)S(1)}) custom-call(f32[4,128,128]{2,1,0:T(8,128)S(1)} %bitcast.18, f32[512,8,128]{2,1,0:T(8,128)S(1)} %get-tuple-element.25.alpha_ref, f32[4104,128]{1,0:T(8,128)S(1)} %get-tuple-element.26.weight_ref, f32[3,520,128]{2,1,0:T(8,128)S(1)} %get-tuple-element.27.shade_ref, ...), custom_call_target="tpu_custom_call" | custom-call | tf_op jit(solution)/shard_map/pallas_call | solution.py:605
  65.9 17.6 %all_to_all.16 = f32[128,1,128]{2,1,0:T(1,128)S(1)} all-to-all(f32[128,1,128]{2,1,0:T(1,128)S(1)} %bitcast.22), channel_id=1, replica_groups={{0,6,8,14,16,22,24,30,32,38,40,46,48,54,56,62,64,70,72,78,80,86,88,94,9..., dimensions={0} | all-to-all | bytes 131072 | tf_op jit(solution)/shard_map/all_to_all | solution.py:510
  83.4 0.8 shard_map.162
  84.2 7.1 %all-gather.1 = f32[640,128]{1,0:T(8,128)S(1)} all-gather(f32[160,128]{1,0:T(8,128)S(1)} %shard_map.162), channel_id=3, replica_groups=mesh['tile_z'=8,'tile_y'=8,'tile_x'=2,'depth_x'=2,'depth_core'=2] {'dept..., dimensions={0}, use_global_device_ids=true | all-gather | bytes 409600 | tf_op jit(solution)/shard_map/all_gather | solution.py:627
  91.4 0.0 copy-done.2
  91.4 0.0 copy-done.3
  91.4 0.0 copy-done.4
  91.4 0.8 shard_map.163
Async XLA Ops:
  2.8 23.1 %collective-permute-start = (f32[160,128]{1,0:T(8,128)}, f32[160,128]{1,0:T(8,128)S(1)}, u32[]{:S(2)}, u32[]{:S(2)}) collective-permute-start(f32[160,128]{1,0:T(8,128)} %get-tuple-element.20.mine_ref.params_ref), channel_id=1, source_target_pairs={{0,6},{6,0},{2,4},{4,2},{1,7},{7,1},{3,5},{5,3},{8,14},{14,8},{10,... | collective-permute-start | bytes 245768 | tf_op jit(solution)/shard_map/ppermute | solution.py:558
  8.0 27.1 %all-to-all-start = ((s32[64,1,128]{2,1,0:T(1,128)}), s32[64,1,128]{2,1,0:T(1,128)S(1)}, u32[]{:S(2)}, u32[]{:S(2)}) async-start(s32[64,1,128]{2,1,0:T(1,128)} %bitcast.24), calls=%async_computation | async-start | bytes 65536 | tf_op jit(solution)/shard_map/all_to_all | solution.py:503
  25.9 0.9 copy-start
  26.8 0.9 copy-start.1
  63.0 28.4 %copy-start.2 = (f32[160,128]{1,0:T(8,128)S(1)}, f32[160,128]{1,0:T(8,128)}, u32[]{:S(2)}) copy-start(f32[160,128]{1,0:T(8,128)} %get-tuple-element.20.mine_ref.params_ref) | copy-start | bytes 245764
  63.0 28.4 %copy-start.3 = (f32[10,2048]{1,0:T(8,128)S(1)}, f32[10,2048]{1,0:T(8,128)}, u32[]{:S(2)}) copy-start(f32[10,2048]{1,0:T(8,128)} %first_ref.1) | copy-start | bytes 245764
  63.0 28.4 %copy-start.4 = (f32[10,2048]{1,0:T(8,128)S(1)}, f32[10,2048]{1,0:T(8,128)}, u32[]{:S(2)}) copy-start(f32[10,2048]{1,0:T(8,128)} %second_ref.1) | copy-start | bytes 245764

commit v8 on v7

--- a/solution.py
+++ b/solution.py
@@ -159,8 +159,18 @@
     fixed_ref[OWNER : OWNER + 16, :] = list_ref[...].astype(F32)
 
 
-def table_kernel(side_ref, mine_ref, theirs_ref, loose_ref, table_ref, fixed_ref):
+def monomials(shape, rows):
+    index, pixel = iota(shape, 0), iota(shape, 1)
+    x, y = (pixel & 31) - 16, (pixel >> 5) - 16
+    out = jnp.zeros(shape, I32)
+    for k in range(3 * rows):
+        out = jnp.where(index == k, (1, x, y, x * x, x * y, y * y)[k % rows], out)
+    return out.astype(F32).astype(BF16)
+
+
+def table_kernel(side_ref, mine_ref, theirs_ref, loose_ref, table_ref, fixed_ref, powers_ref):
     fixed_ref[...] = loose_ref[...]
+    powers_ref[...] = monomials((32, 1024), 6)
     first = side_ref[0] == 0
     blank = jnp.zeros((16 - PARAMS, LANES), F32)
     for a in range(BLOCKS):
@@ -221,6 +231,7 @@
 def forward_kernel(
     fetched_ref,
     fixed_ref,
+    powers_ref,
     slab_ref,
     alpha_ref,
     weight_ref,
@@ -228,7 +239,6 @@
     entry_ref,
     found,
     rows,
-    spread,
 ):
     fetched = side_by_side(fetched_ref[...].T)
     for b in range(TILES):
@@ -241,53 +251,55 @@
         entry_ref[b * 16 : (b + 1) * 16, :] = value
     entry = [entry_ref[pl.ds(p, TILES, stride=16), :] for p in range(PARAMS)]
     jac = camera_rows(fixed_ref)
-    center_x = sum(jac[0][j] * entry[j] for j in range(3)) + jac[0][3] + 16.0
-    center_y = sum(jac[1][j] * entry[j] for j in range(3)) + jac[1][3] + 16.0
+    cx = sum(jac[0][j] * entry[j] for j in range(3)) + jac[0][3] - 0.5
+    cy = sum(jac[1][j] * entry[j] for j in range(3)) + jac[1][3] - 0.5
     _, xx, xy, yy, det = covariance(entry[3:6], jac)
-    opacity = jax.nn.sigmoid(entry[6]) * fixed_ref[LIVE : LIVE + TILES, :]
+    qa = (-0.5 * LOG2E) * (yy / det)
+    qb = LOG2E * (xy / det)
+    qc = (-0.5 * LOG2E) * (xx / det)
+    live = fixed_ref[LIVE : LIVE + TILES, :]
+    height = LOG2E * jnp.log(jax.nn.sigmoid(entry[6])) - 1e5 * (1.0 - live)
     factors = [
-        center_x,
-        center_y,
-        (-0.5 * LOG2E) * (yy / det),
-        LOG2E * (xy / det),
-        (-0.5 * LOG2E) * (xx / det),
-        opacity,
-        *entry[7:10],
+        cx * (qa * cx + qb * cy) + qc * cy * cy + height,
+        -(2.0 * qa * cx + qb * cy),
+        -(2.0 * qc * cy + qb * cx),
+        qa,
+        qb,
+        qc,
     ]
-    for p, factor in enumerate(factors):
-        rows[p * TILES : (p + 1) * TILES, :] = factor
-    rows[len(factors) * TILES :, :] = jnp.zeros((LANES - len(factors) * TILES, LANES), F32)
+    rows[...] = jnp.zeros((LANES, LANES), F32)
+    for k, factor in enumerate(factors):
+        for n, piece in enumerate(pieces(factor)):
+            rows[pl.ds(n * 6 + k, TILES, stride=32), :] = piece.astype(F32)
+    for c in range(3):
+        rows[pl.ds(18 + c, TILES, stride=32), :] = entry[7 + c]
     turned = rows[...].T
-    for p in range(9):
-        for b in range(TILES):
-            column = turned[:, p * TILES + b : p * TILES + b + 1]
-            wide = jnp.broadcast_to(column, (SLAB, LANES))
-            if p < 6:
-                spread[p, b * SLAB : (b + 1) * SLAB, :] = wide
-            else:
-                shade_ref[p - 6, b * SLAB : (b + 1) * SLAB, :] = wide
-    lane = iota((8, LANES), 1)
-    pixel_x = (lane & 31).astype(F32) + 0.5
-    pixel_y = (iota((8, LANES), 0) * 4 + (lane >> 5)).astype(F32) + 0.5
+    powers = powers_ref[...]
+    for b in range(TILES):
+        blank = [jnp.zeros((32, 1024), BF16)] * TILES
+        blank[b] = powers
+        alpha = jnp.exp2(dot(turned.astype(BF16), jnp.concatenate(blank, axis=0), NN))
+        for s in range(8):
+            at = s * PITCH + b * SLAB
+            alpha_ref[at : at + SLAB, :] = alpha[:, s * LANES : (s + 1) * LANES]
+        for c in range(3):
+            column = turned[:, b * 32 + 18 + c : b * 32 + 19 + c]
+            shade_ref[c, b * SLAB : (b + 1) * SLAB, :] = jnp.broadcast_to(column, (SLAB, LANES))
 
     def step(k, carry):
         out = []
         for b in range(TILES):
             trans, red, green, blue = carry[4 * b : 4 * b + 4]
             at = b * SLAB + k
-            get = lambda ref, p: ref[p, pl.ds(at, 8, stride=0), :]
-            ex = pixel_x - get(spread, 0)
-            ey = pixel_y - get(spread, 1)
-            power = ex * (get(spread, 2) * ex + get(spread, 3) * ey) + get(spread, 4) * ey * ey
-            alpha = get(spread, 5) * jnp.exp2(power)
-            weight = alpha * trans
-            alpha_ref[at] = alpha
-            weight_ref[pl.ds(at, 8, stride=PITCH), :] = weight
+            spots = pl.ds(at, 8, stride=PITCH)
+            get = lambda p: shade_ref[p, pl.ds(at, 8, stride=0), :]
+            weight = alpha_ref[spots, :] * trans
+            weight_ref[spots, :] = weight
             out += [
                 trans - weight,
-                red + weight * get(shade_ref, 0),
-                green + weight * get(shade_ref, 1),
-                blue + weight * get(shade_ref, 2),
+                red + weight * get(0),
+                green + weight * get(1),
+                blue + weight * get(2),
             ]
         return tuple(out)
 
@@ -367,7 +379,7 @@
             gap = shade - carry[b]
             rows = pl.ds(at, 8, stride=PITCH)
             slope[rows, :] = weight_ref[rows, :] * gap
-            out.append(carry[b] + alpha_ref[at] * gap)
+            out.append(carry[b] + alpha_ref[rows, :] * gap)
         return tuple(out)
 
     lax.fori_loop(0, SLAB, step, tuple(behind), unroll=8)
@@ -575,9 +587,9 @@
         GRANT_ALL,
     )(depth, *loose)
     side = lax.axis_index(TILE[2]).astype(I32).reshape(1)
-    table, fixed = call(
+    table, fixed, powers = call(
         table_kernel,
-        [((2 * BLOCKS * 16, 3 * LANES), BF16), ((FIXED, LANES), F32)],
+        [((2 * BLOCKS * 16, 3 * LANES), BF16), ((FIXED, LANES), F32), ((32, 1024), BF16)],
         [SMEM, VMEM, VMEM, VMEM],
     )(side, params, theirs, fixed)
     (reply,) = call(
@@ -587,20 +599,19 @@
         [pltpu.VMEM((LANES, plane), I32), held],
     )(asked, table)
     fetched = exchanged_in_plane(reply).reshape(square)
-    field = (TILES * SLAB, 8, LANES)
     tilted = (8 * PITCH, LANES)
     slab, alpha, weight, shade, entry = call(
         forward_kernel,
         [
             (square, F32),
-            (field, F32),
+            (tilted, F32),
             (tilted, F32),
             ((3, TILES * SLAB + 8, LANES), F32),
             ((TILES * 16, LANES), F32),
         ],
-        [VMEM] * 2,
-        [held, held, pltpu.VMEM((6, TILES * SLAB + 8, LANES), F32)],
-    )(fetched, fixed)
+        [VMEM] * 3,
+        [held, held],
+    )(fetched, fixed, powers)
     slabs = lax.all_gather(slab[None], DEPTH, axis=0, tiled=True)
     image, outgoing = call(
         backward_kernel,

time: 92.7 us -> 91.6 us (0.988)
  Pallas kernels: 11.9 us -> 10.8 us
    pallas_call x1, Pallas kernels: 2.62 us -> 1.62 us  [body(): call(forward_kernel, [(square, F32), (tilted, F32), (tilted, F32), ((3, T...]
where the time goes in v8:
time: 91.6 us; the launch traced here: 91.2 us
  blocking collectives  49 us (53%)
  starting transfers between devices  21.5 us (23%)
  Pallas kernels  10.8 us (12%)
  waiting for transfers between devices  7.31 us (8%)
  local copies, waits for them, and re-layouts  1.78 us (2%)
    all_to_all x1, blocking collectives, exchanged(): lax.all_to_all(array.reshape(LANES, 1, LANES), (*TILE, DEPTH[0]), 0, 0, a...  17.6 us
    all_to_all x1, starting transfers between devices, exchanged_in_plane(): return lax.all_to_all(array, TILE[:2], 0, 0, tiled=True)  16.3 us
    all_to_all x1, blocking collectives, exchanged_in_plane(): return lax.all_to_all(array, TILE[:2], 0, 0, tiled=True)  15.7 us
    all_gather x1, blocking collectives, body(): slabs = lax.all_gather(slab[None], DEPTH, axis=0, tiled=True)  8.57 us
    all_to_all x1, waiting for transfers between devices, exchanged_in_plane(): return lax.all_to_all(array, TILE[:2], 0, 0, tiled=True)  7.31 us
    all_gather x1, blocking collectives, body(): sums = lax.all_gather(sums[None], DEPTH, axis=0, tiled=True)  7.12 us
    ppermute x1, starting transfers between devices, body(): lax.ppermute(params, (TILE[2], DEPTH[0]), [(0, 3), (3, 0), (1, 2), (2, 1)])  5.22 us
    pallas_call x1, Pallas kernels, body(): call(backward_kernel, [((3, TILES, 1024), F32), (square, F32)], [VMEM] *...  2.8 us
  transfers between devices with their start and end apart: 2, of which 1 were waited for; matrix products, arithmetic and copies ran while one was open for 0% of the time, Pallas kernels for 2%

profile of v8, /device:TPU:1, one launch (start us, length us, event | category | flops | bytes accessed | tf_op | source)
XLA Modules:
  0.0 91.2 jit_solution(12867697455368496461)
XLA Ops:
  0.6 2.2 %shard_map.156 = (s32[64,128]{1,0:T(8,128)}, s32[16,128]{1,0:T(8,128)}, f32[160,128]{1,0:T(8,128)}) custom-call(s32[4,128]{1,0:T(4,128)} %bitcast.25, s32[4,128]{1,0:T(4,128)} %bitcast.26, f32[3,2048]{1,0:T(4,128)} %position_hbm.1, f32[3,2048]{1,0:T(4,128)} %scale_hbm.1, f32[1,2048]{1,0:T(1,128)} %opacity_hbm.1, f32[3,2048]{1,0:T(4,128)} %color_hbm.1), custom_call_target="tpu_custom_call" | custom-call | tf_op jit(solution)/shard_map/pallas_call | solution.py:562
  2.8 5.2 %collective-permute-start = (f32[160,128]{1,0:T(8,128)}, f32[160,128]{1,0:T(8,128)S(1)}, u32[]{:S(2)}, u32[]{:S(2)}) collective-permute-start(f32[160,128]{1,0:T(8,128)} %get-tuple-element.21.mine_ref.params_ref), channel_id=1, source_target_pairs={{0,6},{6,0},{2,4},{4,2},{1,7},{7,1},{3,5},{5,3},{8,14},{14,8},{10,... | collective-permute-start | bytes 245768 | tf_op jit(solution)/shard_map/ppermute | solution.py:570
  8.0 16.3 %all-to-all-start = ((s32[64,1,128]{2,1,0:T(1,128)}), s32[64,1,128]{2,1,0:T(1,128)S(1)}, u32[]{:S(2)}, u32[]{:S(2)}) async-start(s32[64,1,128]{2,1,0:T(1,128)} %bitcast.24), calls=%async_computation | async-start | bytes 65536 | tf_op jit(solution)/shard_map/all_to_all | solution.py:515
  24.4 1.5 %shard_map.157.loose_ref = f32[184,128]{1,0:T(8,128)} custom-call(s32[1]{0:T(128)} %bitcast.6.depth_ref, s32[4]{0:T(128)} %view_hbm.1, s32[4]{0:T(128)} %length_hbm.1, f32[4,2,4]{2,1,0:T(2,128)} %cams_hbm.1, f32[3]{0:T(128)} %back_hbm.1, f32[3,4,1024]{2,1,0:T(4,128)} %bitcast.23, s32[16,128]{1,0:T(8,128)} %get-tuple-element.22.list_hbm), custom_call_target="tpu_custom_call" | custom-call | tf_op jit(solution)/shard_map/pallas_call | solution.py:580
  25.9 0.0 collective-permute-done.theirs_ref
  25.9 0.0 copy-start
  25.9 0.9 copy-done
  26.8 0.0 copy-start.1
  26.8 0.9 copy-done.1
  27.7 0.1 shard_map.158
  27.8 7.3 %all-to-all-done = s32[64,1,128]{2,1,0:T(1,128)S(1)} async-done(((s32[64,1,128]{2,1,0:T(1,128)}), s32[64,1,128]{2,1,0:T(1,128)S(1)}, u32[]{:S(2)}, u32[]{:S(2)}) %all-to-all-start) | async-done | bytes 32800 | tf_op jit(solution)/shard_map/all_to_all | solution.py:515
  35.1 1.0 %shard_map.159 = f32[64,2,128]{2,1,0:T(2,128)S(1)} custom-call(s32[64,128]{1,0:T(8,128)S(1)} %bitcast.21, bf16[512,384]{1,0:T(8,128)(2,1)S(1)} %get-tuple-element.23.table_ref), custom_call_target="tpu_custom_call" | custom-call | tf_op jit(solution)/shard_map/pallas_call | solution.py:595
  36.1 15.7 %all_to_all.15 = f32[64,2,128]{2,1,0:T(2,128)S(1)} all-to-all(f32[64,2,128]{2,1,0:T(2,128)S(1)} %shard_map.159), channel_id=1, replica_groups=mesh['tile_z'=8,'tile_y'=8,'tile_x'=2,'depth_x'=2,'depth_core'=2] {'tile..., dimensions={0} | all-to-all | bytes 131072 | tf_op jit(solution)/shard_map/all_to_all | solution.py:515
  51.8 1.6 %shard_map.160 = (f32[128,128]{1,0:T(8,128)S(1)}, f32[4104,128]{1,0:T(8,128)S(1)}, f32[4104,128]{1,0:T(8,128)S(1)}, f32[3,520,128]{2,1,0:T(8,128)S(1)}, f32[64,128]{1,0:T(8,128)S(1)}) custom-call(f32[128,128]{1,0:T(8,128)S(1)} %bitcast.19, f32[184,128]{1,0:T(8,128)S(1)} %get-tuple-element.24.fixed_ref, bf16[32,1024]{1,0:T(8,128)(2,1)S(1)} %get-tuple-element.25.powers_ref), custom_call_target="tpu_custom_call" | custom-call | tf_op jit(solution)/shard_map/pallas_call | solution.py:603
  53.5 8.6 %all-gather = f32[512,128]{1,0:T(8,128)S(1)} all-gather(f32[128,128]{1,0:T(8,128)S(1)} %get-tuple-element.26), channel_id=2, replica_groups=mesh['tile_z'=8,'tile_y'=8,'tile_x'=2,'depth_x'=2,'depth_core'=2] {'dept..., dimensions={0}, use_global_device_ids=true | all-gather | bytes 327680 | tf_op jit(solution)/shard_map/all_gather | solution.py:615
  62.0 0.0 copy-start.2
  62.0 0.0 copy-start.3
  62.0 0.0 copy-start.4
  62.0 2.8 %shard_map.161 = (f32[3,4,1024]{2,1,0:T(4,128)}, f32[128,128]{1,0:T(8,128)S(1)}) custom-call(f32[4,128,128]{2,1,0:T(8,128)S(1)} %bitcast.18, f32[4104,128]{1,0:T(8,128)S(1)} %get-tuple-element.27.alpha_ref, f32[4104,128]{1,0:T(8,128)S(1)} %get-tuple-element.28.weight_ref, f32[3,520,128]{2,1,0:T(8,128)S(1)} %get-tuple-element.29.shade_ref, ...), custom_call_target="tpu_custom_call" | custom-call | tf_op jit(solution)/shard_map/pallas_call | solution.py:616
  64.8 17.6 %all_to_all.16 = f32[128,1,128]{2,1,0:T(1,128)S(1)} all-to-all(f32[128,1,128]{2,1,0:T(1,128)S(1)} %bitcast.22), channel_id=1, replica_groups={{0,6,8,14,16,22,24,30,32,38,40,46,48,54,56,62,64,70,72,78,80,86,88,94,9..., dimensions={0} | all-to-all | bytes 131072 | tf_op jit(solution)/shard_map/all_to_all | solution.py:522
  82.4 0.8 shard_map.162
  83.2 7.1 %all-gather.1 = f32[640,128]{1,0:T(8,128)S(1)} all-gather(f32[160,128]{1,0:T(8,128)S(1)} %shard_map.162), channel_id=3, replica_groups=mesh['tile_z'=8,'tile_y'=8,'tile_x'=2,'depth_x'=2,'depth_core'=2] {'dept..., dimensions={0}, use_global_device_ids=true | all-gather | bytes 409600 | tf_op jit(solution)/shard_map/all_gather | solution.py:638
  90.3 0.0 copy-done.2
  90.3 0.0 copy-done.3
  90.3 0.0 copy-done.4
  90.3 0.8 shard_map.163
Async XLA Ops:
  2.8 23.1 %collective-permute-start = (f32[160,128]{1,0:T(8,128)}, f32[160,128]{1,0:T(8,128)S(1)}, u32[]{:S(2)}, u32[]{:S(2)}) collective-permute-start(f32[160,128]{1,0:T(8,128)} %get-tuple-element.21.mine_ref.params_ref), channel_id=1, source_target_pairs={{0,6},{6,0},{2,4},{4,2},{1,7},{7,1},{3,5},{5,3},{8,14},{14,8},{10,... | collective-permute-start | bytes 245768 | tf_op jit(solution)/shard_map/ppermute | solution.py:570
  8.0 27.1 %all-to-all-start = ((s32[64,1,128]{2,1,0:T(1,128)}), s32[64,1,128]{2,1,0:T(1,128)S(1)}, u32[]{:S(2)}, u32[]{:S(2)}) async-start(s32[64,1,128]{2,1,0:T(1,128)} %bitcast.24), calls=%async_computation | async-start | bytes 65536 | tf_op jit(solution)/shard_map/all_to_all | solution.py:515
  25.9 0.9 copy-start
  26.8 0.9 copy-start.1
  62.0 28.3 %copy-start.2 = (f32[160,128]{1,0:T(8,128)S(1)}, f32[160,128]{1,0:T(8,128)}, u32[]{:S(2)}) copy-start(f32[160,128]{1,0:T(8,128)} %get-tuple-element.21.mine_ref.params_ref) | copy-start | bytes 245764
  62.0 28.3 %copy-start.3 = (f32[10,2048]{1,0:T(8,128)S(1)}, f32[10,2048]{1,0:T(8,128)}, u32[]{:S(2)}) copy-start(f32[10,2048]{1,0:T(8,128)} %first_ref.1) | copy-start | bytes 245764
  62.0 28.3 %copy-start.4 = (f32[10,2048]{1,0:T(8,128)S(1)}, f32[10,2048]{1,0:T(8,128)}, u32[]{:S(2)}) copy-start(f32[10,2048]{1,0:T(8,128)} %second_ref.1) | copy-start | bytes 245764

commit v9 on v8

--- a/solution.py
+++ b/solution.py
@@ -46,6 +46,10 @@
 
 def side_by_side(x):
     return jnp.concatenate(pieces(x), axis=1)
+
+
+def two_side_by_side(x):
+    return jnp.concatenate(pieces(x)[:2], axis=1)
 
 
 def dot(a, b, dims):
@@ -464,8 +468,8 @@
         row = jnp.where(here, fixed_ref[ROW + b : ROW + b + 1, :], 0.0)
         placed[SLOTS * PARAMS : SLOTS * PARAMS + 16, :] = row
         named = onehot(listed(fixed_ref, OWNER, b), LANES).astype(BF16)
-        named = jnp.concatenate([named, named, named], axis=1)
-        outgoing = outgoing + dot(named, side_by_side(placed[...]), NT)
+        named = jnp.concatenate([named, named], axis=1)
+        outgoing = outgoing + dot(named, two_side_by_side(placed[...]), NT)
     outgoing_ref[...] = outgoing
     shown.wait()
 
@@ -482,7 +486,7 @@
             [jnp.where(block == a, value, 0.0) for a in range(BLOCKS)], axis=0
         )
         total = total + dot(
-            side_by_side(spread), jnp.concatenate([pick, pick, pick], axis=1), NT
+            two_side_by_side(spread), jnp.concatenate([pick, pick], axis=1), NT
         )
     for a in range(BLOCKS):
         sums_ref[a * PARAMS : (a + 1) * PARAMS, :] = total[a * 16 : a * 16 + PARAMS]

time: 91.6 us -> 91.3 us (level)
  no operation moved by 1% of the time
where the time goes in v9:
time: 91.3 us; the launch traced here: 90.8 us
  blocking collectives  49 us (54%)
  starting transfers between devices  21.5 us (24%)
  Pallas kernels  10.5 us (12%)
  waiting for transfers between devices  7.31 us (8%)
  local copies, waits for them, and re-layouts  1.78 us (2%)
    all_to_all x1, blocking collectives, exchanged(): lax.all_to_all(array.reshape(LANES, 1, LANES), (*TILE, DEPTH[0]), 0, 0, a...  17.6 us
    all_to_all x1, starting transfers between devices, exchanged_in_plane(): return lax.all_to_all(array, TILE[:2], 0, 0, tiled=True)  16.3 us
    all_to_all x1, blocking collectives, exchanged_in_plane(): return lax.all_to_all(array, TILE[:2], 0, 0, tiled=True)  15.7 us
    all_gather x1, blocking collectives, body(): slabs = lax.all_gather(slab[None], DEPTH, axis=0, tiled=True)  8.57 us
    all_to_all x1, waiting for transfers between devices, exchanged_in_plane(): return lax.all_to_all(array, TILE[:2], 0, 0, tiled=True)  7.31 us
    all_gather x1, blocking collectives, body(): sums = lax.all_gather(sums[None], DEPTH, axis=0, tiled=True)  7.12 us
    ppermute x1, starting transfers between devices, body(): lax.ppermute(params, (TILE[2], DEPTH[0]), [(0, 3), (3, 0), (1, 2), (2, 1)])  5.22 us
    pallas_call x1, Pallas kernels, body(): call(backward_kernel, [((3, TILES, 1024), F32), (square, F32)], [VMEM] *...  2.64 us
  transfers between devices with their start and end apart: 2, of which 1 were waited for; matrix products, arithmetic and copies ran while one was open for 0% of the time, Pallas kernels for 2%

profile of v9, /device:TPU:1, one launch (start us, length us, event | category | flops | bytes accessed | tf_op | source)
XLA Modules:
  0.0 90.8 jit_solution(15106126456849798677)
XLA Ops:
  0.6 2.2 %shard_map.156 = (s32[64,128]{1,0:T(8,128)}, s32[16,128]{1,0:T(8,128)}, f32[160,128]{1,0:T(8,128)}) custom-call(s32[4,128]{1,0:T(4,128)} %bitcast.25, s32[4,128]{1,0:T(4,128)} %bitcast.26, f32[3,2048]{1,0:T(4,128)} %position_hbm.1, f32[3,2048]{1,0:T(4,128)} %scale_hbm.1, f32[1,2048]{1,0:T(1,128)} %opacity_hbm.1, f32[3,2048]{1,0:T(4,128)} %color_hbm.1), custom_call_target="tpu_custom_call" | custom-call | tf_op jit(solution)/shard_map/pallas_call | solution.py:566
  2.8 5.2 %collective-permute-start = (f32[160,128]{1,0:T(8,128)}, f32[160,128]{1,0:T(8,128)S(1)}, u32[]{:S(2)}, u32[]{:S(2)}) collective-permute-start(f32[160,128]{1,0:T(8,128)} %get-tuple-element.21.mine_ref.params_ref), channel_id=1, source_target_pairs={{0,6},{6,0},{2,4},{4,2},{1,7},{7,1},{3,5},{5,3},{8,14},{14,8},{10,... | collective-permute-start | bytes 245768 | tf_op jit(solution)/shard_map/ppermute | solution.py:574
  8.0 16.3 %all-to-all-start = ((s32[64,1,128]{2,1,0:T(1,128)}), s32[64,1,128]{2,1,0:T(1,128)S(1)}, u32[]{:S(2)}, u32[]{:S(2)}) async-start(s32[64,1,128]{2,1,0:T(1,128)} %bitcast.24), calls=%async_computation | async-start | bytes 65536 | tf_op jit(solution)/shard_map/all_to_all | solution.py:519
  24.4 1.5 %shard_map.157.loose_ref = f32[184,128]{1,0:T(8,128)} custom-call(s32[1]{0:T(128)} %bitcast.6.depth_ref, s32[4]{0:T(128)} %view_hbm.1, s32[4]{0:T(128)} %length_hbm.1, f32[4,2,4]{2,1,0:T(2,128)} %cams_hbm.1, f32[3]{0:T(128)} %back_hbm.1, f32[3,4,1024]{2,1,0:T(4,128)} %bitcast.23, s32[16,128]{1,0:T(8,128)} %get-tuple-element.22.list_hbm), custom_call_target="tpu_custom_call" | custom-call | tf_op jit(solution)/shard_map/pallas_call | solution.py:584
  25.9 0.0 collective-permute-done.theirs_ref
  25.9 0.0 copy-start
  25.9 0.9 copy-done
  26.8 0.0 copy-start.1
  26.8 0.9 copy-done.1
  27.7 0.1 shard_map.158
  27.8 7.3 %all-to-all-done = s32[64,1,128]{2,1,0:T(1,128)S(1)} async-done(((s32[64,1,128]{2,1,0:T(1,128)}), s32[64,1,128]{2,1,0:T(1,128)S(1)}, u32[]{:S(2)}, u32[]{:S(2)}) %all-to-all-start) | async-done | bytes 32800 | tf_op jit(solution)/shard_map/all_to_all | solution.py:519
  35.1 1.0 %shard_map.159 = f32[64,2,128]{2,1,0:T(2,128)S(1)} custom-call(s32[64,128]{1,0:T(8,128)S(1)} %bitcast.21, bf16[512,384]{1,0:T(8,128)(2,1)S(1)} %get-tuple-element.23.table_ref), custom_call_target="tpu_custom_call" | custom-call | tf_op jit(solution)/shard_map/pallas_call | solution.py:599
  36.1 15.7 %all_to_all.15 = f32[64,2,128]{2,1,0:T(2,128)S(1)} all-to-all(f32[64,2,128]{2,1,0:T(2,128)S(1)} %shard_map.159), channel_id=1, replica_groups=mesh['tile_z'=8,'tile_y'=8,'tile_x'=2,'depth_x'=2,'depth_core'=2] {'tile..., dimensions={0} | all-to-all | bytes 131072 | tf_op jit(solution)/shard_map/all_to_all | solution.py:519
  51.8 1.6 %shard_map.160 = (f32[128,128]{1,0:T(8,128)S(1)}, f32[4104,128]{1,0:T(8,128)S(1)}, f32[4104,128]{1,0:T(8,128)S(1)}, f32[3,520,128]{2,1,0:T(8,128)S(1)}, f32[64,128]{1,0:T(8,128)S(1)}) custom-call(f32[128,128]{1,0:T(8,128)S(1)} %bitcast.19, f32[184,128]{1,0:T(8,128)S(1)} %get-tuple-element.24.fixed_ref, bf16[32,1024]{1,0:T(8,128)(2,1)S(1)} %get-tuple-element.25.powers_ref), custom_call_target="tpu_custom_call" | custom-call | tf_op jit(solution)/shard_map/pallas_call | solution.py:607
  53.5 8.6 %all-gather = f32[512,128]{1,0:T(8,128)S(1)} all-gather(f32[128,128]{1,0:T(8,128)S(1)} %get-tuple-element.26), channel_id=2, replica_groups=mesh['tile_z'=8,'tile_y'=8,'tile_x'=2,'depth_x'=2,'depth_core'=2] {'dept..., dimensions={0}, use_global_device_ids=true | all-gather | bytes 327680 | tf_op jit(solution)/shard_map/all_gather | solution.py:619
  62.0 0.0 copy-start.2
  62.0 0.0 copy-start.3
  62.0 0.0 copy-start.4
  62.0 2.6 %shard_map.161 = (f32[3,4,1024]{2,1,0:T(4,128)}, f32[128,128]{1,0:T(8,128)S(1)}) custom-call(f32[4,128,128]{2,1,0:T(8,128)S(1)} %bitcast.18, f32[4104,128]{1,0:T(8,128)S(1)} %get-tuple-element.27.alpha_ref, f32[4104,128]{1,0:T(8,128)S(1)} %get-tuple-element.28.weight_ref, f32[3,520,128]{2,1,0:T(8,128)S(1)} %get-tuple-element.29.shade_ref, ...), custom_call_target="tpu_custom_call" | custom-call | tf_op jit(solution)/shard_map/pallas_call | solution.py:620
  64.7 17.6 %all_to_all.16 = f32[128,1,128]{2,1,0:T(1,128)S(1)} all-to-all(f32[128,1,128]{2,1,0:T(1,128)S(1)} %bitcast.22), channel_id=1, replica_groups={{0,6,8,14,16,22,24,30,32,38,40,46,48,54,56,62,64,70,72,78,80,86,88,94,9..., dimensions={0} | all-to-all | bytes 131072 | tf_op jit(solution)/shard_map/all_to_all | solution.py:526
  82.2 0.6 shard_map.162
  82.9 7.1 %all-gather.1 = f32[640,128]{1,0:T(8,128)S(1)} all-gather(f32[160,128]{1,0:T(8,128)S(1)} %shard_map.162), channel_id=3, replica_groups=mesh['tile_z'=8,'tile_y'=8,'tile_x'=2,'depth_x'=2,'depth_core'=2] {'dept..., dimensions={0}, use_global_device_ids=true | all-gather | bytes 409600 | tf_op jit(solution)/shard_map/all_gather | solution.py:642
  90.0 0.0 copy-done.2
  90.0 0.0 copy-done.3
  90.0 0.0 copy-done.4
  90.0 0.8 shard_map.163
Async XLA Ops:
  2.8 23.1 %collective-permute-start = (f32[160,128]{1,0:T(8,128)}, f32[160,128]{1,0:T(8,128)S(1)}, u32[]{:S(2)}, u32[]{:S(2)}) collective-permute-start(f32[160,128]{1,0:T(8,128)} %get-tuple-element.21.mine_ref.params_ref), channel_id=1, source_target_pairs={{0,6},{6,0},{2,4},{4,2},{1,7},{7,1},{3,5},{5,3},{8,14},{14,8},{10,... | collective-permute-start | bytes 245768 | tf_op jit(solution)/shard_map/ppermute | solution.py:574
  8.0 27.1 %all-to-all-start = ((s32[64,1,128]{2,1,0:T(1,128)}), s32[64,1,128]{2,1,0:T(1,128)S(1)}, u32[]{:S(2)}, u32[]{:S(2)}) async-start(s32[64,1,128]{2,1,0:T(1,128)} %bitcast.24), calls=%async_computation | async-start | bytes 65536 | tf_op jit(solution)/shard_map/all_to_all | solution.py:519
  25.9 0.9 copy-start
  26.8 0.9 copy-start.1
  62.0 28.0 %copy-start.2 = (f32[160,128]{1,0:T(8,128)S(1)}, f32[160,128]{1,0:T(8,128)}, u32[]{:S(2)}) copy-start(f32[160,128]{1,0:T(8,128)} %get-tuple-element.21.mine_ref.params_ref) | copy-start | bytes 245764
  62.0 28.0 %copy-start.3 = (f32[10,2048]{1,0:T(8,128)S(1)}, f32[10,2048]{1,0:T(8,128)}, u32[]{:S(2)}) copy-start(f32[10,2048]{1,0:T(8,128)} %first_ref.1) | copy-start | bytes 245764
  62.0 28.0 %copy-start.4 = (f32[10,2048]{1,0:T(8,128)S(1)}, f32[10,2048]{1,0:T(8,128)}, u32[]{:S(2)}) copy-start(f32[10,2048]{1,0:T(8,128)} %second_ref.1) | copy-start | bytes 245764

commit v10 on v8

--- a/solution.py
+++ b/solution.py
@@ -304,7 +304,7 @@
         return tuple(out)
 
     one, zero = jnp.ones((8, LANES), F32), jnp.zeros((8, LANES), F32)
-    out = lax.fori_loop(0, SLAB, step, (one, zero, zero, zero) * TILES, unroll=32)
+    out = lax.fori_loop(0, SLAB, step, (one, zero, zero, zero) * TILES, unroll=128)
     for q in range(4 * TILES):
         slab_ref[q * 8 : (q + 1) * 8, :] = out[q]
 
@@ -379,7 +379,8 @@
             gap = shade - carry[b]
             rows = pl.ds(at, 8, stride=PITCH)
             slope[rows, :] = weight_ref[rows, :] * gap
-            out.append(carry[b] + alpha_ref[rows, :] * gap)
+            alpha = alpha_ref[rows, :]
+            out.append(carry[b] * (1.0 - alpha) + alpha * shade)
         return tuple(out)
 
     lax.fori_loop(0, SLAB, step, tuple(behind), unroll=8)

time: 91.6 us -> 91.6 us (level)
  no operation moved by 1% of the time
where the time goes in v10:
time: 91.6 us; the launch traced here: 91.2 us
  blocking collectives  49 us (53%)
  starting transfers between devices  21.5 us (23%)
  Pallas kernels  10.8 us (12%)
  waiting for transfers between devices  7.31 us (8%)
  local copies, waits for them, and re-layouts  1.78 us (2%)
    all_to_all x1, blocking collectives, exchanged(): lax.all_to_all(array.reshape(LANES, 1, LANES), (*TILE, DEPTH[0]), 0, 0, a...  17.6 us
    all_to_all x1, starting transfers between devices, exchanged_in_plane(): return lax.all_to_all(array, TILE[:2], 0, 0, tiled=True)  16.3 us
    all_to_all x1, blocking collectives, exchanged_in_plane(): return lax.all_to_all(array, TILE[:2], 0, 0, tiled=True)  15.7 us
    all_gather x1, blocking collectives, body(): slabs = lax.all_gather(slab[None], DEPTH, axis=0, tiled=True)  8.57 us
    all_to_all x1, waiting for transfers between devices, exchanged_in_plane(): return lax.all_to_all(array, TILE[:2], 0, 0, tiled=True)  7.31 us
    all_gather x1, blocking collectives, body(): sums = lax.all_gather(sums[None], DEPTH, axis=0, tiled=True)  7.12 us
    ppermute x1, starting transfers between devices, body(): lax.ppermute(params, (TILE[2], DEPTH[0]), [(0, 3), (3, 0), (1, 2), (2, 1)])  5.22 us
    pallas_call x1, Pallas kernels, body(): call(backward_kernel, [((3, TILES, 1024), F32), (square, F32)], [VMEM] *...  2.83 us
  transfers between devices with their start and end apart: 2, of which 1 were waited for; matrix products, arithmetic and copies ran while one was open for 0% of the time, Pallas kernels for 2%

profile of v10, /device:TPU:1, one launch (start us, length us, event | category | flops | bytes accessed | tf_op | source)
XLA Modules:
  0.0 91.2 jit_solution(2609122195242870002)
XLA Ops:
  0.6 2.2 %shard_map.156 = (s32[64,128]{1,0:T(8,128)}, s32[16,128]{1,0:T(8,128)}, f32[160,128]{1,0:T(8,128)}) custom-call(s32[4,128]{1,0:T(4,128)} %bitcast.25, s32[4,128]{1,0:T(4,128)} %bitcast.26, f32[3,2048]{1,0:T(4,128)} %position_hbm.1, f32[3,2048]{1,0:T(4,128)} %scale_hbm.1, f32[1,2048]{1,0:T(1,128)} %opacity_hbm.1, f32[3,2048]{1,0:T(4,128)} %color_hbm.1), custom_call_target="tpu_custom_call" | custom-call | tf_op jit(solution)/shard_map/pallas_call | solution.py:563
  2.8 5.2 %collective-permute-start = (f32[160,128]{1,0:T(8,128)}, f32[160,128]{1,0:T(8,128)S(1)}, u32[]{:S(2)}, u32[]{:S(2)}) collective-permute-start(f32[160,128]{1,0:T(8,128)} %get-tuple-element.21.mine_ref.params_ref), channel_id=1, source_target_pairs={{0,6},{6,0},{2,4},{4,2},{1,7},{7,1},{3,5},{5,3},{8,14},{14,8},{10,... | collective-permute-start | bytes 245768 | tf_op jit(solution)/shard_map/ppermute | solution.py:571
  8.0 16.3 %all-to-all-start = ((s32[64,1,128]{2,1,0:T(1,128)}), s32[64,1,128]{2,1,0:T(1,128)S(1)}, u32[]{:S(2)}, u32[]{:S(2)}) async-start(s32[64,1,128]{2,1,0:T(1,128)} %bitcast.24), calls=%async_computation | async-start | bytes 65536 | tf_op jit(solution)/shard_map/all_to_all | solution.py:516
  24.4 1.5 %shard_map.157.loose_ref = f32[184,128]{1,0:T(8,128)} custom-call(s32[1]{0:T(128)} %bitcast.6.depth_ref, s32[4]{0:T(128)} %view_hbm.1, s32[4]{0:T(128)} %length_hbm.1, f32[4,2,4]{2,1,0:T(2,128)} %cams_hbm.1, f32[3]{0:T(128)} %back_hbm.1, f32[3,4,1024]{2,1,0:T(4,128)} %bitcast.23, s32[16,128]{1,0:T(8,128)} %get-tuple-element.22.list_hbm), custom_call_target="tpu_custom_call" | custom-call | tf_op jit(solution)/shard_map/pallas_call | solution.py:581
  25.9 0.0 collective-permute-done.theirs_ref
  25.9 0.0 copy-start
  25.9 0.9 copy-done
  26.8 0.0 copy-start.1
  26.8 0.9 copy-done.1
  27.7 0.1 shard_map.158
  27.8 7.3 %all-to-all-done = s32[64,1,128]{2,1,0:T(1,128)S(1)} async-done(((s32[64,1,128]{2,1,0:T(1,128)}), s32[64,1,128]{2,1,0:T(1,128)S(1)}, u32[]{:S(2)}, u32[]{:S(2)}) %all-to-all-start) | async-done | bytes 32800 | tf_op jit(solution)/shard_map/all_to_all | solution.py:516
  35.1 1.0 %shard_map.159 = f32[64,2,128]{2,1,0:T(2,128)S(1)} custom-call(s32[64,128]{1,0:T(8,128)S(1)} %bitcast.21, bf16[512,384]{1,0:T(8,128)(2,1)S(1)} %get-tuple-element.23.table_ref), custom_call_target="tpu_custom_call" | custom-call | tf_op jit(solution)/shard_map/pallas_call | solution.py:596
  36.1 15.7 %all_to_all.15 = f32[64,2,128]{2,1,0:T(2,128)S(1)} all-to-all(f32[64,2,128]{2,1,0:T(2,128)S(1)} %shard_map.159), channel_id=1, replica_groups=mesh['tile_z'=8,'tile_y'=8,'tile_x'=2,'depth_x'=2,'depth_core'=2] {'tile..., dimensions={0} | all-to-all | bytes 131072 | tf_op jit(solution)/shard_map/all_to_all | solution.py:516
  51.8 1.6 %shard_map.160 = (f32[128,128]{1,0:T(8,128)S(1)}, f32[4104,128]{1,0:T(8,128)S(1)}, f32[4104,128]{1,0:T(8,128)S(1)}, f32[3,520,128]{2,1,0:T(8,128)S(1)}, f32[64,128]{1,0:T(8,128)S(1)}) custom-call(f32[128,128]{1,0:T(8,128)S(1)} %bitcast.19, f32[184,128]{1,0:T(8,128)S(1)} %get-tuple-element.24.fixed_ref, bf16[32,1024]{1,0:T(8,128)(2,1)S(1)} %get-tuple-element.25.powers_ref), custom_call_target="tpu_custom_call" | custom-call | tf_op jit(solution)/shard_map/pallas_call | solution.py:604
  53.4 8.6 %all-gather = f32[512,128]{1,0:T(8,128)S(1)} all-gather(f32[128,128]{1,0:T(8,128)S(1)} %get-tuple-element.26), channel_id=2, replica_groups=mesh['tile_z'=8,'tile_y'=8,'tile_x'=2,'depth_x'=2,'depth_core'=2] {'dept..., dimensions={0}, use_global_device_ids=true | all-gather | bytes 327680 | tf_op jit(solution)/shard_map/all_gather | solution.py:616
  62.0 0.0 copy-start.2
  62.0 0.0 copy-start.3
  62.0 0.0 copy-start.4
  62.0 2.8 %shard_map.161 = (f32[3,4,1024]{2,1,0:T(4,128)}, f32[128,128]{1,0:T(8,128)S(1)}) custom-call(f32[4,128,128]{2,1,0:T(8,128)S(1)} %bitcast.18, f32[4104,128]{1,0:T(8,128)S(1)} %get-tuple-element.27.alpha_ref, f32[4104,128]{1,0:T(8,128)S(1)} %get-tuple-element.28.weight_ref, f32[3,520,128]{2,1,0:T(8,128)S(1)} %get-tuple-element.29.shade_ref, ...), custom_call_target="tpu_custom_call" | custom-call | tf_op jit(solution)/shard_map/pallas_call | solution.py:617
  64.8 17.6 %all_to_all.16 = f32[128,1,128]{2,1,0:T(1,128)S(1)} all-to-all(f32[128,1,128]{2,1,0:T(1,128)S(1)} %bitcast.22), channel_id=1, replica_groups={{0,6,8,14,16,22,24,30,32,38,40,46,48,54,56,62,64,70,72,78,80,86,88,94,9..., dimensions={0} | all-to-all | bytes 131072 | tf_op jit(solution)/shard_map/all_to_all | solution.py:523
  82.4 0.8 shard_map.162
  83.2 7.1 %all-gather.1 = f32[640,128]{1,0:T(8,128)S(1)} all-gather(f32[160,128]{1,0:T(8,128)S(1)} %shard_map.162), channel_id=3, replica_groups=mesh['tile_z'=8,'tile_y'=8,'tile_x'=2,'depth_x'=2,'depth_core'=2] {'dept..., dimensions={0}, use_global_device_ids=true | all-gather | bytes 409600 | tf_op jit(solution)/shard_map/all_gather | solution.py:639
  90.3 0.0 copy-done.2
  90.3 0.0 copy-done.3
  90.3 0.0 copy-done.4
  90.3 0.8 shard_map.163
Async XLA Ops:
  2.8 23.1 %collective-permute-start = (f32[160,128]{1,0:T(8,128)}, f32[160,128]{1,0:T(8,128)S(1)}, u32[]{:S(2)}, u32[]{:S(2)}) collective-permute-start(f32[160,128]{1,0:T(8,128)} %get-tuple-element.21.mine_ref.params_ref), channel_id=1, source_target_pairs={{0,6},{6,0},{2,4},{4,2},{1,7},{7,1},{3,5},{5,3},{8,14},{14,8},{10,... | collective-permute-start | bytes 245768 | tf_op jit(solution)/shard_map/ppermute | solution.py:571
  8.0 27.1 %all-to-all-start = ((s32[64,1,128]{2,1,0:T(1,128)}), s32[64,1,128]{2,1,0:T(1,128)S(1)}, u32[]{:S(2)}, u32[]{:S(2)}) async-start(s32[64,1,128]{2,1,0:T(1,128)} %bitcast.24), calls=%async_computation | async-start | bytes 65536 | tf_op jit(solution)/shard_map/all_to_all | solution.py:516
  25.9 0.9 copy-start
  26.8 0.9 copy-start.1
  62.0 28.3 %copy-start.2 = (f32[160,128]{1,0:T(8,128)S(1)}, f32[160,128]{1,0:T(8,128)}, u32[]{:S(2)}) copy-start(f32[160,128]{1,0:T(8,128)} %get-tuple-element.21.mine_ref.params_ref) | copy-start | bytes 245764
  62.0 28.3 %copy-start.3 = (f32[10,2048]{1,0:T(8,128)S(1)}, f32[10,2048]{1,0:T(8,128)}, u32[]{:S(2)}) copy-start(f32[10,2048]{1,0:T(8,128)} %first_ref.1) | copy-start | bytes 245764
  62.0 28.3 %copy-start.4 = (f32[10,2048]{1,0:T(8,128)S(1)}, f32[10,2048]{1,0:T(8,128)}, u32[]{:S(2)}) copy-start(f32[10,2048]{1,0:T(8,128)} %second_ref.1) | copy-start | bytes 245764
